TPU v7x, 768 devices: a whole 4x8x12 slice. The times are simulated.
768 devices in a mesh: src: 32 (over y, z_lo), dst: 24 (over x, z_hi, core).
Axes of the slice: x: 4, y: 8, z: 12 (z_hi: 3, z_lo: 4; z = z_hi * 4 + z_lo), core: 2. Of those that a mesh axis runs over, the one named last changes fastest.
Arguments:
- prior: float32 [98304, 256], P(('src', 'dst')), may hold values from -6 to 6
- degrees: int32 [98304], P(('src', 'dst')), may hold values from 1 to 15360, as said below
- seed_mask: int32 [98304], P(('src', 'dst')), may hold values 0 or 1
- seed_labels: int32 [98304], P(('src', 'dst')), may hold values from 0 to 255
- adjacency: bfloat16 [32, 24, 24, 5, 128, 128], P('src', 'dst'), may hold values from 0 to 1, as said below
- block_cols: int32 [32, 24, 24, 5], P('src', 'dst'), may hold values from 0 to 31
- slot_counts: int32 [32, 24, 24], P('src', 'dst'), may hold values from 1 to 5, as said below
Outputs:
- scores: float32 [98304, 256], P(('src', 'dst'))
Inputs may be any that keep to these rules, and one draw needn't show every extreme that they name: `slot_counts`: each device holds at most 5 live slots in a row block; local row block 0 of row group 0 has exactly 5 on every device. `block_cols`: local column indices within one column group. `adjacency`: entries are 0 or 1. degrees[n] is the number of ones in node n's row of the adjacency, over the live slots of all devices; some node reaches the most.
All inputs are finite; a program needn't handle non-finite values. No bound on the sum of `seed_mask` on one device may be relied on, other than what follows from the above.
Results may differ from a plain program's by a relative error of at most 0.005.
Values may be sent and summed in bfloat16 or wider, within the bound.
No kernel may reach another device: no remote copies, remote signals or barrier semaphores. Data moves between devices by JAX's collectives and lax.ppermute only.
A program may use at most 32 MiB of HBM per device.

v0:
```python
import jax
import jax.numpy as jnp
from jax import lax
from jax.sharding import PartitionSpec as P

SWEEPS = 2


RETAIN = 0.8


def per_device(prior, degrees, seed_mask, seed_labels, adjacency, block_cols, slot_counts):
    classes = prior.shape[1]
    block_size = adjacency.shape[-1]
    weights = adjacency[0, 0]
    columns = block_cols[0, 0]
    counts = slot_counts[0, 0]
    inverse_root = lax.rsqrt(degrees.astype(jnp.float32))[:, None]
    onehot = (seed_labels[:, None] == jnp.arange(classes, dtype=jnp.int32)[None, :]).astype(
        jnp.float32
    )
    seeded = seed_mask[:, None] > 0
    active = jnp.arange(weights.shape[1], dtype=jnp.int32)[None, :] < counts[:, None]
    scores = prior
    for sweep_index in range(SWEEPS):
        outgoing = (inverse_root * scores).astype(jnp.bfloat16)
        copies = lax.all_gather(outgoing, "src", axis=0, tiled=True)
        blocks = copies.reshape(-1, block_size, classes)
        picked = jnp.take(blocks, columns, axis=0)
        picked = jnp.where(active[:, :, None, None], picked, jnp.zeros_like(picked))
        partial_value = jnp.einsum(
            "rsij,rsjc->ric", weights, picked, preferred_element_type=jnp.float32
        )
        summed = lax.psum_scatter(
            partial_value.reshape(-1, classes).astype(jnp.bfloat16),
            "dst",
            scatter_dimension=0,
            tiled=True,
        ).astype(jnp.float32)
        hidden = RETAIN * inverse_root * summed + (1.0 - RETAIN) * prior
        scores = jnp.where(seeded, onehot, hidden)
    return scores


def solution(mesh):
    in_specs = (
        P(("src", "dst"), None),
        P(("src", "dst")),
        P(("src", "dst")),
        P(("src", "dst")),
        P("src", "dst", None, None, None, None),
        P("src", "dst", None, None),
        P("src", "dst", None),
    )
    out_specs = P(("src", "dst"), None)
    return jax.shard_map(
        per_device, mesh=mesh, in_specs=in_specs, out_specs=out_specs, check_vma=False
    )
```

profile of v0, /device:TPU:1, one launch (start us, length us, event | category | flops | bytes accessed | tf_op | source)
XLA Modules:
  0.0 635.5 jit_solution(4715639934952777678)
XLA Ops:
  6.5 0.0 all-gather.3.cloned.1.call-start
  6.5 0.7 broadcast_multiply_fusion
  7.2 1.6 multiply_convert_fusion
  8.8 0.0 all-gather.3.cloned.1.call-update
  8.8 0.0 reduce-scatter.3.cloned.1.call-start
  8.9 0.7 compare_select_fusion
  9.6 0.1 copy.14
  9.7 0.1 reshape.67
  9.8 0.7 compare_and_fusion
  10.5 0.1 copy.12
  10.6 0.7 iota_compare_fusion.1
  11.3 147.3 %all-gather.3.cloned.1.call-done = bf16[4096,256]{1,0:T(8,128)(2,1)} async-done(((bf16[128,256]{1,0:T(8,128)(2,1)}), bf16[4096,256]{1,0:T(8,128)(2,1)}) %all-gather.3.cloned.1.call-update) | async-done | bytes 2097168 | tf_op jit(solution)/shard_map/all_gather | solution.py:27
  158.6 8.0 %gather_fusion = bf16[120,128,256]{2,1,0:T(8,128)(2,1)} fusion(bf16[32,128,256]{2,1,0:T(8,128)(2,1)} %bitcast.30, s32[1024]{0:T(1024)S(1)} %pad_clamp_fusion), kind=kCustom, calls=%fused_computation.clone | custom fusion | bytes 15729120 | tf_op jit(solution)/shard_map/jit(_take)/gather | solution.py:29
  166.6 0.0 copy-start.2
  166.6 0.0 copy-start
  166.6 0.0 copy-start.1
  166.6 7.4 %bitcast_convert_fusion.1 = bf16[24,256,128]{1,2,0:T(8,128)(2,1)} fusion(bf16[24,5,128,256]{3,2,1,0:T(8,128)(2,1)} %bitcast.33, pred[24,5]{1,0:T(8,128)(4,1)S(1)} %copy.12, pred[24,5]{1,0:T(8,128)(4,1)S(1)} %iota_compare_fusion.1, bf16[1,1,24,5,128,128]{5,4,3,2,1,0:T(8,128)(2,1)} %param.13), kind=kOutput, calls=%fused_computation.17 | convolution fusion | flops 1015283712 | bytes 13369584 | tf_op jit(solution)/shard_map/rsij,rsjc->ric/dot_general | solution.py:31
  174.0 0.0 reduce-scatter.3.cloned.1.call-update
  174.1 0.0 all-gather.5.cloned.1.call-start
  174.1 0.0 copy-done.2
  174.1 148.5 %reduce-scatter.3.cloned.1.call-done = bf16[128,256]{1,0:T(8,128)(2,1)} async-done(((bf16[3072,256]{1,0:T(8,128)(2,1)}), bf16[128,256]{1,0:T(8,128)(2,1)}) %reduce-scatter.3.cloned.1.call-update) | async-done | bytes 65552 | tf_op jit(solution)/shard_map/reduce_scatter | solution.py:34
  322.7 0.0 copy-done
  322.7 0.0 copy-done.1
  322.7 1.6 fusion.17
  324.3 0.0 all-gather.5.cloned.1.call-update
  324.3 0.0 reduce-scatter.5.cloned.1.call-start
  324.3 139.0 %all-gather.5.cloned.1.call-done = bf16[4096,256]{1,0:T(8,128)(2,1)} async-done(((bf16[128,256]{1,0:T(8,128)(2,1)}), bf16[4096,256]{1,0:T(8,128)(2,1)}) %all-gather.5.cloned.1.call-update) | async-done | bytes 2097168 | tf_op jit(solution)/shard_map/all_gather | solution.py:27
  463.3 8.0 %gather_fusion.1 = bf16[120,128,256]{2,1,0:T(8,128)(2,1)} fusion(bf16[32,128,256]{2,1,0:T(8,128)(2,1)} %bitcast.31, s32[1024]{0:T(1024)S(1)} %pad_clamp_fusion), kind=kCustom, calls=%fused_computation.1.clone | custom fusion | bytes 15729120 | tf_op jit(solution)/shard_map/jit(_take)/gather | solution.py:29
  471.3 7.4 %bitcast_convert_fusion = bf16[24,256,128]{1,2,0:T(8,128)(2,1)} fusion(bf16[24,5,128,256]{3,2,1,0:T(8,128)(2,1)} %bitcast.32, pred[24,5]{1,0:T(8,128)(4,1)S(1)} %copy.12, pred[24,5]{1,0:T(8,128)(4,1)S(1)} %iota_compare_fusion.1, bf16[1,1,24,5,128,128]{5,4,3,2,1,0:T(8,128)(2,1)} %param.13), kind=kOutput, calls=%fused_computation.16 | convolution fusion | flops 1015283712 | bytes 13369584 | tf_op jit(solution)/shard_map/rsij,rsjc->ric/dot_general | solution.py:31
  478.7 0.0 reduce-scatter.5.cloned.1.call-update
  478.7 148.6 %reduce-scatter.5.cloned.1.call-done = bf16[128,256]{1,0:T(8,128)(2,1)} async-done(((bf16[3072,256]{1,0:T(8,128)(2,1)}), bf16[128,256]{1,0:T(8,128)(2,1)}) %reduce-scatter.5.cloned.1.call-update) | async-done | bytes 65552 | tf_op jit(solution)/shard_map/reduce_scatter | solution.py:34
  627.4 1.6 convert_select_fusion
  (2 shorter events, 0.0 us)
Async XLA Ops:
  6.5 152.1 %all-gather.3.cloned.1.call-start = ((), (), s32[]{:S(2)}) async-start(), calls=%async_computation.2 | async-start | bytes 2162688 | tf_op jit(solution)/shard_map/all_gather | solution.py:27
  8.8 313.8 %reduce-scatter.3.cloned.1.call-start = ((), (), s32[]{:S(2)}) async-start(), calls=%async_computation.3 | async-start | bytes 1638400 | tf_op jit(solution)/shard_map/reduce_scatter | solution.py:34
  166.6 7.5 %copy-start.2 = (s32[128]{0:T(128)S(1)}, s32[128]{0:T(128)}, u32[]{:S(2)}) copy-start(s32[128]{0:T(128)} %param.11) | copy-start | bytes 1540
  166.6 156.0 %copy-start = (f32[128,256]{1,0:T(8,128)S(1)}, f32[128,256]{1,0:T(8,128)}, u32[]{:S(2)}) copy-start(f32[128,256]{1,0:T(8,128)} %param.9) | copy-start | bytes 393220
  166.6 156.0 %copy-start.1 = (s32[128]{0:T(128)S(1)}, s32[128]{0:T(128)}, u32[]{:S(2)}) copy-start(s32[128]{0:T(128)} %param.12) | copy-start | bytes 1540
  174.1 289.3 %all-gather.5.cloned.1.call-start = ((), (), s32[]{:S(2)}) async-start(), calls=%async_computation.4 | async-start | bytes 2162688 | tf_op jit(solution)/shard_map/all_gather | solution.py:27
  324.3 303.1 %reduce-scatter.5.cloned.1.call-start = ((), (), s32[]{:S(2)}) async-start(), calls=%async_computation.5 | async-start | bytes 1638400 | tf_op jit(solution)/shard_map/reduce_scatter | solution.py:34
Sparse Core Ops, SparseCore 0:
  9.7 148.8 all-gather.2
  174.2 148.4 reduce-scatter.2
  325.3 137.9 all-gather.4
  478.9 148.4 reduce-scatter.4
where the time goes:
time: 636 us
  waiting for transfers between devices  584 us (92%)
  local copies, waits for them, and re-layouts  16.3 us (3%)
  matrix products  14.8 us (2%)
  between operations  13.2 us (2%)
  other arithmetic  7.62 us (1%)
    reduce_scatter x2, waiting for transfers between devices, per_device(): lax.psum_scatter(partial_value.reshape(-1, classes).astype(jnp.bfloat16),...  297 us
    all_gather x2, waiting for transfers between devices, per_device(): copies = lax.all_gather(outgoing, 'src', axis=0, tiled=True)  286 us
    gather x2, local copies, waits for them, and re-layouts, per_device(): picked = jnp.take(blocks, columns, axis=0)  16 us
    dot_general x2, matrix products, per_device(): jnp.einsum('rsij,rsjc->ric', weights, picked, preferred_element_type=jnp....  14.8 us
  transfers between devices with their start and end apart: 4, of which 4 were waited for; matrix products, arithmetic and copies ran while one was open for 0% of the time, Pallas kernels for 0%

commit v1 on v0

v1 whole, which is shorter than its diff:
```python
import jax
import jax.numpy as jnp
from jax import lax
from jax.experimental import pallas as pl
from jax.experimental.pallas import tpu as pltpu
from jax.sharding import PartitionSpec as P

SWEEPS = 2
RETAIN = 0.8

Y, ZL, X, ZH, CORES = 8, 4, 4, 3, 2
PAIRS = X * ZH
STEP = 4

Z_GROUPS = [[y * ZL + z for z in range(ZL)] for y in range(Y)]
X_GROUPS = [
    [(x * ZH + z) * CORES + c for x in range(X)] for z in range(ZH) for c in range(CORES)
]
H_GROUPS = [
    [(x * ZH + z) * CORES + c for z in range(ZH)] for x in range(X) for c in range(CORES)
]
SWAP = [(d, d ^ 1) for d in range(X * ZH * CORES)]


def y_shift(step):
    return [
        (y * ZL + z, (y + step) % Y * ZL + z) for y in range(Y) for z in range(ZL)
    ]


UP, DOWN = y_shift(1), y_shift(-1)
PIECE_AT = (0, 4, 8, 12, 16, 18, 20, 24, 28)
PIECE_LEN = (4, 4, 4, 4, 2, 2, 4, 4, 4)
LIVE = Y * ZL


def sum_kernel(parity, slots, weights, *refs):
    pieces = refs[: len(PIECE_AT)]
    out, blocks, sems = refs[len(PIECE_AT) :]
    step = pl.program_id(0)

    @pl.when(step == 0)
    def _():
        copies = [
            pltpu.make_async_copy(piece, blocks.at[pl.ds(at, count)], sems.at[i])
            for i, (piece, at, count) in enumerate(zip(pieces, PIECE_AT, PIECE_LEN))
        ]
        for copy in copies:
            copy.start()
        blocks[LIVE] = jnp.zeros(blocks.shape[1:], blocks.dtype)
        for copy in copies:
            copy.wait()

    depth = weights.shape[2]
    for q in range(STEP):
        base = ((step * STEP + q) * CORES + parity[0]) * depth
        total = None
        for t in range(0, depth, 2):
            group = range(t, min(t + 2, depth))
            left = jnp.concatenate([weights[q, 0, u] for u in group], axis=1)
            right = jnp.concatenate([blocks[slots[base + u]] for u in group], axis=0)
            term = jnp.dot(left, right, preferred_element_type=jnp.float32)
            total = term if total is None else total + term
        out[q] = total.astype(out.dtype)


def partial_sums(parity, slots, weights, pieces, dtype):
    _, _, depth, size, _ = weights.shape
    classes = pieces[0].shape[-1]
    grid_spec = pltpu.PrefetchScalarGridSpec(
        num_scalar_prefetch=2,
        grid=(PAIRS // STEP,),
        in_specs=[
            pl.BlockSpec(
                (STEP, 1, depth, size, size), lambda i, parity, slots: (i, parity[0], 0, 0, 0)
            )
        ]
        + [pl.BlockSpec(memory_space=pl.ANY)] * len(pieces),
        out_specs=pl.BlockSpec((STEP, size, classes), lambda i, parity, slots: (i, 0, 0)),
        scratch_shapes=[
            pltpu.VMEM((LIVE + 1, size, classes), jnp.bfloat16),
            pltpu.SemaphoreType.DMA((len(pieces),)),
        ],
    )
    return pl.pallas_call(
        sum_kernel,
        grid_spec=grid_spec,
        out_shape=jax.ShapeDtypeStruct((PAIRS, size, classes), dtype),
        compiler_params=pltpu.CompilerParams(vmem_limit_bytes=32 * 1024 * 1024),
        cost_estimate=pl.CostEstimate(
            flops=2 * PAIRS * depth * size * size * classes,
            bytes_accessed=6 * 1024 * 1024,
            transcendentals=0,
        ),
    )(parity, slots, weights, *pieces)


def gather_blocks(outgoing):
    spread = jnp.broadcast_to(outgoing[None], (ZL,) + outgoing.shape)
    own = lax.all_to_all(spread, "src", 0, 0, axis_index_groups=Z_GROUPS)
    up, down = [own], [own]
    for _ in range(3):
        up.append(lax.ppermute(up[-1], "src", UP))
        down.append(lax.ppermute(down[-1], "src", DOWN))
    far_up = lax.ppermute(up[3][:2], "src", UP)
    far_down = lax.ppermute(down[3][2:], "src", DOWN)
    return [own, down[1], down[2], down[3], far_up, far_down, up[3], up[2], up[1]]


def per_device(prior, degrees, seed_mask, seed_labels, adjacency, block_cols, slot_counts):
    classes = prior.shape[1]
    depth, size = adjacency.shape[3], adjacency.shape[4]
    weights = adjacency.reshape(PAIRS, CORES, depth, size, size)
    core = lax.axis_index("dst") % CORES
    mine = core.astype(jnp.int32).reshape(1)
    other = 1 - mine
    y = lax.axis_index("src") // ZL
    columns = block_cols[0, 0]
    relative = (columns // ZL - y) % Y * ZL + columns % ZL
    active = jnp.arange(depth, dtype=jnp.int32)[None, :] < slot_counts[0, 0][:, None]
    slots = jnp.where(active, relative, LIVE).astype(jnp.int32).reshape(-1)
    inverse_root = lax.rsqrt(degrees.astype(jnp.float32))[:, None]
    onehot = (seed_labels[:, None] == jnp.arange(classes, dtype=jnp.int32)[None, :]).astype(
        jnp.float32
    )
    seeded = seed_mask[:, None] > 0
    scores = prior
    for _ in range(SWEEPS):
        outgoing = (inverse_root * scores).astype(jnp.bfloat16)
        pieces = gather_blocks(outgoing)
        send = partial_sums(other, slots, weights, pieces, jnp.bfloat16)
        swapped = lax.ppermute(send, "dst", SWAP)
        keep = partial_sums(mine, slots, weights, pieces, jnp.float32)
        chip = (keep + swapped.astype(jnp.float32)).astype(jnp.bfloat16)
        chip = chip.reshape(X, ZH, size, classes)
        rows = lax.all_to_all(chip, "dst", 0, 0, axis_index_groups=X_GROUPS)
        rows = jnp.sum(rows.astype(jnp.float32), axis=0).astype(jnp.bfloat16)
        parts = lax.all_to_all(rows, "dst", 0, 0, axis_index_groups=H_GROUPS)
        summed = jnp.sum(parts.astype(jnp.float32), axis=0)
        hidden = RETAIN * inverse_root * summed + (1.0 - RETAIN) * prior
        scores = jnp.where(seeded, onehot, hidden)
    return scores


def solution(mesh):
    in_specs = (
        P(("src", "dst"), None),
        P(("src", "dst")),
        P(("src", "dst")),
        P(("src", "dst")),
        P("src", "dst", None, None, None, None),
        P("src", "dst", None, None),
        P("src", "dst", None),
    )
    out_specs = P(("src", "dst"), None)
    return jax.shard_map(
        per_device, mesh=mesh, in_specs=in_specs, out_specs=out_specs, check_vma=False
    )
```

time: 636 us -> 200 us (0.31)
  the two profiles are of different devices: /device:TPU:1 before, /device:TPU:24 now
where the time goes in v1:
time: 200 us; the launch traced here: 199 us
  blocking collectives  75.7 us (38%)
  starting transfers between devices  68.9 us (34%)
  waiting for transfers between devices  33.9 us (17%)
  Pallas kernels  9.84 us (5%)
  local copies, waits for them, and re-layouts  5.29 us (3%)
  other arithmetic  4.85 us (2%)
    all_to_all x2, blocking collectives, per_device(): rows = lax.all_to_all(chip, 'dst', 0, 0, axis_index_groups=X_GROUPS)  32.8 us
    all_to_all x2, blocking collectives, gather_blocks(): own = lax.all_to_all(spread, 'src', 0, 0, axis_index_groups=Z_GROUPS)  29.9 us
    ppermute x6, starting transfers between devices, gather_blocks(): up.append(lax.ppermute(up[-1], 'src', UP))  25.2 us
    ppermute x6, starting transfers between devices, gather_blocks(): down.append(lax.ppermute(down[-1], 'src', DOWN))  14.3 us
    all_to_all x1, blocking collectives, per_device(): parts = lax.all_to_all(rows, 'dst', 0, 0, axis_index_groups=H_GROUPS)  13.1 us
    ppermute x6, waiting for transfers between devices, gather_blocks(): up.append(lax.ppermute(up[-1], 'src', UP))  11.6 us
    ppermute x2, waiting for transfers between devices, gather_blocks(): far_down = lax.ppermute(down[3][2:], 'src', DOWN)  11.4 us
    all_to_all x1, starting transfers between devices, per_device(): parts = lax.all_to_all(rows, 'dst', 0, 0, axis_index_groups=H_GROUPS)  11.2 us
  transfers between devices with their start and end apart: 19, of which 12 were waited for; matrix products, arithmetic and copies ran while one was open for 1% of the time, Pallas kernels for 2%

profile of v1, /device:TPU:24, one launch (start us, length us, event | category | flops | bytes accessed | tf_op | source)
XLA Modules:
  0.0 198.9 jit_solution(1659062438686672306)
XLA Ops:
  0.0 0.7 broadcast_multiply_fusion
  0.7 1.0 multiply_convert_fusion
  1.7 15.9 %all_to_all.30.refs_0_ = bf16[4,128,256]{2,1,0:T(8,128)(2,1)S(1)} all-to-all(bf16[4,128,256]{2,1,0:T(8,128)(2,1)S(1)} %broadcast_in_dim.34), channel_id=1, replica_groups={{0,24,48,72},{96,120,144,168},{192,216,240,264},{288,312,336,360},{384,..., dimensions={0} | all-to-all | bytes 524288 | tf_op jit(solution)/shard_map/all_to_all | solution.py:100
  17.6 4.7 %collective-permute-start.3 = (bf16[4,128,256]{2,1,0:T(8,128)(2,1)S(1)}, bf16[4,128,256]{2,1,0:T(8,128)(2,1)S(1)}, u32[]{:S(2)}, u32[]{:S(2)}) collective-permute-start(bf16[4,128,256]{2,1,0:T(8,128)(2,1)S(1)} %all_to_all.30.refs_0_), channel_id=1, source_target_pairs={{0,96},{24,120},{48,144},{72,168},{96,192},{120,216},{144,240},{16... | collective-permute-start | bytes 786440 | tf_op jit(solution)/shard_map/ppermute | solution.py:103
  22.3 1.9 collective-permute-start
  24.2 1.9 collective-permute-done.3.refs_8_
  26.2 5.6 %collective-permute-start.4 = (bf16[4,128,256]{2,1,0:T(8,128)(2,1)S(1)}, bf16[4,128,256]{2,1,0:T(8,128)(2,1)S(1)}, u32[]{:S(2)}, u32[]{:S(2)}) collective-permute-start(bf16[4,128,256]{2,1,0:T(8,128)(2,1)S(1)} %collective-permute-done.3.refs_8_), channel_id=1, source_target_pairs={{0,96},{24,120},{48,144},{72,168},{96,192},{120,216},{144,240},{16... | collective-permute-start | bytes 786440 | tf_op jit(solution)/shard_map/ppermute | solution.py:103
  31.8 0.0 collective-permute-done.refs_1_
  31.8 1.9 collective-permute-start.1
  33.7 1.9 collective-permute-done.4.refs_7_
  35.6 5.6 %collective-permute-start.5 = (bf16[4,128,256]{2,1,0:T(8,128)(2,1)S(1)}, bf16[4,128,256]{2,1,0:T(8,128)(2,1)S(1)}, u32[]{:S(2)}, u32[]{:S(2)}) collective-permute-start(bf16[4,128,256]{2,1,0:T(8,128)(2,1)S(1)} %collective-permute-done.4.refs_7_), channel_id=1, source_target_pairs={{0,96},{24,120},{48,144},{72,168},{96,192},{120,216},{144,240},{16... | collective-permute-start | bytes 786440 | tf_op jit(solution)/shard_map/ppermute | solution.py:103
  41.2 0.0 collective-permute-done.1.refs_2_
  41.3 1.9 collective-permute-start.2
  43.2 0.8 copy.10
  44.0 0.1 squeeze.3
  44.1 0.7 iota_compare_fusion.1
  44.8 0.1 lt.40
  44.9 0.3 collective-permute-done.5.refs_6_
  45.2 5.6 %collective-permute-start.6 = (bf16[2,128,256]{2,1,0:T(8,128)(2,1)S(1)}, bf16[2,128,256]{2,1,0:T(8,128)(2,1)S(1)}, u32[]{:S(2)}, u32[]{:S(2)}) collective-permute-start(bf16[2,128,256]{2,1,0:T(8,128)(2,1)S(1)} %slice.16), channel_id=1, source_target_pairs={{0,96},{24,120},{48,144},{72,168},{96,192},{120,216},{144,240},{16... | collective-permute-start | bytes 393224 | tf_op jit(solution)/shard_map/ppermute | solution.py:105
  50.8 0.3 collective-permute-done.2.refs_3_
  51.1 1.9 collective-permute-start.7
  53.1 0.3 collective-permute-done.6.refs_4_
  53.3 5.8 %collective-permute-done.7.refs_5_ = bf16[2,128,256]{2,1,0:T(8,128)(2,1)S(1)} collective-permute-done((bf16[2,128,256]{2,1,0:T(8,128)(2,1)S(1)}, bf16[2,128,256]{2,1,0:T(8,128)(2,1)S(1)}, u32[]{:S(2)}, u32[]{:S(2)}) %collective-permute-start.7) | collective-permute-done | bytes 131104 | tf_op jit(solution)/shard_map/ppermute | solution.py:106
  59.2 2.1 %copy-done = bf16[1,1,24,5,128,128]{5,4,3,2,1,0:T(8,128)(2,1)S(1)} copy-done((bf16[1,1,24,5,128,128]{5,4,3,2,1,0:T(8,128)(2,1)S(1)}, bf16[1,1,24,5,128,128]{5,4,3,2,1,0:T(8,128)(2,1)}, u32[]{:S(2)}) %copy-start) | copy-done | bytes 3932184
  61.3 2.5 %shard_map.74 = bf16[12,128,256]{2,1,0:T(8,128)(2,1)S(1)} custom-call(s32[1]{0:T(128)S(6)} %sub.24.parity, s32[120]{0:T(128)S(1)} %fusion.3.slots, bf16[12,2,5,128,128]{4,3,2,1,0:T(8,128)(2,1)S(1)} %bitcast.7, bf16[4,128,256]{2,1,0:T(8,128)(2,1)S(1)} %all_to_all.30.refs_0_, bf16[4,128,256]{2,1,0:T(8,128)(2,1)S(1)} %collective-permute-done.refs_1_, ...), custom_call_target="tpu_custom_call" | custom-call | flops 503316480 | bytes 6291456 | tf_op jit(solution)/shard_map/pallas_call | solution.py:85
  63.8 1.9 collective-permute-start.8
  65.7 2.5 %shard_map.73 = f32[12,128,256]{2,1,0:T(8,128)S(1)} custom-call(s32[1]{0:T(128)} %bitcast.parity, s32[120]{0:T(128)S(1)} %fusion.3.slots, bf16[12,2,5,128,128]{4,3,2,1,0:T(8,128)(2,1)S(1)} %bitcast.8, bf16[4,128,256]{2,1,0:T(8,128)(2,1)S(1)} %all_to_all.30.refs_0_, bf16[4,128,256]{2,1,0:T(8,128)(2,1)S(1)} %collective-permute-done.refs_1_, ...), custom_call_target="tpu_custom_call" | custom-call | flops 503316480 | bytes 6291456 | tf_op jit(solution)/shard_map/pallas_call | solution.py:85
  68.2 0.0 collective-permute-done.8
  68.2 0.2 add_convert_fusion.1
  68.4 0.0 copy-start.6
  68.4 0.0 copy-start.4
  68.5 0.0 copy-start.5
  68.5 17.2 %all_to_all.31 = bf16[4,3,128,256]{3,2,1,0:T(8,128)(2,1)S(1)} all-to-all(bf16[4,3,128,256]{3,2,1,0:T(8,128)(2,1)S(1)} %bitcast.11), channel_id=1, replica_groups={{0,6,12,18},{1,7,13,19},{2,8,14,20},{3,9,15,21},{4,10,16,22},{5,11,17,2..., dimensions={0} | all-to-all | bytes 1572864 | tf_op jit(solution)/shard_map/all_to_all | solution.py:136
  85.6 0.8 reduce_sum.42
  86.5 11.2 %all-to-all-start.2 = ((bf16[3,128,256]{2,1,0:T(8,128)(2,1)}), bf16[3,128,256]{2,1,0:T(8,128)(2,1)S(1)}, u32[]{:S(2)}, u32[]{:S(2)}) async-start(bf16[3,128,256]{2,1,0:T(8,128)(2,1)} %reduce_sum.42), calls=%async_computation.2 | async-start | bytes 393216 | tf_op jit(solution)/shard_map/all_to_all | solution.py:138
  97.7 9.7 %all-to-all-done.2 = bf16[3,128,256]{2,1,0:T(8,128)(2,1)S(1)} async-done(((bf16[3,128,256]{2,1,0:T(8,128)(2,1)}), bf16[3,128,256]{2,1,0:T(8,128)(2,1)S(1)}, u32[]{:S(2)}, u32[]{:S(2)}) %all-to-all-start.2) | async-done | bytes 196640 | tf_op jit(solution)/shard_map/all_to_all | solution.py:138
  107.5 0.1 fusion.1
  107.6 13.9 %all_to_all.32.refs_0_ = bf16[4,128,256]{2,1,0:T(8,128)(2,1)S(1)} all-to-all(bf16[4,128,256]{2,1,0:T(8,128)(2,1)S(1)} %broadcast_in_dim.35), channel_id=1, replica_groups={{0,24,48,72},{96,120,144,168},{192,216,240,264},{288,312,336,360},{384,..., dimensions={0} | all-to-all | bytes 524288 | tf_op jit(solution)/shard_map/all_to_all | solution.py:100
  121.6 1.9 collective-permute-start.12
  123.5 3.9 %collective-permute-start.9 = (bf16[4,128,256]{2,1,0:T(8,128)(2,1)S(1)}, bf16[4,128,256]{2,1,0:T(8,128)(2,1)S(1)}, u32[]{:S(2)}, u32[]{:S(2)}) collective-permute-start(bf16[4,128,256]{2,1,0:T(8,128)(2,1)S(1)} %all_to_all.32.refs_0_), channel_id=1, source_target_pairs={{0,672},{24,696},{48,720},{72,744},{96,0},{120,24},{144,48},{168,7... | collective-permute-start | bytes 786440 | tf_op jit(solution)/shard_map/ppermute | solution.py:104
  127.4 2.4 %collective-permute-done.12.refs_8_ = bf16[4,128,256]{2,1,0:T(8,128)(2,1)S(1)} collective-permute-done((bf16[4,128,256]{2,1,0:T(8,128)(2,1)S(1)}, bf16[4,128,256]{2,1,0:T(8,128)(2,1)S(1)}, u32[]{:S(2)}, u32[]{:S(2)}) %collective-permute-start.12) | collective-permute-done | bytes 262176 | tf_op jit(solution)/shard_map/ppermute | solution.py:103
  129.8 3.1 %collective-permute-start.13 = (bf16[4,128,256]{2,1,0:T(8,128)(2,1)S(1)}, bf16[4,128,256]{2,1,0:T(8,128)(2,1)S(1)}, u32[]{:S(2)}, u32[]{:S(2)}) collective-permute-start(bf16[4,128,256]{2,1,0:T(8,128)(2,1)S(1)} %collective-permute-done.12.refs_8_), channel_id=1, source_target_pairs={{0,96},{24,120},{48,144},{72,168},{96,192},{120,216},{144,240},{16... | collective-permute-start | bytes 786440 | tf_op jit(solution)/shard_map/ppermute | solution.py:103
  132.9 0.0 collective-permute-done.9.refs_1_
  133.0 2.7 %collective-permute-start.10 = (bf16[4,128,256]{2,1,0:T(8,128)(2,1)S(1)}, bf16[4,128,256]{2,1,0:T(8,128)(2,1)S(1)}, u32[]{:S(2)}, u32[]{:S(2)}) collective-permute-start(bf16[4,128,256]{2,1,0:T(8,128)(2,1)S(1)} %collective-permute-done.9.refs_1_), channel_id=1, source_target_pairs={{0,672},{24,696},{48,720},{72,744},{96,0},{120,24},{144,48},{168,7... | collective-permute-start | bytes 786440 | tf_op jit(solution)/shard_map/ppermute | solution.py:104
  135.7 2.4 %collective-permute-done.13.refs_7_ = bf16[4,128,256]{2,1,0:T(8,128)(2,1)S(1)} collective-permute-done((bf16[4,128,256]{2,1,0:T(8,128)(2,1)S(1)}, bf16[4,128,256]{2,1,0:T(8,128)(2,1)S(1)}, u32[]{:S(2)}, u32[]{:S(2)}) %collective-permute-start.13) | collective-permute-done | bytes 262176 | tf_op jit(solution)/shard_map/ppermute | solution.py:103
  138.1 4.3 %collective-permute-start.14 = (bf16[4,128,256]{2,1,0:T(8,128)(2,1)S(1)}, bf16[4,128,256]{2,1,0:T(8,128)(2,1)S(1)}, u32[]{:S(2)}, u32[]{:S(2)}) collective-permute-start(bf16[4,128,256]{2,1,0:T(8,128)(2,1)S(1)} %collective-permute-done.13.refs_7_), channel_id=1, source_target_pairs={{0,96},{24,120},{48,144},{72,168},{96,192},{120,216},{144,240},{16... | collective-permute-start | bytes 786440 | tf_op jit(solution)/shard_map/ppermute | solution.py:103
  142.4 0.0 collective-permute-done.10.refs_2_
  142.4 1.9 collective-permute-start.11
  144.4 2.6 %collective-permute-done.14.refs_6_ = bf16[4,128,256]{2,1,0:T(8,128)(2,1)S(1)} collective-permute-done((bf16[4,128,256]{2,1,0:T(8,128)(2,1)S(1)}, bf16[4,128,256]{2,1,0:T(8,128)(2,1)S(1)}, u32[]{:S(2)}, u32[]{:S(2)}) %collective-permute-start.14) | collective-permute-done | bytes 262176 | tf_op jit(solution)/shard_map/ppermute | solution.py:103
  147.0 4.9 %collective-permute-start.15 = (bf16[2,128,256]{2,1,0:T(8,128)(2,1)S(1)}, bf16[2,128,256]{2,1,0:T(8,128)(2,1)S(1)}, u32[]{:S(2)}, u32[]{:S(2)}) collective-permute-start(bf16[2,128,256]{2,1,0:T(8,128)(2,1)S(1)} %slice.18), channel_id=1, source_target_pairs={{0,96},{24,120},{48,144},{72,168},{96,192},{120,216},{144,240},{16... | collective-permute-start | bytes 393224 | tf_op jit(solution)/shard_map/ppermute | solution.py:105
  151.9 0.0 collective-permute-done.11.refs_3_
  151.9 1.9 collective-permute-start.16
  153.9 0.5 collective-permute-done.15.refs_4_
  154.4 5.6 %collective-permute-done.16.refs_5_ = bf16[2,128,256]{2,1,0:T(8,128)(2,1)S(1)} collective-permute-done((bf16[2,128,256]{2,1,0:T(8,128)(2,1)S(1)}, bf16[2,128,256]{2,1,0:T(8,128)(2,1)S(1)}, u32[]{:S(2)}, u32[]{:S(2)}) %collective-permute-start.16) | collective-permute-done | bytes 131104 | tf_op jit(solution)/shard_map/ppermute | solution.py:106
  160.0 2.1 %copy-done.2 = bf16[1,1,24,5,128,128]{5,4,3,2,1,0:T(8,128)(2,1)S(1)} copy-done((bf16[1,1,24,5,128,128]{5,4,3,2,1,0:T(8,128)(2,1)S(1)}, bf16[1,1,24,5,128,128]{5,4,3,2,1,0:T(8,128)(2,1)}, u32[]{:S(2)}) %copy-start.2) | copy-done | bytes 3932184
  162.1 2.5 %shard_map.76 = bf16[12,128,256]{2,1,0:T(8,128)(2,1)S(1)} custom-call(s32[1]{0:T(128)S(6)} %sub.24.parity, s32[120]{0:T(128)S(1)} %fusion.3.slots, bf16[12,2,5,128,128]{4,3,2,1,0:T(8,128)(2,1)S(1)} %bitcast.9, bf16[4,128,256]{2,1,0:T(8,128)(2,1)S(1)} %all_to_all.32.refs_0_, bf16[4,128,256]{2,1,0:T(8,128)(2,1)S(1)} %collective-permute-done.9.refs_1_, ...), custom_call_target="tpu_custom_call" | custom-call | flops 503316480 | bytes 6291456 | tf_op jit(solution)/shard_map/pallas_call | solution.py:85
  164.6 1.9 collective-permute-start.17
  166.5 2.5 %shard_map.75 = f32[12,128,256]{2,1,0:T(8,128)S(1)} custom-call(s32[1]{0:T(128)} %bitcast.parity, s32[120]{0:T(128)S(1)} %fusion.3.slots, bf16[12,2,5,128,128]{4,3,2,1,0:T(8,128)(2,1)S(1)} %bitcast.10, bf16[4,128,256]{2,1,0:T(8,128)(2,1)S(1)} %all_to_all.32.refs_0_, bf16[4,128,256]{2,1,0:T(8,128)(2,1)S(1)} %collective-permute-done.9.refs_1_, ...), custom_call_target="tpu_custom_call" | custom-call | flops 503316480 | bytes 6291456 | tf_op jit(solution)/shard_map/pallas_call | solution.py:85
  169.0 0.0 collective-permute-done.17
  169.0 0.2 add_convert_fusion
  169.3 15.6 %all_to_all.33 = bf16[4,3,128,256]{3,2,1,0:T(8,128)(2,1)S(1)} all-to-all(bf16[4,3,128,256]{3,2,1,0:T(8,128)(2,1)S(1)} %bitcast.12), channel_id=1, replica_groups={{0,6,12,18},{1,7,13,19},{2,8,14,20},{3,9,15,21},{4,10,16,22},{5,11,17,2..., dimensions={0} | all-to-all | bytes 1572864 | tf_op jit(solution)/shard_map/all_to_all | solution.py:136
  184.9 0.2 reduce_sum.44
  185.1 13.1 %all_to_all.34 = bf16[3,128,256]{2,1,0:T(8,128)(2,1)S(1)} all-to-all(bf16[3,128,256]{2,1,0:T(8,128)(2,1)S(1)} %reduce_sum.44), channel_id=1, replica_groups={{0,2,4},{1,3,5},{6,8,10},{7,9,11},{12,14,16},{13,15,17},{18,20,22},{19,..., dimensions={0} | all-to-all | bytes 393216 | tf_op jit(solution)/shard_map/all_to_all | solution.py:138
  198.2 0.8 convert_select_fusion
  (19 shorter events, 0.2 us)
Async XLA Ops:
  17.6 8.6 %collective-permute-start.3 = (bf16[4,128,256]{2,1,0:T(8,128)(2,1)S(1)}, bf16[4,128,256]{2,1,0:T(8,128)(2,1)S(1)}, u32[]{:S(2)}, u32[]{:S(2)}) collective-permute-start(bf16[4,128,256]{2,1,0:T(8,128)(2,1)S(1)} %all_to_all.30.refs_0_), channel_id=1, source_target_pairs={{0,96},{24,120},{48,144},{72,168},{96,192},{120,216},{144,240},{16... | collective-permute-start | bytes 786440 | tf_op jit(solution)/shard_map/ppermute | solution.py:103
  22.3 9.5 %collective-permute-start = (bf16[4,128,256]{2,1,0:T(8,128)(2,1)S(1)}, bf16[4,128,256]{2,1,0:T(8,128)(2,1)S(1)}, u32[]{:S(2)}, u32[]{:S(2)}) collective-permute-start(bf16[4,128,256]{2,1,0:T(8,128)(2,1)S(1)} %all_to_all.30.refs_0_), channel_id=1, source_target_pairs={{0,672},{24,696},{48,720},{72,744},{96,0},{120,24},{144,48},{168,7... | collective-permute-start | bytes 786440 | tf_op jit(solution)/shard_map/ppermute | solution.py:104
  26.2 9.5 %collective-permute-start.4 = (bf16[4,128,256]{2,1,0:T(8,128)(2,1)S(1)}, bf16[4,128,256]{2,1,0:T(8,128)(2,1)S(1)}, u32[]{:S(2)}, u32[]{:S(2)}) collective-permute-start(bf16[4,128,256]{2,1,0:T(8,128)(2,1)S(1)} %collective-permute-done.3.refs_8_), channel_id=1, source_target_pairs={{0,96},{24,120},{48,144},{72,168},{96,192},{120,216},{144,240},{16... | collective-permute-start | bytes 786440 | tf_op jit(solution)/shard_map/ppermute | solution.py:103
  31.8 9.5 %collective-permute-start.1 = (bf16[4,128,256]{2,1,0:T(8,128)(2,1)S(1)}, bf16[4,128,256]{2,1,0:T(8,128)(2,1)S(1)}, u32[]{:S(2)}, u32[]{:S(2)}) collective-permute-start(bf16[4,128,256]{2,1,0:T(8,128)(2,1)S(1)} %collective-permute-done.refs_1_), channel_id=1, source_target_pairs={{0,672},{24,696},{48,720},{72,744},{96,0},{120,24},{144,48},{168,7... | collective-permute-start | bytes 786440 | tf_op jit(solution)/shard_map/ppermute | solution.py:104
  35.6 9.6 %collective-permute-start.5 = (bf16[4,128,256]{2,1,0:T(8,128)(2,1)S(1)}, bf16[4,128,256]{2,1,0:T(8,128)(2,1)S(1)}, u32[]{:S(2)}, u32[]{:S(2)}) collective-permute-start(bf16[4,128,256]{2,1,0:T(8,128)(2,1)S(1)} %collective-permute-done.4.refs_7_), channel_id=1, source_target_pairs={{0,96},{24,120},{48,144},{72,168},{96,192},{120,216},{144,240},{16... | collective-permute-start | bytes 786440 | tf_op jit(solution)/shard_map/ppermute | solution.py:103
  41.3 9.8 %collective-permute-start.2 = (bf16[4,128,256]{2,1,0:T(8,128)(2,1)S(1)}, bf16[4,128,256]{2,1,0:T(8,128)(2,1)S(1)}, u32[]{:S(2)}, u32[]{:S(2)}) collective-permute-start(bf16[4,128,256]{2,1,0:T(8,128)(2,1)S(1)} %collective-permute-done.1.refs_2_), channel_id=1, source_target_pairs={{0,672},{24,696},{48,720},{72,744},{96,0},{120,24},{144,48},{168,7... | collective-permute-start | bytes 786440 | tf_op jit(solution)/shard_map/ppermute | solution.py:104
  45.2 8.1 %collective-permute-start.6 = (bf16[2,128,256]{2,1,0:T(8,128)(2,1)S(1)}, bf16[2,128,256]{2,1,0:T(8,128)(2,1)S(1)}, u32[]{:S(2)}, u32[]{:S(2)}) collective-permute-start(bf16[2,128,256]{2,1,0:T(8,128)(2,1)S(1)} %slice.16), channel_id=1, source_target_pairs={{0,96},{24,120},{48,144},{72,168},{96,192},{120,216},{144,240},{16... | collective-permute-start | bytes 393224 | tf_op jit(solution)/shard_map/ppermute | solution.py:105
  51.1 8.1 %collective-permute-start.7 = (bf16[2,128,256]{2,1,0:T(8,128)(2,1)S(1)}, bf16[2,128,256]{2,1,0:T(8,128)(2,1)S(1)}, u32[]{:S(2)}, u32[]{:S(2)}) collective-permute-start(bf16[2,128,256]{2,1,0:T(8,128)(2,1)S(1)} %slice.17), channel_id=1, source_target_pairs={{0,672},{24,696},{48,720},{72,744},{96,0},{120,24},{144,48},{168,7... | collective-permute-start | bytes 393224 | tf_op jit(solution)/shard_map/ppermute | solution.py:106
  59.2 2.1 %copy-start = (bf16[1,1,24,5,128,128]{5,4,3,2,1,0:T(8,128)(2,1)S(1)}, bf16[1,1,24,5,128,128]{5,4,3,2,1,0:T(8,128)(2,1)}, u32[]{:S(2)}) copy-start(bf16[1,1,24,5,128,128]{5,4,3,2,1,0:T(8,128)(2,1)} %param.11) | copy-start | bytes 11796484
  61.3 4.4 %copy-start.1 = (bf16[1,1,24,5,128,128]{5,4,3,2,1,0:T(8,128)(2,1)S(1)}, bf16[1,1,24,5,128,128]{5,4,3,2,1,0:T(8,128)(2,1)}, u32[]{:S(2)}) copy-start(bf16[1,1,24,5,128,128]{5,4,3,2,1,0:T(8,128)(2,1)} %param.11) | copy-start | bytes 11796484
  63.8 4.4 %collective-permute-start.8 = (bf16[12,128,256]{2,1,0:T(8,128)(2,1)S(1)}, bf16[12,128,256]{2,1,0:T(8,128)(2,1)S(1)}, u32[]{:S(2)}, u32[]{:S(2)}) collective-permute-start(bf16[12,128,256]{2,1,0:T(8,128)(2,1)S(1)} %shard_map.74), channel_id=1, source_target_pairs={{0,1},{1,0},{2,3},{3,2},{4,5},{5,4},{6,7},{7,6},{8,9},{9,8},{10,11... | collective-permute-start | bytes 2359304 | tf_op jit(solution)/shard_map/ppermute | solution.py:132
  68.4 29.3 %copy-start.6 = (s32[128]{0:T(128)S(1)}, s32[128]{0:T(128)}, u32[]{:S(2)}) copy-start(s32[128]{0:T(128)} %param.9) | copy-start | bytes 1540
  68.4 39.0 %copy-start.4 = (f32[128,256]{1,0:T(8,128)S(1)}, f32[128,256]{1,0:T(8,128)}, u32[]{:S(2)}) copy-start(f32[128,256]{1,0:T(8,128)} %param.7) | copy-start | bytes 393220
  68.5 39.0 %copy-start.5 = (s32[128]{0:T(128)S(1)}, s32[128]{0:T(128)}, u32[]{:S(2)}) copy-start(s32[128]{0:T(128)} %param.10) | copy-start | bytes 1540
  86.5 21.0 %all-to-all-start.2 = ((bf16[3,128,256]{2,1,0:T(8,128)(2,1)}), bf16[3,128,256]{2,1,0:T(8,128)(2,1)S(1)}, u32[]{:S(2)}, u32[]{:S(2)}) async-start(bf16[3,128,256]{2,1,0:T(8,128)(2,1)} %reduce_sum.42), calls=%async_computation.2 | async-start | bytes 393216 | tf_op jit(solution)/shard_map/all_to_all | solution.py:138
  121.6 8.3 %collective-permute-start.12 = (bf16[4,128,256]{2,1,0:T(8,128)(2,1)S(1)}, bf16[4,128,256]{2,1,0:T(8,128)(2,1)S(1)}, u32[]{:S(2)}, u32[]{:S(2)}) collective-permute-start(bf16[4,128,256]{2,1,0:T(8,128)(2,1)S(1)} %all_to_all.32.refs_0_), channel_id=1, source_target_pairs={{0,96},{24,120},{48,144},{72,168},{96,192},{120,216},{144,240},{16... | collective-permute-start | bytes 786440 | tf_op jit(solution)/shard_map/ppermute | solution.py:103
  123.5 9.5 %collective-permute-start.9 = (bf16[4,128,256]{2,1,0:T(8,128)(2,1)S(1)}, bf16[4,128,256]{2,1,0:T(8,128)(2,1)S(1)}, u32[]{:S(2)}, u32[]{:S(2)}) collective-permute-start(bf16[4,128,256]{2,1,0:T(8,128)(2,1)S(1)} %all_to_all.32.refs_0_), channel_id=1, source_target_pairs={{0,672},{24,696},{48,720},{72,744},{96,0},{120,24},{144,48},{168,7... | collective-permute-start | bytes 786440 | tf_op jit(solution)/shard_map/ppermute | solution.py:104
  129.8 8.3 %collective-permute-start.13 = (bf16[4,128,256]{2,1,0:T(8,128)(2,1)S(1)}, bf16[4,128,256]{2,1,0:T(8,128)(2,1)S(1)}, u32[]{:S(2)}, u32[]{:S(2)}) collective-permute-start(bf16[4,128,256]{2,1,0:T(8,128)(2,1)S(1)} %collective-permute-done.12.refs_8_), channel_id=1, source_target_pairs={{0,96},{24,120},{48,144},{72,168},{96,192},{120,216},{144,240},{16... | collective-permute-start | bytes 786440 | tf_op jit(solution)/shard_map/ppermute | solution.py:103
  133.0 9.5 %collective-permute-start.10 = (bf16[4,128,256]{2,1,0:T(8,128)(2,1)S(1)}, bf16[4,128,256]{2,1,0:T(8,128)(2,1)S(1)}, u32[]{:S(2)}, u32[]{:S(2)}) collective-permute-start(bf16[4,128,256]{2,1,0:T(8,128)(2,1)S(1)} %collective-permute-done.9.refs_1_), channel_id=1, source_target_pairs={{0,672},{24,696},{48,720},{72,744},{96,0},{120,24},{144,48},{168,7... | collective-permute-start | bytes 786440 | tf_op jit(solution)/shard_map/ppermute | solution.py:104
  138.1 8.9 %collective-permute-start.14 = (bf16[4,128,256]{2,1,0:T(8,128)(2,1)S(1)}, bf16[4,128,256]{2,1,0:T(8,128)(2,1)S(1)}, u32[]{:S(2)}, u32[]{:S(2)}) collective-permute-start(bf16[4,128,256]{2,1,0:T(8,128)(2,1)S(1)} %collective-permute-done.13.refs_7_), channel_id=1, source_target_pairs={{0,96},{24,120},{48,144},{72,168},{96,192},{120,216},{144,240},{16... | collective-permute-start | bytes 786440 | tf_op jit(solution)/shard_map/ppermute | solution.py:103
  142.4 9.5 %collective-permute-start.11 = (bf16[4,128,256]{2,1,0:T(8,128)(2,1)S(1)}, bf16[4,128,256]{2,1,0:T(8,128)(2,1)S(1)}, u32[]{:S(2)}, u32[]{:S(2)}) collective-permute-start(bf16[4,128,256]{2,1,0:T(8,128)(2,1)S(1)} %collective-permute-done.10.refs_2_), channel_id=1, source_target_pairs={{0,672},{24,696},{48,720},{72,744},{96,0},{120,24},{144,48},{168,7... | collective-permute-start | bytes 786440 | tf_op jit(solution)/shard_map/ppermute | solution.py:104
  147.0 7.4 %collective-permute-start.15 = (bf16[2,128,256]{2,1,0:T(8,128)(2,1)S(1)}, bf16[2,128,256]{2,1,0:T(8,128)(2,1)S(1)}, u32[]{:S(2)}, u32[]{:S(2)}) collective-permute-start(bf16[2,128,256]{2,1,0:T(8,128)(2,1)S(1)} %slice.18), channel_id=1, source_target_pairs={{0,96},{24,120},{48,144},{72,168},{96,192},{120,216},{144,240},{16... | collective-permute-start | bytes 393224 | tf_op jit(solution)/shard_map/ppermute | solution.py:105
  151.9 8.1 %collective-permute-start.16 = (bf16[2,128,256]{2,1,0:T(8,128)(2,1)S(1)}, bf16[2,128,256]{2,1,0:T(8,128)(2,1)S(1)}, u32[]{:S(2)}, u32[]{:S(2)}) collective-permute-start(bf16[2,128,256]{2,1,0:T(8,128)(2,1)S(1)} %slice.19), channel_id=1, source_target_pairs={{0,672},{24,696},{48,720},{72,744},{96,0},{120,24},{144,48},{168,7... | collective-permute-start | bytes 393224 | tf_op jit(solution)/shard_map/ppermute | solution.py:106
  160.0 2.1 %copy-start.2 = (bf16[1,1,24,5,128,128]{5,4,3,2,1,0:T(8,128)(2,1)S(1)}, bf16[1,1,24,5,128,128]{5,4,3,2,1,0:T(8,128)(2,1)}, u32[]{:S(2)}) copy-start(bf16[1,1,24,5,128,128]{5,4,3,2,1,0:T(8,128)(2,1)} %param.11) | copy-start | bytes 11796484
  162.1 4.4 %copy-start.3 = (bf16[1,1,24,5,128,128]{5,4,3,2,1,0:T(8,128)(2,1)S(1)}, bf16[1,1,24,5,128,128]{5,4,3,2,1,0:T(8,128)(2,1)}, u32[]{:S(2)}) copy-start(bf16[1,1,24,5,128,128]{5,4,3,2,1,0:T(8,128)(2,1)} %param.11) | copy-start | bytes 11796484
  164.6 4.4 %collective-permute-start.17 = (bf16[12,128,256]{2,1,0:T(8,128)(2,1)S(1)}, bf16[12,128,256]{2,1,0:T(8,128)(2,1)S(1)}, u32[]{:S(2)}, u32[]{:S(2)}) collective-permute-start(bf16[12,128,256]{2,1,0:T(8,128)(2,1)S(1)} %shard_map.76), channel_id=1, source_target_pairs={{0,1},{1,0},{2,3},{3,2},{4,5},{5,4},{6,7},{7,6},{8,9},{9,8},{10,11... | collective-permute-start | bytes 2359304 | tf_op jit(solution)/shard_map/ppermute | solution.py:132

commit v2 on v1

v2 whole, which is shorter than its diff:
```python
import jax
import jax.numpy as jnp
from jax import lax
from jax.experimental import pallas as pl
from jax.experimental.pallas import tpu as pltpu
from jax.sharding import PartitionSpec as P

SWEEPS = 2
RETAIN = 0.8
VMEM_LIMIT = 56 * 1024 * 1024

Y, ZL, X, ZH, CORES = 8, 4, 4, 3, 2
LIVE = Y * ZL

Z_GROUPS = [[y * ZL + z for z in range(ZL)] for y in range(Y)]
H_GROUPS = [
    [(x * ZH + z) * CORES + c for z in range(ZH)] for x in range(X) for c in range(CORES)
]


def along_y(partner):
    return [(y * ZL + z, partner(y) * ZL + z) for y in range(Y) for z in range(ZL)]


def along_x(flip):
    rest = ZH * CORES
    return [(x * rest + i, (x ^ flip) * rest + i) for x in range(X) for i in range(rest)]


Y_EVEN = along_y(lambda y: y ^ 1)
Y_ODD = along_y(lambda y: (y - 1 if y % 2 == 0 else y + 1) % Y)
X_EVEN, X_ODD = along_x(1), along_x(3)
SWAP = [(d, d ^ 1) for d in range(X * ZH * CORES)]

PIECE_AT = (0, 4, 8, 12, 16, 18, 20, 24, 28)
PIECE_LEN = (4, 4, 4, 4, 2, 2, 4, 4, 4)


def sum_kernel(place, slots, weights, *refs):
    pieces = refs[: len(PIECE_AT)]
    out, blocks, sems = refs[len(PIECE_AT) :]
    step = pl.program_id(0)

    @pl.when(step == 0)
    def _():
        copies = [
            pltpu.make_async_copy(piece, blocks.at[pl.ds(at, count)], sems.at[i])
            for i, (piece, at, count) in enumerate(zip(pieces, PIECE_AT, PIECE_LEN))
        ]
        for copy in copies:
            copy.start()
        blocks[LIVE] = jnp.zeros(blocks.shape[1:], blocks.dtype)
        for copy in copies:
            copy.wait()

    depth = weights.shape[2]
    for q in range(ZH):
        base = (((step ^ place[0]) * ZH + q) * CORES + place[1]) * depth
        total = None
        for t in range(0, depth, 2):
            group = range(t, min(t + 2, depth))
            left = jnp.concatenate([weights[q, 0, u] for u in group], axis=1)
            right = jnp.concatenate([blocks[slots[base + u]] for u in group], axis=0)
            term = jnp.dot(left, right, preferred_element_type=jnp.float32)
            total = term if total is None else total + term
        out[0, q] = total.astype(out.dtype)


def partial_sums(place, slots, weights, pieces, dtype):
    _, _, depth, size, _ = weights.shape
    classes = pieces[0].shape[-1]
    grid_spec = pltpu.PrefetchScalarGridSpec(
        num_scalar_prefetch=2,
        grid=(X,),
        in_specs=[
            pl.BlockSpec(
                (ZH, 1, depth, size, size),
                lambda i, place, slots: (i ^ place[0], place[1], 0, 0, 0),
            )
        ]
        + [pl.BlockSpec(memory_space=pl.ANY)] * len(pieces),
        out_specs=pl.BlockSpec((1, ZH, size, classes), lambda i, place, slots: (i, 0, 0, 0)),
        scratch_shapes=[
            pltpu.VMEM((LIVE + 1, size, classes), jnp.bfloat16),
            pltpu.SemaphoreType.DMA((len(pieces),)),
        ],
    )
    return pl.pallas_call(
        sum_kernel,
        grid_spec=grid_spec,
        out_shape=jax.ShapeDtypeStruct((X, ZH, size, classes), dtype),
        compiler_params=pltpu.CompilerParams(vmem_limit_bytes=VMEM_LIMIT),
        cost_estimate=pl.CostEstimate(
            flops=2 * X * ZH * depth * size * size * classes,
            bytes_accessed=6 * 1024 * 1024,
            transcendentals=0,
        ),
    )(place, slots, weights, *pieces)


def gather_blocks(outgoing):
    spread = jnp.broadcast_to(outgoing[None], (ZL,) + outgoing.shape)
    own = lax.all_to_all(spread, "src", 0, 0, axis_index_groups=Z_GROUPS)
    even, odd = [own], [own]
    for _ in range(3):
        over_even = lax.ppermute(odd[-1], "src", Y_EVEN)
        over_odd = lax.ppermute(even[-1], "src", Y_ODD)
        even.append(over_even)
        odd.append(over_odd)
    half = ZL // 2
    far_even = lax.ppermute(odd[3][:half], "src", Y_EVEN)
    far_odd = lax.ppermute(even[3][half:], "src", Y_ODD)
    return [own, even[1], even[2], even[3], far_even, far_odd, odd[3], odd[2], odd[1]]


def reduce_over_x(chip):
    half = chip.shape[-1] // 2
    first, second = chip[..., :half], chip[..., half:]
    wire = jnp.bfloat16
    near_a = lax.ppermute(first[1:3].astype(wire), "dst", X_EVEN)
    near_b = lax.ppermute(second[2:4].astype(wire), "dst", X_ODD)
    pass_a = (first[3] + near_a[1].astype(jnp.float32)).astype(wire)
    far_a = lax.ppermute(pass_a, "dst", X_ODD)
    pass_b = (second[1] + near_b[0].astype(jnp.float32)).astype(wire)
    far_b = lax.ppermute(pass_b, "dst", X_EVEN)
    whole_a = first[0] + near_a[0].astype(jnp.float32) + far_a.astype(jnp.float32)
    whole_b = second[0] + near_b[1].astype(jnp.float32) + far_b.astype(jnp.float32)
    return jnp.concatenate([whole_a, whole_b], axis=-1)


def per_device(prior, degrees, seed_mask, seed_labels, adjacency, block_cols, slot_counts):
    classes = prior.shape[1]
    depth, size = adjacency.shape[3], adjacency.shape[4]
    weights = adjacency.reshape(X * ZH, CORES, depth, size, size)
    dst = lax.axis_index("dst").astype(jnp.int32)
    x, core = dst // (ZH * CORES), dst % CORES
    mine = jnp.stack([x, core])
    other = jnp.stack([x, 1 - core])
    y = (lax.axis_index("src") // ZL).astype(jnp.int32)
    toward = 1 - 2 * (y % 2)
    columns = block_cols[0, 0]
    relative = ((columns // ZL - y) * toward + Y) % Y * ZL + columns % ZL
    active = jnp.arange(depth, dtype=jnp.int32)[None, :] < slot_counts[0, 0][:, None]
    slots = jnp.where(active, relative, LIVE).astype(jnp.int32).reshape(-1)
    inverse_root = lax.rsqrt(degrees.astype(jnp.float32))[:, None]
    onehot = (seed_labels[:, None] == jnp.arange(classes, dtype=jnp.int32)[None, :]).astype(
        jnp.float32
    )
    seeded = seed_mask[:, None] > 0
    scores = prior
    for _ in range(SWEEPS):
        outgoing = (inverse_root * scores).astype(jnp.bfloat16)
        pieces = gather_blocks(outgoing)
        send = partial_sums(other, slots, weights, pieces, jnp.bfloat16)
        swapped = lax.ppermute(send, "dst", SWAP)
        keep = partial_sums(mine, slots, weights, pieces, jnp.float32)
        chip = keep + swapped.astype(jnp.float32)
        rows = reduce_over_x(chip).astype(jnp.bfloat16)
        parts = lax.all_to_all(rows, "dst", 0, 0, axis_index_groups=H_GROUPS)
        summed = jnp.sum(parts.astype(jnp.float32), axis=0)
        hidden = RETAIN * inverse_root * summed + (1.0 - RETAIN) * prior
        scores = jnp.where(seeded, onehot, hidden)
    return scores


def solution(mesh):
    in_specs = (
        P(("src", "dst"), None),
        P(("src", "dst")),
        P(("src", "dst")),
        P(("src", "dst")),
        P("src", "dst", None, None, None, None),
        P("src", "dst", None, None),
        P("src", "dst", None),
    )
    out_specs = P(("src", "dst"), None)
    return jax.shard_map(
        per_device, mesh=mesh, in_specs=in_specs, out_specs=out_specs, check_vma=False
    )
```

time: 200 us -> 233 us (1.17)
  blocking collectives: 75.7 us -> 39.3 us
  waiting for transfers between devices: 33.9 us -> 68.8 us
  Pallas kernels: 9.84 us -> 26.1 us
  starting transfers between devices: 68.9 us -> 84.1 us
  other arithmetic: 4.85 us -> 9.52 us
  local copies, waits for them, and re-layouts: 5.29 us -> 2.56 us
    ppermute x16 -> x24, waiting for transfers between devices: 24.2 us -> 59.6 us  [the longest x6 17.4 us: gather_blocks(): over_odd = lax.ppermute(even[-1], 'src', Y_ODD)]
    all_to_all x2 -> x0, blocking collectives: 32.8 us -> none  [per_device(): rows = lax.all_to_all(chip, 'dst', 0, 0, axis_index_groups=X_GROUPS)]
    pallas_call x4, Pallas kernels: 9.84 us -> 26.1 us  [partial_sums(): pl.pallas_call(sum_kernel, grid_spec=grid_spec, out_shape=jax.ShapeDtypeS...]
    ppermute x16 -> x24, starting transfers between devices: 53.8 us -> 69 us  [the longest x6 21.3 us: gather_blocks(): over_odd = lax.ppermute(even[-1], 'src', Y_ODD)]
    another operation x0 -> x6, other arithmetic: none -> 4.73 us
    all_to_all x2, blocking collectives: 29.9 us -> 25.6 us  [gather_blocks(): own = lax.all_to_all(spread, 'src', 0, 0, axis_index_groups=Z_GROUPS)]
    unnamed x15 -> x43, local copies, waits for them, and re-layouts: 5.02 us -> 2.12 us
  transfers between devices with their start and end apart: 19 -> 27, of which waited for: 12 -> 22; matrix products, arithmetic and copies ran while one was open for 1% -> 2% of each run, Pallas kernels for 2% -> 6%
where the time goes in v2:
time: 233 us; the launch traced here: 231 us
  starting transfers between devices  84.1 us (36%)
  waiting for transfers between devices  68.8 us (30%)
  blocking collectives  39.3 us (17%)
  Pallas kernels  26.1 us (11%)
  other arithmetic  9.52 us (4%)
  local copies, waits for them, and re-layouts  2.56 us (1%)
    pallas_call x4, Pallas kernels, partial_sums(): pl.pallas_call(sum_kernel, grid_spec=grid_spec, out_shape=jax.ShapeDtypeS...  26.1 us
    all_to_all x2, blocking collectives, gather_blocks(): own = lax.all_to_all(spread, 'src', 0, 0, axis_index_groups=Z_GROUPS)  25.6 us
    ppermute x6, starting transfers between devices, gather_blocks(): over_odd = lax.ppermute(even[-1], 'src', Y_ODD)  21.3 us
    ppermute x6, waiting for transfers between devices, gather_blocks(): over_odd = lax.ppermute(even[-1], 'src', Y_ODD)  17.4 us
    all_to_all x1, blocking collectives, per_device(): parts = lax.all_to_all(rows, 'dst', 0, 0, axis_index_groups=H_GROUPS)  13.7 us
    ppermute x6, starting transfers between devices, gather_blocks(): over_even = lax.ppermute(odd[-1], 'src', Y_EVEN)  11.5 us
    all_to_all x1, starting transfers between devices, per_device(): parts = lax.all_to_all(rows, 'dst', 0, 0, axis_index_groups=H_GROUPS)  11.2 us
    ppermute x6, waiting for transfers between devices, gather_blocks(): over_even = lax.ppermute(odd[-1], 'src', Y_EVEN)  10.9 us
  transfers between devices with their start and end apart: 27, of which 22 were waited for; matrix products, arithmetic and copies ran while one was open for 2% of the time, Pallas kernels for 6%

profile of v2, /device:TPU:24, one launch (start us, length us, event | category | flops | bytes accessed | tf_op | source)
XLA Modules:
  0.0 230.9 jit_solution(17676695843820968366)
XLA Ops:
  0.0 0.7 broadcast_multiply_fusion
  0.7 1.0 multiply_convert_fusion
  1.7 15.9 %all_to_all.20.refs_0_ = bf16[4,128,256]{2,1,0:T(8,128)(2,1)S(1)} all-to-all(bf16[4,128,256]{2,1,0:T(8,128)(2,1)S(1)} %broadcast_in_dim.34), channel_id=1, replica_groups={{0,24,48,72},{96,120,144,168},{192,216,240,264},{288,312,336,360},{384,..., dimensions={0} | all-to-all | bytes 524288 | tf_op jit(solution)/shard_map/all_to_all | solution.py:103
  17.6 4.7 %collective-permute-start.1 = (bf16[4,128,256]{2,1,0:T(8,128)(2,1)S(1)}, bf16[4,128,256]{2,1,0:T(8,128)(2,1)S(1)}, u32[]{:S(2)}, u32[]{:S(2)}) collective-permute-start(bf16[4,128,256]{2,1,0:T(8,128)(2,1)S(1)} %all_to_all.20.refs_0_), channel_id=1, source_target_pairs={{0,672},{24,696},{48,720},{72,744},{96,192},{120,216},{144,240},{1... | collective-permute-start | bytes 786440 | tf_op jit(solution)/shard_map/ppermute | solution.py:107
  22.3 1.9 collective-permute-start
  24.2 2.8 %collective-permute-done.1.refs_8_ = bf16[4,128,256]{2,1,0:T(8,128)(2,1)S(1)} collective-permute-done((bf16[4,128,256]{2,1,0:T(8,128)(2,1)S(1)}, bf16[4,128,256]{2,1,0:T(8,128)(2,1)S(1)}, u32[]{:S(2)}, u32[]{:S(2)}) %collective-permute-start.1) | collective-permute-done | bytes 262176 | tf_op jit(solution)/shard_map/ppermute | solution.py:107
  27.1 1.9 collective-permute-start.2
  29.0 4.2 %collective-permute-done.refs_1_ = bf16[4,128,256]{2,1,0:T(8,128)(2,1)S(1)} collective-permute-done((bf16[4,128,256]{2,1,0:T(8,128)(2,1)S(1)}, bf16[4,128,256]{2,1,0:T(8,128)(2,1)S(1)}, u32[]{:S(2)}, u32[]{:S(2)}) %collective-permute-start) | collective-permute-done | bytes 262176 | tf_op jit(solution)/shard_map/ppermute | solution.py:106
  33.2 1.9 collective-permute-start.3
  35.1 1.1 collective-permute-done.2.refs_2_
  36.2 4.1 %collective-permute-start.5 = (bf16[4,128,256]{2,1,0:T(8,128)(2,1)S(1)}, bf16[4,128,256]{2,1,0:T(8,128)(2,1)S(1)}, u32[]{:S(2)}, u32[]{:S(2)}) collective-permute-start(bf16[4,128,256]{2,1,0:T(8,128)(2,1)S(1)} %collective-permute-done.2.refs_2_), channel_id=1, source_target_pairs={{0,672},{24,696},{48,720},{72,744},{96,192},{120,216},{144,240},{1... | collective-permute-start | bytes 786440 | tf_op jit(solution)/shard_map/ppermute | solution.py:107
  40.3 4.8 %collective-permute-done.3.refs_7_ = bf16[4,128,256]{2,1,0:T(8,128)(2,1)S(1)} collective-permute-done((bf16[4,128,256]{2,1,0:T(8,128)(2,1)S(1)}, bf16[4,128,256]{2,1,0:T(8,128)(2,1)S(1)}, u32[]{:S(2)}, u32[]{:S(2)}) %collective-permute-start.3) | collective-permute-done | bytes 262176 | tf_op jit(solution)/shard_map/ppermute | solution.py:107
  45.0 1.9 collective-permute-start.4
  47.0 0.8 copy.9
  47.8 0.7 iota_compare_fusion.1
  48.7 3.9 %collective-permute-start.6 = (bf16[2,128,256]{2,1,0:T(8,128)(2,1)S(1)}, bf16[2,128,256]{2,1,0:T(8,128)(2,1)S(1)}, u32[]{:S(2)}, u32[]{:S(2)}) collective-permute-start(bf16[2,128,256]{2,1,0:T(8,128)(2,1)S(1)} %slice.116), channel_id=1, source_target_pairs={{0,96},{24,120},{48,144},{72,168},{96,0},{120,24},{144,48},{168,72... | collective-permute-start | bytes 393224 | tf_op jit(solution)/shard_map/ppermute | solution.py:111
  52.6 0.8 collective-permute-done.4.refs_3_
  53.5 2.4 %collective-permute-start.7 = (bf16[2,128,256]{2,1,0:T(8,128)(2,1)S(1)}, bf16[2,128,256]{2,1,0:T(8,128)(2,1)S(1)}, u32[]{:S(2)}, u32[]{:S(2)}) collective-permute-start(bf16[2,128,256]{2,1,0:T(8,128)(2,1)S(1)} %slice.117), channel_id=1, source_target_pairs={{0,672},{24,696},{48,720},{72,744},{96,192},{120,216},{144,240},{1... | collective-permute-start | bytes 393224 | tf_op jit(solution)/shard_map/ppermute | solution.py:112
  57.1 4.5 %collective-permute-done.7.refs_5_ = bf16[2,128,256]{2,1,0:T(8,128)(2,1)S(1)} collective-permute-done((bf16[2,128,256]{2,1,0:T(8,128)(2,1)S(1)}, bf16[2,128,256]{2,1,0:T(8,128)(2,1)S(1)}, u32[]{:S(2)}, u32[]{:S(2)}) %collective-permute-start.7) | collective-permute-done | bytes 131104 | tf_op jit(solution)/shard_map/ppermute | solution.py:112
  62.2 6.4 %shard_map.74 = bf16[4,3,128,256]{3,2,1,0:T(8,128)(2,1)} custom-call(s32[2]{0:T(128)} %pad_add_fusion.1.place, s32[120]{0:T(128)} %fusion.23.slots, bf16[12,2,5,128,128]{4,3,2,1,0:T(8,128)(2,1)} %bitcast.39, bf16[4,128,256]{2,1,0:T(8,128)(2,1)} %copy-done, bf16[4,128,256]{2,1,0:T(8,128)(2,1)} %copy-done.8, bf16[4,128,256]{2,1,0:T(8,128)(2,1)} %copy-done.9, ...), custom_call_target="tpu_custom_call" | custom-call | flops 503316480 | bytes 6291456 | tf_op jit(solution)/shard_map/pallas_call | solution.py:88
  68.7 1.9 collective-permute-start.8
  71.3 6.6 %shard_map.73 = f32[4,3,128,256]{3,2,1,0:T(8,128)} custom-call(s32[2]{0:T(128)} %pad_add_fusion.place, s32[120]{0:T(128)} %fusion.23.slots, bf16[12,2,5,128,128]{4,3,2,1,0:T(8,128)(2,1)} %bitcast.40, bf16[4,128,256]{2,1,0:T(8,128)(2,1)} %copy-done, bf16[4,128,256]{2,1,0:T(8,128)(2,1)} %copy-done.8, bf16[4,128,256]{2,1,0:T(8,128)(2,1)} %copy-done.9, ...), custom_call_target="tpu_custom_call" | custom-call | flops 503316480 | bytes 6291456 | tf_op jit(solution)/shard_map/pallas_call | solution.py:88
  77.9 1.7 fusion.27
  79.7 4.8 %collective-permute-start.11 = (bf16[2,3,128,128]{3,2,1,0:T(8,128)(2,1)S(1)}, bf16[2,3,128,128]{3,2,1,0:T(8,128)(2,1)S(1)}, u32[]{:S(2)}, u32[]{:S(2)}) collective-permute-start(bf16[2,3,128,128]{3,2,1,0:T(8,128)(2,1)S(1)} %get-tuple-element.20), channel_id=1, source_target_pairs={{0,18},{1,19},{2,20},{3,21},{4,22},{5,23},{6,12},{7,13},{8,14},{9,... | collective-permute-start | bytes 589832 | tf_op jit(solution)/shard_map/ppermute | solution.py:121
  84.5 2.1 collective-permute-start.9
  86.6 3.6 %collective-permute-done.11 = bf16[2,3,128,128]{3,2,1,0:T(8,128)(2,1)S(1)} collective-permute-done((bf16[2,3,128,128]{3,2,1,0:T(8,128)(2,1)S(1)}, bf16[2,3,128,128]{3,2,1,0:T(8,128)(2,1)S(1)}, u32[]{:S(2)}, u32[]{:S(2)}) %collective-permute-start.11) | collective-permute-done | bytes 196640 | tf_op jit(solution)/shard_map/ppermute | solution.py:121
  90.2 3.2 %collective-permute-done.9 = bf16[2,3,128,128]{3,2,1,0:T(8,128)(2,1)S(1)} collective-permute-done((bf16[2,3,128,128]{3,2,1,0:T(8,128)(2,1)S(1)}, bf16[2,3,128,128]{3,2,1,0:T(8,128)(2,1)S(1)}, u32[]{:S(2)}, u32[]{:S(2)}) %collective-permute-start.9) | collective-permute-done | bytes 196640 | tf_op jit(solution)/shard_map/ppermute | solution.py:120
  93.5 2.4 %collective-permute-start.10 = (bf16[3,128,128]{2,1,0:T(8,128)(2,1)S(1)}, bf16[3,128,128]{2,1,0:T(8,128)(2,1)S(1)}, u32[]{:S(2)}, u32[]{:S(2)}) collective-permute-start(bf16[3,128,128]{2,1,0:T(8,128)(2,1)S(1)} %get-tuple-element.15), channel_id=1, source_target_pairs={{0,18},{1,19},{2,20},{3,21},{4,22},{5,23},{6,12},{7,13},{8,14},{9,... | collective-permute-start | bytes 294920 | tf_op jit(solution)/shard_map/ppermute | solution.py:123
  95.9 2.2 collective-permute-start.12
  98.0 3.1 %collective-permute-done.10 = bf16[3,128,128]{2,1,0:T(8,128)(2,1)S(1)} collective-permute-done((bf16[3,128,128]{2,1,0:T(8,128)(2,1)S(1)}, bf16[3,128,128]{2,1,0:T(8,128)(2,1)S(1)}, u32[]{:S(2)}, u32[]{:S(2)}) %collective-permute-start.10) | collective-permute-done | bytes 98336 | tf_op jit(solution)/shard_map/ppermute | solution.py:123
  101.2 1.2 collective-permute-done.12
  102.4 0.7 pad_maximum_fusion
  103.1 11.2 %all-to-all-start.1 = ((bf16[3,128,256]{2,1,0:T(8,128)(2,1)}), bf16[3,128,256]{2,1,0:T(8,128)(2,1)S(1)}, u32[]{:S(2)}, u32[]{:S(2)}) async-start(bf16[3,128,256]{2,1,0:T(8,128)(2,1)} %pad_maximum_fusion), calls=%async_computation.1 | async-start | bytes 393216 | tf_op jit(solution)/shard_map/all_to_all | solution.py:159
  114.4 9.2 %all-to-all-done.1 = bf16[3,128,256]{2,1,0:T(8,128)(2,1)S(1)} async-done(((bf16[3,128,256]{2,1,0:T(8,128)(2,1)}), bf16[3,128,256]{2,1,0:T(8,128)(2,1)S(1)}, u32[]{:S(2)}, u32[]{:S(2)}) %all-to-all-start.1) | async-done | bytes 196640 | tf_op jit(solution)/shard_map/all_to_all | solution.py:159
  123.8 9.7 %all_to_all.21.refs_0_ = bf16[4,128,256]{2,1,0:T(8,128)(2,1)S(1)} all-to-all(bf16[4,128,256]{2,1,0:T(8,128)(2,1)S(1)} %broadcast_in_dim.35), channel_id=1, replica_groups={{0,24,48,72},{96,120,144,168},{192,216,240,264},{288,312,336,360},{384,..., dimensions={0} | all-to-all | bytes 524288 | tf_op jit(solution)/shard_map/all_to_all | solution.py:103
  133.5 2.9 %collective-permute-start.14 = (bf16[4,128,256]{2,1,0:T(8,128)(2,1)S(1)}, bf16[4,128,256]{2,1,0:T(8,128)(2,1)S(1)}, u32[]{:S(2)}, u32[]{:S(2)}) collective-permute-start(bf16[4,128,256]{2,1,0:T(8,128)(2,1)S(1)} %all_to_all.21.refs_0_), channel_id=1, source_target_pairs={{0,672},{24,696},{48,720},{72,744},{96,192},{120,216},{144,240},{1... | collective-permute-start | bytes 786440 | tf_op jit(solution)/shard_map/ppermute | solution.py:107
  136.4 1.9 collective-permute-start.13
  138.3 4.6 %collective-permute-done.14.refs_8_ = bf16[4,128,256]{2,1,0:T(8,128)(2,1)S(1)} collective-permute-done((bf16[4,128,256]{2,1,0:T(8,128)(2,1)S(1)}, bf16[4,128,256]{2,1,0:T(8,128)(2,1)S(1)}, u32[]{:S(2)}, u32[]{:S(2)}) %collective-permute-start.14) | collective-permute-done | bytes 262176 | tf_op jit(solution)/shard_map/ppermute | solution.py:107
  142.9 1.9 collective-permute-start.15
  144.8 1.3 collective-permute-done.13.refs_1_
  146.2 4.8 %collective-permute-start.16 = (bf16[4,128,256]{2,1,0:T(8,128)(2,1)S(1)}, bf16[4,128,256]{2,1,0:T(8,128)(2,1)S(1)}, u32[]{:S(2)}, u32[]{:S(2)}) collective-permute-start(bf16[4,128,256]{2,1,0:T(8,128)(2,1)S(1)} %collective-permute-done.13.refs_1_), channel_id=1, source_target_pairs={{0,672},{24,696},{48,720},{72,744},{96,192},{120,216},{144,240},{1... | collective-permute-start | bytes 786440 | tf_op jit(solution)/shard_map/ppermute | solution.py:107
  151.2 2.9 %collective-permute-start.18 = (bf16[4,128,256]{2,1,0:T(8,128)(2,1)S(1)}, bf16[4,128,256]{2,1,0:T(8,128)(2,1)S(1)}, u32[]{:S(2)}, u32[]{:S(2)}) collective-permute-start(bf16[4,128,256]{2,1,0:T(8,128)(2,1)S(1)} %collective-permute-done.15.refs_2_), channel_id=1, source_target_pairs={{0,672},{24,696},{48,720},{72,744},{96,192},{120,216},{144,240},{1... | collective-permute-start | bytes 786440 | tf_op jit(solution)/shard_map/ppermute | solution.py:107
  154.1 4.2 %collective-permute-done.16.refs_7_ = bf16[4,128,256]{2,1,0:T(8,128)(2,1)S(1)} collective-permute-done((bf16[4,128,256]{2,1,0:T(8,128)(2,1)S(1)}, bf16[4,128,256]{2,1,0:T(8,128)(2,1)S(1)}, u32[]{:S(2)}, u32[]{:S(2)}) %collective-permute-start.16) | collective-permute-done | bytes 262176 | tf_op jit(solution)/shard_map/ppermute | solution.py:107
  158.3 1.9 collective-permute-start.17
  160.2 1.0 collective-permute-done.18.refs_6_
  161.3 2.9 %collective-permute-start.19 = (bf16[2,128,256]{2,1,0:T(8,128)(2,1)S(1)}, bf16[2,128,256]{2,1,0:T(8,128)(2,1)S(1)}, u32[]{:S(2)}, u32[]{:S(2)}) collective-permute-start(bf16[2,128,256]{2,1,0:T(8,128)(2,1)S(1)} %slice.128), channel_id=1, source_target_pairs={{0,96},{24,120},{48,144},{72,168},{96,0},{120,24},{144,48},{168,72... | collective-permute-start | bytes 393224 | tf_op jit(solution)/shard_map/ppermute | solution.py:111
  164.2 3.2 %collective-permute-done.17.refs_3_ = bf16[4,128,256]{2,1,0:T(8,128)(2,1)S(1)} collective-permute-done((bf16[4,128,256]{2,1,0:T(8,128)(2,1)S(1)}, bf16[4,128,256]{2,1,0:T(8,128)(2,1)S(1)}, u32[]{:S(2)}, u32[]{:S(2)}) %collective-permute-start.17) | collective-permute-done | bytes 262176 | tf_op jit(solution)/shard_map/ppermute | solution.py:106
  167.4 2.6 %collective-permute-start.20 = (bf16[2,128,256]{2,1,0:T(8,128)(2,1)S(1)}, bf16[2,128,256]{2,1,0:T(8,128)(2,1)S(1)}, u32[]{:S(2)}, u32[]{:S(2)}) collective-permute-start(bf16[2,128,256]{2,1,0:T(8,128)(2,1)S(1)} %slice.129), channel_id=1, source_target_pairs={{0,672},{24,696},{48,720},{72,744},{96,192},{120,216},{144,240},{1... | collective-permute-start | bytes 393224 | tf_op jit(solution)/shard_map/ppermute | solution.py:112
  170.0 5.5 %collective-permute-done.20.refs_5_ = bf16[2,128,256]{2,1,0:T(8,128)(2,1)S(1)} collective-permute-done((bf16[2,128,256]{2,1,0:T(8,128)(2,1)S(1)}, bf16[2,128,256]{2,1,0:T(8,128)(2,1)S(1)}, u32[]{:S(2)}, u32[]{:S(2)}) %collective-permute-start.20) | collective-permute-done | bytes 131104 | tf_op jit(solution)/shard_map/ppermute | solution.py:112
  175.6 0.7 copy-done.18
  176.2 6.4 %shard_map.76 = bf16[4,3,128,256]{3,2,1,0:T(8,128)(2,1)} custom-call(s32[2]{0:T(128)} %pad_add_fusion.1.place, s32[120]{0:T(128)} %fusion.23.slots, bf16[12,2,5,128,128]{4,3,2,1,0:T(8,128)(2,1)} %bitcast.41, bf16[4,128,256]{2,1,0:T(8,128)(2,1)} %copy-done.1, bf16[4,128,256]{2,1,0:T(8,128)(2,1)} %copy-done.12, bf16[4,128,256]{2,1,0:T(8,128)(2,1)} %copy-done.13, ...), custom_call_target="tpu_custom_call" | custom-call | flops 503316480 | bytes 6291456 | tf_op jit(solution)/shard_map/pallas_call | solution.py:88
  182.7 1.9 collective-permute-start.21
  184.6 6.6 %shard_map.75 = f32[4,3,128,256]{3,2,1,0:T(8,128)} custom-call(s32[2]{0:T(128)} %pad_add_fusion.place, s32[120]{0:T(128)} %fusion.23.slots, bf16[12,2,5,128,128]{4,3,2,1,0:T(8,128)(2,1)} %bitcast.42, bf16[4,128,256]{2,1,0:T(8,128)(2,1)} %copy-done.1, bf16[4,128,256]{2,1,0:T(8,128)(2,1)} %copy-done.12, bf16[4,128,256]{2,1,0:T(8,128)(2,1)} %copy-done.13, ...), custom_call_target="tpu_custom_call" | custom-call | flops 503316480 | bytes 6291456 | tf_op jit(solution)/shard_map/pallas_call | solution.py:88
  191.2 1.7 fusion.26
  193.0 1.9 collective-permute-start.22
  195.0 4.7 %collective-permute-start.24 = (bf16[2,3,128,128]{3,2,1,0:T(8,128)(2,1)S(1)}, bf16[2,3,128,128]{3,2,1,0:T(8,128)(2,1)S(1)}, u32[]{:S(2)}, u32[]{:S(2)}) collective-permute-start(bf16[2,3,128,128]{3,2,1,0:T(8,128)(2,1)S(1)} %get-tuple-element.18), channel_id=1, source_target_pairs={{0,18},{1,19},{2,20},{3,21},{4,22},{5,23},{6,12},{7,13},{8,14},{9,... | collective-permute-start | bytes 589832 | tf_op jit(solution)/shard_map/ppermute | solution.py:121
  199.6 2.6 %collective-permute-done.22 = bf16[2,3,128,128]{3,2,1,0:T(8,128)(2,1)S(1)} collective-permute-done((bf16[2,3,128,128]{3,2,1,0:T(8,128)(2,1)S(1)}, bf16[2,3,128,128]{3,2,1,0:T(8,128)(2,1)S(1)}, u32[]{:S(2)}, u32[]{:S(2)}) %collective-permute-start.22) | collective-permute-done | bytes 196640 | tf_op jit(solution)/shard_map/ppermute | solution.py:120
  202.2 3.1 %collective-permute-done.24 = bf16[2,3,128,128]{3,2,1,0:T(8,128)(2,1)S(1)} collective-permute-done((bf16[2,3,128,128]{3,2,1,0:T(8,128)(2,1)S(1)}, bf16[2,3,128,128]{3,2,1,0:T(8,128)(2,1)S(1)}, u32[]{:S(2)}, u32[]{:S(2)}) %collective-permute-start.24) | collective-permute-done | bytes 196640 | tf_op jit(solution)/shard_map/ppermute | solution.py:121
  205.4 4.4 %collective-permute-start.23 = (bf16[3,128,128]{2,1,0:T(8,128)(2,1)S(1)}, bf16[3,128,128]{2,1,0:T(8,128)(2,1)S(1)}, u32[]{:S(2)}, u32[]{:S(2)}) collective-permute-start(bf16[3,128,128]{2,1,0:T(8,128)(2,1)S(1)} %get-tuple-element.11), channel_id=1, source_target_pairs={{0,18},{1,19},{2,20},{3,21},{4,22},{5,23},{6,12},{7,13},{8,14},{9,... | collective-permute-start | bytes 294920 | tf_op jit(solution)/shard_map/ppermute | solution.py:123
  209.8 1.9 collective-permute-start.25
  211.8 1.4 collective-permute-done.23
  213.1 3.2 %collective-permute-done.25 = bf16[3,128,128]{2,1,0:T(8,128)(2,1)S(1)} collective-permute-done((bf16[3,128,128]{2,1,0:T(8,128)(2,1)S(1)}, bf16[3,128,128]{2,1,0:T(8,128)(2,1)S(1)}, u32[]{:S(2)}, u32[]{:S(2)}) %collective-permute-start.25) | collective-permute-done | bytes 98336 | tf_op jit(solution)/shard_map/ppermute | solution.py:125
  216.5 13.7 %all_to_all.22 = bf16[3,128,256]{2,1,0:T(8,128)(2,1)S(1)} all-to-all(bf16[3,128,256]{2,1,0:T(8,128)(2,1)S(1)} %pad_maximum_fusion.1), channel_id=1, replica_groups={{0,2,4},{1,3,5},{6,8,10},{7,9,11},{12,14,16},{13,15,17},{18,20,22},{19,..., dimensions={0} | all-to-all | bytes 393216 | tf_op jit(solution)/shard_map/all_to_all | solution.py:159
  230.2 0.8 convert_select_fusion
  (69 shorter events, 3.7 us)
Async XLA Ops:
  17.6 44.0 %copy-start = (bf16[4,128,256]{2,1,0:T(8,128)(2,1)}, bf16[4,128,256]{2,1,0:T(8,128)(2,1)S(1)}, u32[]{:S(2)}) copy-start(bf16[4,128,256]{2,1,0:T(8,128)(2,1)S(1)} %all_to_all.20.refs_0_) | copy-start | bytes 786436
  17.6 9.5 %collective-permute-start.1 = (bf16[4,128,256]{2,1,0:T(8,128)(2,1)S(1)}, bf16[4,128,256]{2,1,0:T(8,128)(2,1)S(1)}, u32[]{:S(2)}, u32[]{:S(2)}) collective-permute-start(bf16[4,128,256]{2,1,0:T(8,128)(2,1)S(1)} %all_to_all.20.refs_0_), channel_id=1, source_target_pairs={{0,672},{24,696},{48,720},{72,744},{96,192},{120,216},{144,240},{1... | collective-permute-start | bytes 786440 | tf_op jit(solution)/shard_map/ppermute | solution.py:107
  22.3 10.9 %collective-permute-start = (bf16[4,128,256]{2,1,0:T(8,128)(2,1)S(1)}, bf16[4,128,256]{2,1,0:T(8,128)(2,1)S(1)}, u32[]{:S(2)}, u32[]{:S(2)}) collective-permute-start(bf16[4,128,256]{2,1,0:T(8,128)(2,1)S(1)} %all_to_all.20.refs_0_), channel_id=1, source_target_pairs={{0,96},{24,120},{48,144},{72,168},{96,0},{120,24},{144,48},{168,72... | collective-permute-start | bytes 786440 | tf_op jit(solution)/shard_map/ppermute | solution.py:106
  27.1 34.5 %copy-start.7 = (bf16[4,128,256]{2,1,0:T(8,128)(2,1)}, bf16[4,128,256]{2,1,0:T(8,128)(2,1)S(1)}, u32[]{:S(2)}) copy-start(bf16[4,128,256]{2,1,0:T(8,128)(2,1)S(1)} %collective-permute-done.1.refs_8_) | copy-start | bytes 786436
  27.1 9.1 %collective-permute-start.2 = (bf16[4,128,256]{2,1,0:T(8,128)(2,1)S(1)}, bf16[4,128,256]{2,1,0:T(8,128)(2,1)S(1)}, u32[]{:S(2)}, u32[]{:S(2)}) collective-permute-start(bf16[4,128,256]{2,1,0:T(8,128)(2,1)S(1)} %collective-permute-done.1.refs_8_), channel_id=1, source_target_pairs={{0,96},{24,120},{48,144},{72,168},{96,0},{120,24},{144,48},{168,72... | collective-permute-start | bytes 786440 | tf_op jit(solution)/shard_map/ppermute | solution.py:106
  33.2 28.4 %copy-start.8 = (bf16[4,128,256]{2,1,0:T(8,128)(2,1)}, bf16[4,128,256]{2,1,0:T(8,128)(2,1)S(1)}, u32[]{:S(2)}) copy-start(bf16[4,128,256]{2,1,0:T(8,128)(2,1)S(1)} %collective-permute-done.refs_1_) | copy-start | bytes 786436
  33.2 11.8 %collective-permute-start.3 = (bf16[4,128,256]{2,1,0:T(8,128)(2,1)S(1)}, bf16[4,128,256]{2,1,0:T(8,128)(2,1)S(1)}, u32[]{:S(2)}, u32[]{:S(2)}) collective-permute-start(bf16[4,128,256]{2,1,0:T(8,128)(2,1)S(1)} %collective-permute-done.refs_1_), channel_id=1, source_target_pairs={{0,672},{24,696},{48,720},{72,744},{96,192},{120,216},{144,240},{1... | collective-permute-start | bytes 786440 | tf_op jit(solution)/shard_map/ppermute | solution.py:107
  36.2 25.4 %copy-start.9 = (bf16[4,128,256]{2,1,0:T(8,128)(2,1)}, bf16[4,128,256]{2,1,0:T(8,128)(2,1)S(1)}, u32[]{:S(2)}) copy-start(bf16[4,128,256]{2,1,0:T(8,128)(2,1)S(1)} %collective-permute-done.2.refs_2_) | copy-start | bytes 786436
  36.2 12.5 %collective-permute-start.5 = (bf16[4,128,256]{2,1,0:T(8,128)(2,1)S(1)}, bf16[4,128,256]{2,1,0:T(8,128)(2,1)S(1)}, u32[]{:S(2)}, u32[]{:S(2)}) collective-permute-start(bf16[4,128,256]{2,1,0:T(8,128)(2,1)S(1)} %collective-permute-done.2.refs_2_), channel_id=1, source_target_pairs={{0,672},{24,696},{48,720},{72,744},{96,192},{120,216},{144,240},{1... | collective-permute-start | bytes 786440 | tf_op jit(solution)/shard_map/ppermute | solution.py:107
  45.0 16.6 %copy-start.10 = (bf16[4,128,256]{2,1,0:T(8,128)(2,1)}, bf16[4,128,256]{2,1,0:T(8,128)(2,1)S(1)}, u32[]{:S(2)}) copy-start(bf16[4,128,256]{2,1,0:T(8,128)(2,1)S(1)} %collective-permute-done.3.refs_7_) | copy-start | bytes 786436
  45.0 8.5 %collective-permute-start.4 = (bf16[4,128,256]{2,1,0:T(8,128)(2,1)S(1)}, bf16[4,128,256]{2,1,0:T(8,128)(2,1)S(1)}, u32[]{:S(2)}, u32[]{:S(2)}) collective-permute-start(bf16[4,128,256]{2,1,0:T(8,128)(2,1)S(1)} %collective-permute-done.3.refs_7_), channel_id=1, source_target_pairs={{0,96},{24,120},{48,144},{72,168},{96,0},{120,24},{144,48},{168,72... | collective-permute-start | bytes 786440 | tf_op jit(solution)/shard_map/ppermute | solution.py:106
  48.7 12.9 %copy-start.2 = (bf16[4,128,256]{2,1,0:T(8,128)(2,1)}, bf16[4,128,256]{2,1,0:T(8,128)(2,1)S(1)}, u32[]{:S(2)}) copy-start(bf16[4,128,256]{2,1,0:T(8,128)(2,1)S(1)} %collective-permute-done.5.refs_6_) | copy-start | bytes 786436
  48.7 8.4 %collective-permute-start.6 = (bf16[2,128,256]{2,1,0:T(8,128)(2,1)S(1)}, bf16[2,128,256]{2,1,0:T(8,128)(2,1)S(1)}, u32[]{:S(2)}, u32[]{:S(2)}) collective-permute-start(bf16[2,128,256]{2,1,0:T(8,128)(2,1)S(1)} %slice.116), channel_id=1, source_target_pairs={{0,96},{24,120},{48,144},{72,168},{96,0},{120,24},{144,48},{168,72... | collective-permute-start | bytes 393224 | tf_op jit(solution)/shard_map/ppermute | solution.py:111
  53.5 8.1 %copy-start.3 = (bf16[4,128,256]{2,1,0:T(8,128)(2,1)}, bf16[4,128,256]{2,1,0:T(8,128)(2,1)S(1)}, u32[]{:S(2)}) copy-start(bf16[4,128,256]{2,1,0:T(8,128)(2,1)S(1)} %collective-permute-done.4.refs_3_) | copy-start | bytes 786436
  53.5 8.1 %collective-permute-start.7 = (bf16[2,128,256]{2,1,0:T(8,128)(2,1)S(1)}, bf16[2,128,256]{2,1,0:T(8,128)(2,1)S(1)}, u32[]{:S(2)}, u32[]{:S(2)}) collective-permute-start(bf16[2,128,256]{2,1,0:T(8,128)(2,1)S(1)} %slice.117), channel_id=1, source_target_pairs={{0,672},{24,696},{48,720},{72,744},{96,192},{120,216},{144,240},{1... | collective-permute-start | bytes 393224 | tf_op jit(solution)/shard_map/ppermute | solution.py:112
  57.1 4.5 %copy-start.15 = (bf16[2,128,256]{2,1,0:T(8,128)(2,1)}, bf16[2,128,256]{2,1,0:T(8,128)(2,1)S(1)}, u32[]{:S(2)}) copy-start(bf16[2,128,256]{2,1,0:T(8,128)(2,1)S(1)} %collective-permute-done.6.refs_4_) | copy-start | bytes 393220
  61.6 0.7 copy-start.16
  68.7 9.2 %collective-permute-start.8 = (bf16[4,3,128,256]{3,2,1,0:T(8,128)(2,1)}, bf16[4,3,128,256]{3,2,1,0:T(8,128)(2,1)S(1)}, u32[]{:S(2)}, u32[]{:S(2)}) collective-permute-start(bf16[4,3,128,256]{3,2,1,0:T(8,128)(2,1)} %shard_map.74), channel_id=1, source_target_pairs={{0,1},{1,0},{2,3},{3,2},{4,5},{5,4},{6,7},{7,6},{8,9},{9,8},{10,11... | collective-permute-start | bytes 2359304 | tf_op jit(solution)/shard_map/ppermute | solution.py:155
  79.5 34.8 %copy-start.20 = (s32[128]{0:T(128)S(1)}, s32[128]{0:T(128)}, u32[]{:S(2)}) copy-start(s32[128]{0:T(128)} %param.9) | copy-start | bytes 1540
  79.7 44.0 %copy-start.6 = (f32[128,256]{1,0:T(8,128)S(1)}, f32[128,256]{1,0:T(8,128)}, u32[]{:S(2)}) copy-start(f32[128,256]{1,0:T(8,128)} %param.7) | copy-start | bytes 393220
  79.7 44.0 %copy-start.19 = (s32[128]{0:T(128)S(1)}, s32[128]{0:T(128)}, u32[]{:S(2)}) copy-start(s32[128]{0:T(128)} %param.10) | copy-start | bytes 1540
  79.7 10.5 %collective-permute-start.11 = (bf16[2,3,128,128]{3,2,1,0:T(8,128)(2,1)S(1)}, bf16[2,3,128,128]{3,2,1,0:T(8,128)(2,1)S(1)}, u32[]{:S(2)}, u32[]{:S(2)}) collective-permute-start(bf16[2,3,128,128]{3,2,1,0:T(8,128)(2,1)S(1)} %get-tuple-element.20), channel_id=1, source_target_pairs={{0,18},{1,19},{2,20},{3,21},{4,22},{5,23},{6,12},{7,13},{8,14},{9,... | collective-permute-start | bytes 589832 | tf_op jit(solution)/shard_map/ppermute | solution.py:121
  84.5 8.9 %collective-permute-start.9 = (bf16[2,3,128,128]{3,2,1,0:T(8,128)(2,1)S(1)}, bf16[2,3,128,128]{3,2,1,0:T(8,128)(2,1)S(1)}, u32[]{:S(2)}, u32[]{:S(2)}) collective-permute-start(bf16[2,3,128,128]{3,2,1,0:T(8,128)(2,1)S(1)} %get-tuple-element.19), channel_id=1, source_target_pairs={{0,6},{1,7},{2,8},{3,9},{4,10},{5,11},{6,0},{7,1},{8,2},{9,3},{10,... | collective-permute-start | bytes 589832 | tf_op jit(solution)/shard_map/ppermute | solution.py:120
  93.5 7.7 %collective-permute-start.10 = (bf16[3,128,128]{2,1,0:T(8,128)(2,1)S(1)}, bf16[3,128,128]{2,1,0:T(8,128)(2,1)S(1)}, u32[]{:S(2)}, u32[]{:S(2)}) collective-permute-start(bf16[3,128,128]{2,1,0:T(8,128)(2,1)S(1)} %get-tuple-element.15), channel_id=1, source_target_pairs={{0,18},{1,19},{2,20},{3,21},{4,22},{5,23},{6,12},{7,13},{8,14},{9,... | collective-permute-start | bytes 294920 | tf_op jit(solution)/shard_map/ppermute | solution.py:123
  95.9 6.5 %collective-permute-start.12 = (bf16[3,128,128]{2,1,0:T(8,128)(2,1)S(1)}, bf16[3,128,128]{2,1,0:T(8,128)(2,1)S(1)}, u32[]{:S(2)}, u32[]{:S(2)}) collective-permute-start(bf16[3,128,128]{2,1,0:T(8,128)(2,1)S(1)} %get-tuple-element.16), channel_id=1, source_target_pairs={{0,6},{1,7},{2,8},{3,9},{4,10},{5,11},{6,0},{7,1},{8,2},{9,3},{10,... | collective-permute-start | bytes 294920 | tf_op jit(solution)/shard_map/ppermute | solution.py:125
  103.1 20.4 %all-to-all-start.1 = ((bf16[3,128,256]{2,1,0:T(8,128)(2,1)}), bf16[3,128,256]{2,1,0:T(8,128)(2,1)S(1)}, u32[]{:S(2)}, u32[]{:S(2)}) async-start(bf16[3,128,256]{2,1,0:T(8,128)(2,1)} %pad_maximum_fusion), calls=%async_computation.1 | async-start | bytes 393216 | tf_op jit(solution)/shard_map/all_to_all | solution.py:159
  133.4 42.1 %copy-start.1 = (bf16[4,128,256]{2,1,0:T(8,128)(2,1)}, bf16[4,128,256]{2,1,0:T(8,128)(2,1)S(1)}, u32[]{:S(2)}) copy-start(bf16[4,128,256]{2,1,0:T(8,128)(2,1)S(1)} %all_to_all.21.refs_0_) | copy-start | bytes 786436
  133.5 9.5 %collective-permute-start.14 = (bf16[4,128,256]{2,1,0:T(8,128)(2,1)S(1)}, bf16[4,128,256]{2,1,0:T(8,128)(2,1)S(1)}, u32[]{:S(2)}, u32[]{:S(2)}) collective-permute-start(bf16[4,128,256]{2,1,0:T(8,128)(2,1)S(1)} %all_to_all.21.refs_0_), channel_id=1, source_target_pairs={{0,672},{24,696},{48,720},{72,744},{96,192},{120,216},{144,240},{1... | collective-permute-start | bytes 786440 | tf_op jit(solution)/shard_map/ppermute | solution.py:107
  136.4 9.8 %collective-permute-start.13 = (bf16[4,128,256]{2,1,0:T(8,128)(2,1)S(1)}, bf16[4,128,256]{2,1,0:T(8,128)(2,1)S(1)}, u32[]{:S(2)}, u32[]{:S(2)}) collective-permute-start(bf16[4,128,256]{2,1,0:T(8,128)(2,1)S(1)} %all_to_all.21.refs_0_), channel_id=1, source_target_pairs={{0,96},{24,120},{48,144},{72,168},{96,0},{120,24},{144,48},{168,72... | collective-permute-start | bytes 786440 | tf_op jit(solution)/shard_map/ppermute | solution.py:106
  142.9 32.6 %copy-start.11 = (bf16[4,128,256]{2,1,0:T(8,128)(2,1)}, bf16[4,128,256]{2,1,0:T(8,128)(2,1)S(1)}, u32[]{:S(2)}) copy-start(bf16[4,128,256]{2,1,0:T(8,128)(2,1)S(1)} %collective-permute-done.14.refs_8_) | copy-start | bytes 786436
  142.9 8.3 %collective-permute-start.15 = (bf16[4,128,256]{2,1,0:T(8,128)(2,1)S(1)}, bf16[4,128,256]{2,1,0:T(8,128)(2,1)S(1)}, u32[]{:S(2)}, u32[]{:S(2)}) collective-permute-start(bf16[4,128,256]{2,1,0:T(8,128)(2,1)S(1)} %collective-permute-done.14.refs_8_), channel_id=1, source_target_pairs={{0,96},{24,120},{48,144},{72,168},{96,0},{120,24},{144,48},{168,72... | collective-permute-start | bytes 786440 | tf_op jit(solution)/shard_map/ppermute | solution.py:106
  146.2 29.4 %copy-start.12 = (bf16[4,128,256]{2,1,0:T(8,128)(2,1)}, bf16[4,128,256]{2,1,0:T(8,128)(2,1)S(1)}, u32[]{:S(2)}) copy-start(bf16[4,128,256]{2,1,0:T(8,128)(2,1)S(1)} %collective-permute-done.13.refs_1_) | copy-start | bytes 786436
  146.2 12.1 %collective-permute-start.16 = (bf16[4,128,256]{2,1,0:T(8,128)(2,1)S(1)}, bf16[4,128,256]{2,1,0:T(8,128)(2,1)S(1)}, u32[]{:S(2)}, u32[]{:S(2)}) collective-permute-start(bf16[4,128,256]{2,1,0:T(8,128)(2,1)S(1)} %collective-permute-done.13.refs_1_), channel_id=1, source_target_pairs={{0,672},{24,696},{48,720},{72,744},{96,192},{120,216},{144,240},{1... | collective-permute-start | bytes 786440 | tf_op jit(solution)/shard_map/ppermute | solution.py:107
  151.2 24.3 %copy-start.13 = (bf16[4,128,256]{2,1,0:T(8,128)(2,1)}, bf16[4,128,256]{2,1,0:T(8,128)(2,1)S(1)}, u32[]{:S(2)}) copy-start(bf16[4,128,256]{2,1,0:T(8,128)(2,1)S(1)} %collective-permute-done.15.refs_2_) | copy-start | bytes 786436
  151.2 10.1 %collective-permute-start.18 = (bf16[4,128,256]{2,1,0:T(8,128)(2,1)S(1)}, bf16[4,128,256]{2,1,0:T(8,128)(2,1)S(1)}, u32[]{:S(2)}, u32[]{:S(2)}) collective-permute-start(bf16[4,128,256]{2,1,0:T(8,128)(2,1)S(1)} %collective-permute-done.15.refs_2_), channel_id=1, source_target_pairs={{0,672},{24,696},{48,720},{72,744},{96,192},{120,216},{144,240},{1... | collective-permute-start | bytes 786440 | tf_op jit(solution)/shard_map/ppermute | solution.py:107
  158.3 17.2 %copy-start.14 = (bf16[4,128,256]{2,1,0:T(8,128)(2,1)}, bf16[4,128,256]{2,1,0:T(8,128)(2,1)S(1)}, u32[]{:S(2)}) copy-start(bf16[4,128,256]{2,1,0:T(8,128)(2,1)S(1)} %collective-permute-done.16.refs_7_) | copy-start | bytes 786436
  158.3 9.1 %collective-permute-start.17 = (bf16[4,128,256]{2,1,0:T(8,128)(2,1)S(1)}, bf16[4,128,256]{2,1,0:T(8,128)(2,1)S(1)}, u32[]{:S(2)}, u32[]{:S(2)}) collective-permute-start(bf16[4,128,256]{2,1,0:T(8,128)(2,1)S(1)} %collective-permute-done.16.refs_7_), channel_id=1, source_target_pairs={{0,96},{24,120},{48,144},{72,168},{96,0},{120,24},{144,48},{168,72... | collective-permute-start | bytes 786440 | tf_op jit(solution)/shard_map/ppermute | solution.py:106
  161.2 14.3 %copy-start.4 = (bf16[4,128,256]{2,1,0:T(8,128)(2,1)}, bf16[4,128,256]{2,1,0:T(8,128)(2,1)S(1)}, u32[]{:S(2)}) copy-start(bf16[4,128,256]{2,1,0:T(8,128)(2,1)S(1)} %collective-permute-done.18.refs_6_) | copy-start | bytes 786436
  161.3 8.8 %collective-permute-start.19 = (bf16[2,128,256]{2,1,0:T(8,128)(2,1)S(1)}, bf16[2,128,256]{2,1,0:T(8,128)(2,1)S(1)}, u32[]{:S(2)}, u32[]{:S(2)}) collective-permute-start(bf16[2,128,256]{2,1,0:T(8,128)(2,1)S(1)} %slice.128), channel_id=1, source_target_pairs={{0,96},{24,120},{48,144},{72,168},{96,0},{120,24},{144,48},{168,72... | collective-permute-start | bytes 393224 | tf_op jit(solution)/shard_map/ppermute | solution.py:111
  167.4 8.1 %copy-start.5 = (bf16[4,128,256]{2,1,0:T(8,128)(2,1)}, bf16[4,128,256]{2,1,0:T(8,128)(2,1)S(1)}, u32[]{:S(2)}) copy-start(bf16[4,128,256]{2,1,0:T(8,128)(2,1)S(1)} %collective-permute-done.17.refs_3_) | copy-start | bytes 786436
  167.4 8.1 %collective-permute-start.20 = (bf16[2,128,256]{2,1,0:T(8,128)(2,1)S(1)}, bf16[2,128,256]{2,1,0:T(8,128)(2,1)S(1)}, u32[]{:S(2)}, u32[]{:S(2)}) collective-permute-start(bf16[2,128,256]{2,1,0:T(8,128)(2,1)S(1)} %slice.129), channel_id=1, source_target_pairs={{0,672},{24,696},{48,720},{72,744},{96,192},{120,216},{144,240},{1... | collective-permute-start | bytes 393224 | tf_op jit(solution)/shard_map/ppermute | solution.py:112
  170.0 5.5 %copy-start.17 = (bf16[2,128,256]{2,1,0:T(8,128)(2,1)}, bf16[2,128,256]{2,1,0:T(8,128)(2,1)S(1)}, u32[]{:S(2)}) copy-start(bf16[2,128,256]{2,1,0:T(8,128)(2,1)S(1)} %collective-permute-done.19.refs_4_) | copy-start | bytes 393220
  175.6 0.7 copy-start.18
  182.7 8.6 %collective-permute-start.21 = (bf16[4,3,128,256]{3,2,1,0:T(8,128)(2,1)}, bf16[4,3,128,256]{3,2,1,0:T(8,128)(2,1)S(1)}, u32[]{:S(2)}, u32[]{:S(2)}) collective-permute-start(bf16[4,3,128,256]{3,2,1,0:T(8,128)(2,1)} %shard_map.76), channel_id=1, source_target_pairs={{0,1},{1,0},{2,3},{3,2},{4,5},{5,4},{6,7},{7,6},{8,9},{9,8},{10,11... | collective-permute-start | bytes 2359304 | tf_op jit(solution)/shard_map/ppermute | solution.py:155
  193.0 9.2 %collective-permute-start.22 = (bf16[2,3,128,128]{3,2,1,0:T(8,128)(2,1)S(1)}, bf16[2,3,128,128]{3,2,1,0:T(8,128)(2,1)S(1)}, u32[]{:S(2)}, u32[]{:S(2)}) collective-permute-start(bf16[2,3,128,128]{3,2,1,0:T(8,128)(2,1)S(1)} %get-tuple-element.17), channel_id=1, source_target_pairs={{0,6},{1,7},{2,8},{3,9},{4,10},{5,11},{6,0},{7,1},{8,2},{9,3},{10,... | collective-permute-start | bytes 589832 | tf_op jit(solution)/shard_map/ppermute | solution.py:120
  195.0 10.4 %collective-permute-start.24 = (bf16[2,3,128,128]{3,2,1,0:T(8,128)(2,1)S(1)}, bf16[2,3,128,128]{3,2,1,0:T(8,128)(2,1)S(1)}, u32[]{:S(2)}, u32[]{:S(2)}) collective-permute-start(bf16[2,3,128,128]{3,2,1,0:T(8,128)(2,1)S(1)} %get-tuple-element.18), channel_id=1, source_target_pairs={{0,18},{1,19},{2,20},{3,21},{4,22},{5,23},{6,12},{7,13},{8,14},{9,... | collective-permute-start | bytes 589832 | tf_op jit(solution)/shard_map/ppermute | solution.py:121
  205.4 7.7 %collective-permute-start.23 = (bf16[3,128,128]{2,1,0:T(8,128)(2,1)S(1)}, bf16[3,128,128]{2,1,0:T(8,128)(2,1)S(1)}, u32[]{:S(2)}, u32[]{:S(2)}) collective-permute-start(bf16[3,128,128]{2,1,0:T(8,128)(2,1)S(1)} %get-tuple-element.11), channel_id=1, source_target_pairs={{0,18},{1,19},{2,20},{3,21},{4,22},{5,23},{6,12},{7,13},{8,14},{9,... | collective-permute-start | bytes 294920 | tf_op jit(solution)/shard_map/ppermute | solution.py:123
  209.8 6.5 %collective-permute-start.25 = (bf16[3,128,128]{2,1,0:T(8,128)(2,1)S(1)}, bf16[3,128,128]{2,1,0:T(8,128)(2,1)S(1)}, u32[]{:S(2)}, u32[]{:S(2)}) collective-permute-start(bf16[3,128,128]{2,1,0:T(8,128)(2,1)S(1)} %get-tuple-element.12), channel_id=1, source_target_pairs={{0,6},{1,7},{2,8},{3,9},{4,10},{5,11},{6,0},{7,1},{8,2},{9,3},{10,... | collective-permute-start | bytes 294920 | tf_op jit(solution)/shard_map/ppermute | solution.py:125

commit v3 on v1

--- a/solution.py
+++ b/solution.py
@@ -22,13 +22,18 @@
 SWAP = [(d, d ^ 1) for d in range(X * ZH * CORES)]
 
 
-def y_shift(step):
-    return [
-        (y * ZL + z, (y + step) % Y * ZL + z) for y in range(Y) for z in range(ZL)
-    ]
+def along_y(step):
+    rest = X * ZH * CORES
+    pairs = []
+    for y in range(Y):
+        for z in range(ZL):
+            for d in range(rest):
+                there = (y + (step if d % CORES == 0 else -step)) % Y
+                pairs.append(((y * ZL + z) * rest + d, (there * ZL + z) * rest + d))
+    return pairs
 
 
-UP, DOWN = y_shift(1), y_shift(-1)
+ALONG, AGAINST = along_y(1), along_y(-1)
 PIECE_AT = (0, 4, 8, 12, 16, 18, 20, 24, 28)
 PIECE_LEN = (4, 4, 4, 4, 2, 2, 4, 4, 4)
 LIVE = Y * ZL
@@ -47,7 +52,6 @@
         ]
         for copy in copies:
             copy.start()
-        blocks[LIVE] = jnp.zeros(blocks.shape[1:], blocks.dtype)
         for copy in copies:
             copy.wait()
 
@@ -78,7 +82,7 @@
         + [pl.BlockSpec(memory_space=pl.ANY)] * len(pieces),
         out_specs=pl.BlockSpec((STEP, size, classes), lambda i, parity, slots: (i, 0, 0)),
         scratch_shapes=[
-            pltpu.VMEM((LIVE + 1, size, classes), jnp.bfloat16),
+            pltpu.VMEM((LIVE, size, classes), jnp.bfloat16),
             pltpu.SemaphoreType.DMA((len(pieces),)),
         ],
     )
@@ -98,27 +102,29 @@
 def gather_blocks(outgoing):
     spread = jnp.broadcast_to(outgoing[None], (ZL,) + outgoing.shape)
     own = lax.all_to_all(spread, "src", 0, 0, axis_index_groups=Z_GROUPS)
-    up, down = [own], [own]
+    first, second = [own], [own]
     for _ in range(3):
-        up.append(lax.ppermute(up[-1], "src", UP))
-        down.append(lax.ppermute(down[-1], "src", DOWN))
-    far_up = lax.ppermute(up[3][:2], "src", UP)
-    far_down = lax.ppermute(down[3][2:], "src", DOWN)
-    return [own, down[1], down[2], down[3], far_up, far_down, up[3], up[2], up[1]]
+        first.append(lax.ppermute(first[-1], ("src", "dst"), ALONG))
+        second.append(lax.ppermute(second[-1], ("src", "dst"), AGAINST))
+    half = ZL // 2
+    far_first = lax.ppermute(first[3][:half], ("src", "dst"), ALONG)
+    far_second = lax.ppermute(second[3][half:], ("src", "dst"), AGAINST)
+    return [own, first[1], first[2], first[3], far_first, far_second, second[3], second[2], second[1]]
 
 
 def per_device(prior, degrees, seed_mask, seed_labels, adjacency, block_cols, slot_counts):
     classes = prior.shape[1]
     depth, size = adjacency.shape[3], adjacency.shape[4]
-    weights = adjacency.reshape(PAIRS, CORES, depth, size, size)
-    core = lax.axis_index("dst") % CORES
-    mine = core.astype(jnp.int32).reshape(1)
+    active = jnp.arange(depth, dtype=jnp.int32)[None, :] < slot_counts[0, 0][:, None]
+    weights = jnp.where(active[:, :, None, None], adjacency[0, 0], jnp.zeros((), adjacency.dtype))
+    weights = weights.reshape(PAIRS, CORES, depth, size, size)
+    core = lax.axis_index("dst").astype(jnp.int32) % CORES
+    mine = core.reshape(1)
     other = 1 - mine
-    y = lax.axis_index("src") // ZL
+    y = lax.axis_index("src").astype(jnp.int32) // ZL
     columns = block_cols[0, 0]
-    relative = (columns // ZL - y) % Y * ZL + columns % ZL
-    active = jnp.arange(depth, dtype=jnp.int32)[None, :] < slot_counts[0, 0][:, None]
-    slots = jnp.where(active, relative, LIVE).astype(jnp.int32).reshape(-1)
+    away = (columns // ZL - y) * (2 * core - 1)
+    slots = ((away + Y) % Y * ZL + columns % ZL).reshape(-1)
     inverse_root = lax.rsqrt(degrees.astype(jnp.float32))[:, None]
     onehot = (seed_labels[:, None] == jnp.arange(classes, dtype=jnp.int32)[None, :]).astype(
         jnp.float32

time: 200 us -> 210 us (1.050)
  waiting for transfers between devices: 33.9 us -> 40.7 us
  other arithmetic: 4.85 us -> 7.94 us
    ppermute x16, waiting for transfers between devices: 24.2 us -> 29.6 us  [the longest x6 14.6 us: gather_blocks(): first.append(lax.ppermute(first[-1], ('src', 'dst'), ALONG))]
    select_n x1, other arithmetic: 0.02 us -> 2.45 us  [per_device(): jnp.where(active[:, :, None, None], adjacency[0, 0], jnp.zeros((), adjace...]
    unnamed x15 -> x14, local copies, waits for them, and re-layouts: 5.02 us -> 3.44 us
  transfers between devices with their start and end apart: 19 -> 19, of which waited for: 12 -> 11; matrix products, arithmetic and copies ran while one was open for 1% -> 3% of each run, Pallas kernels for 2% -> 2%
where the time goes in v3:
time: 210 us; the launch traced here: 209 us
  blocking collectives  76.4 us (36%)
  starting transfers between devices  69.9 us (33%)
  waiting for transfers between devices  40.7 us (19%)
  Pallas kernels  9.82 us (5%)
  other arithmetic  7.94 us (4%)
  local copies, waits for them, and re-layouts  3.7 us (2%)
    all_to_all x2, blocking collectives, per_device(): rows = lax.all_to_all(chip, 'dst', 0, 0, axis_index_groups=X_GROUPS)  32.8 us
    all_to_all x2, blocking collectives, gather_blocks(): own = lax.all_to_all(spread, 'src', 0, 0, axis_index_groups=Z_GROUPS)  28.7 us
    ppermute x6, starting transfers between devices, gather_blocks(): first.append(lax.ppermute(first[-1], ('src', 'dst'), ALONG))  25.6 us
    all_to_all x1, blocking collectives, per_device(): parts = lax.all_to_all(rows, 'dst', 0, 0, axis_index_groups=H_GROUPS)  14.9 us
    ppermute x6, starting transfers between devices, gather_blocks(): second.append(lax.ppermute(second[-1], ('src', 'dst'), AGAINST))  14.6 us
    ppermute x6, waiting for transfers between devices, gather_blocks(): first.append(lax.ppermute(first[-1], ('src', 'dst'), ALONG))  14.6 us
    all_to_all x1, starting transfers between devices, per_device(): parts = lax.all_to_all(rows, 'dst', 0, 0, axis_index_groups=H_GROUPS)  11.2 us
    ppermute x2, waiting for transfers between devices, gather_blocks(): far_second = lax.ppermute(second[3][half:], ('src', 'dst'), AGAINST)  11.2 us
  transfers between devices with their start and end apart: 19, of which 11 were waited for; matrix products, arithmetic and copies ran while one was open for 3% of the time, Pallas kernels for 2%

profile of v3, /device:TPU:24, one launch (start us, length us, event | category | flops | bytes accessed | tf_op | source)
XLA Modules:
  0.0 208.9 jit_solution(13298525322846212278)
XLA Ops:
  0.0 0.7 broadcast_multiply_fusion
  0.7 1.0 multiply_convert_fusion
  1.7 15.9 %all_to_all.30.refs_0_ = bf16[4,128,256]{2,1,0:T(8,128)(2,1)S(1)} all-to-all(bf16[4,128,256]{2,1,0:T(8,128)(2,1)S(1)} %broadcast_in_dim.44), channel_id=1, replica_groups={{0,24,48,72},{96,120,144,168},{192,216,240,264},{288,312,336,360},{384,..., dimensions={0} | all-to-all | bytes 524288 | tf_op jit(solution)/shard_map/all_to_all | solution.py:104
  17.6 4.7 %collective-permute-start = (bf16[4,128,256]{2,1,0:T(8,128)(2,1)S(1)}, bf16[4,128,256]{2,1,0:T(8,128)(2,1)S(1)}, u32[]{:S(2)}, u32[]{:S(2)}) collective-permute-start(bf16[4,128,256]{2,1,0:T(8,128)(2,1)S(1)} %all_to_all.30.refs_0_), channel_id=1, source_target_pairs={{0,96},{1,673},{2,98},{3,675},{4,100},{5,677},{6,102},{7,679},{8,1... | collective-permute-start | bytes 786440 | tf_op jit(solution)/shard_map/ppermute | solution.py:107
  22.3 1.9 collective-permute-start.4
  24.2 3.4 %collective-permute-done.refs_1_ = bf16[4,128,256]{2,1,0:T(8,128)(2,1)S(1)} collective-permute-done((bf16[4,128,256]{2,1,0:T(8,128)(2,1)S(1)}, bf16[4,128,256]{2,1,0:T(8,128)(2,1)S(1)}, u32[]{:S(2)}, u32[]{:S(2)}) %collective-permute-start) | collective-permute-done | bytes 262176 | tf_op jit(solution)/shard_map/ppermute | solution.py:107
  27.7 5.6 %collective-permute-start.1 = (bf16[4,128,256]{2,1,0:T(8,128)(2,1)S(1)}, bf16[4,128,256]{2,1,0:T(8,128)(2,1)S(1)}, u32[]{:S(2)}, u32[]{:S(2)}) collective-permute-start(bf16[4,128,256]{2,1,0:T(8,128)(2,1)S(1)} %collective-permute-done.refs_1_), channel_id=1, source_target_pairs={{0,96},{1,673},{2,98},{3,675},{4,100},{5,677},{6,102},{7,679},{8,1... | collective-permute-start | bytes 786440 | tf_op jit(solution)/shard_map/ppermute | solution.py:107
  33.3 1.1 collective-permute-done.4.refs_8_
  34.4 1.9 collective-permute-start.5
  36.3 0.8 copy.10
  37.1 0.1 squeeze.6
  37.2 0.5 broadcast.78
  37.7 1.3 reduce.5
  39.0 0.1 lt.39
  39.1 0.1 iota_compare_fusion.1
  39.2 0.0 collective-permute-done.1.refs_2_
  39.2 5.1 %collective-permute-start.2 = (bf16[4,128,256]{2,1,0:T(8,128)(2,1)S(1)}, bf16[4,128,256]{2,1,0:T(8,128)(2,1)S(1)}, u32[]{:S(2)}, u32[]{:S(2)}) collective-permute-start(bf16[4,128,256]{2,1,0:T(8,128)(2,1)S(1)} %collective-permute-done.1.refs_2_), channel_id=1, source_target_pairs={{0,96},{1,673},{2,98},{3,675},{4,100},{5,677},{6,102},{7,679},{8,1... | collective-permute-start | bytes 786440 | tf_op jit(solution)/shard_map/ppermute | solution.py:107
  44.4 1.6 collective-permute-done.5.refs_7_
  46.0 1.9 collective-permute-start.6
  47.9 2.5 %broadcast_select_fusion.weights = bf16[12,2,5,128,128]{4,3,2,1,0:T(8,128)(2,1)S(1)} fusion(bf16[12,2,5,128,128]{4,3,2,1,0:T(8,128)(2,1)} %bitcast.6, pred[12,2,5]{2,1,0:T(4,128)(4,1)S(1)} %iota_compare_fusion.1), kind=kLoop, calls=%fused_computation | loop fusion | flops 1966080 | bytes 7864440 | tf_op jit(solution)/shard_map/jit(_where)/select_n | solution.py:119
  50.4 5.1 %collective-permute-start.3 = (bf16[2,128,256]{2,1,0:T(8,128)(2,1)S(1)}, bf16[2,128,256]{2,1,0:T(8,128)(2,1)S(1)}, u32[]{:S(2)}, u32[]{:S(2)}) collective-permute-start(bf16[2,128,256]{2,1,0:T(8,128)(2,1)S(1)} %slice.16), channel_id=1, source_target_pairs={{0,96},{1,673},{2,98},{3,675},{4,100},{5,677},{6,102},{7,679},{8,1... | collective-permute-start | bytes 393224 | tf_op jit(solution)/shard_map/ppermute | solution.py:110
  55.5 0.0 collective-permute-done.6.refs_6_
  55.6 1.9 collective-permute-start.7
  57.5 0.5 collective-permute-done.3.refs_4_
  58.0 5.6 %collective-permute-done.7.refs_5_ = bf16[2,128,256]{2,1,0:T(8,128)(2,1)S(1)} collective-permute-done((bf16[2,128,256]{2,1,0:T(8,128)(2,1)S(1)}, bf16[2,128,256]{2,1,0:T(8,128)(2,1)S(1)}, u32[]{:S(2)}, u32[]{:S(2)}) %collective-permute-start.7) | collective-permute-done | bytes 131104 | tf_op jit(solution)/shard_map/ppermute | solution.py:111
  63.6 2.5 %shard_map.74 = bf16[12,128,256]{2,1,0:T(8,128)(2,1)S(1)} custom-call(s32[1]{0:T(128)S(6)} %sub.28.parity, s32[120]{0:T(128)S(1)} %fusion.2.slots, bf16[12,2,5,128,128]{4,3,2,1,0:T(8,128)(2,1)S(1)} %broadcast_select_fusion.weights, bf16[4,128,256]{2,1,0:T(8,128)(2,1)S(1)} %all_to_all.30.refs_0_, bf16[4,128,256]{2,1,0:T(8,128)(2,1)S(1)} %collective-permute-done.refs_1_, ...), custom_call_target="tpu_custom_call" | custom-call | flops 503316480 | bytes 6291456 | tf_op jit(solution)/shard_map/pallas_call | solution.py:89
  66.1 1.9 collective-permute-start.8
  68.0 2.5 %shard_map.73 = f32[12,128,256]{2,1,0:T(8,128)S(1)} custom-call(s32[1]{0:T(128)} %bitcast.parity, s32[120]{0:T(128)S(1)} %fusion.2.slots, bf16[12,2,5,128,128]{4,3,2,1,0:T(8,128)(2,1)S(1)} %broadcast_select_fusion.weights, bf16[4,128,256]{2,1,0:T(8,128)(2,1)S(1)} %all_to_all.30.refs_0_, bf16[4,128,256]{2,1,0:T(8,128)(2,1)S(1)} %collective-permute-done.refs_1_, ...), custom_call_target="tpu_custom_call" | custom-call | flops 503316480 | bytes 6291456 | tf_op jit(solution)/shard_map/pallas_call | solution.py:89
  70.5 0.2 add_convert_fusion.1
  70.8 0.0 copy-start.5
  70.8 0.0 copy-start.3
  70.8 0.0 copy-start.4
  70.8 17.2 %all_to_all.31 = bf16[4,3,128,256]{3,2,1,0:T(8,128)(2,1)S(1)} all-to-all(bf16[4,3,128,256]{3,2,1,0:T(8,128)(2,1)S(1)} %bitcast.7), channel_id=1, replica_groups={{0,6,12,18},{1,7,13,19},{2,8,14,20},{3,9,15,21},{4,10,16,22},{5,11,17,2..., dimensions={0} | all-to-all | bytes 1572864 | tf_op jit(solution)/shard_map/all_to_all | solution.py:142
  88.0 0.8 reduce_sum.42
  88.8 11.2 %all-to-all-start.2 = ((bf16[3,128,256]{2,1,0:T(8,128)(2,1)}), bf16[3,128,256]{2,1,0:T(8,128)(2,1)S(1)}, u32[]{:S(2)}, u32[]{:S(2)}) async-start(bf16[3,128,256]{2,1,0:T(8,128)(2,1)} %reduce_sum.42), calls=%async_computation.2 | async-start | bytes 393216 | tf_op jit(solution)/shard_map/all_to_all | solution.py:144
  100.0 11.1 %all-to-all-done.2 = bf16[3,128,256]{2,1,0:T(8,128)(2,1)S(1)} async-done(((bf16[3,128,256]{2,1,0:T(8,128)(2,1)}), bf16[3,128,256]{2,1,0:T(8,128)(2,1)S(1)}, u32[]{:S(2)}, u32[]{:S(2)}) %all-to-all-start.2) | async-done | bytes 196640 | tf_op jit(solution)/shard_map/all_to_all | solution.py:144
  111.2 0.1 fusion.1
  111.3 12.8 %all_to_all.32.refs_0_ = bf16[4,128,256]{2,1,0:T(8,128)(2,1)S(1)} all-to-all(bf16[4,128,256]{2,1,0:T(8,128)(2,1)S(1)} %broadcast_in_dim.45), channel_id=1, replica_groups={{0,24,48,72},{96,120,144,168},{192,216,240,264},{288,312,336,360},{384,..., dimensions={0} | all-to-all | bytes 524288 | tf_op jit(solution)/shard_map/all_to_all | solution.py:104
  124.1 1.9 collective-permute-start.9
  126.0 3.9 %collective-permute-start.13 = (bf16[4,128,256]{2,1,0:T(8,128)(2,1)S(1)}, bf16[4,128,256]{2,1,0:T(8,128)(2,1)S(1)}, u32[]{:S(2)}, u32[]{:S(2)}) collective-permute-start(bf16[4,128,256]{2,1,0:T(8,128)(2,1)S(1)} %all_to_all.32.refs_0_), channel_id=1, source_target_pairs={{0,672},{1,97},{2,674},{3,99},{4,676},{5,101},{6,678},{7,103},{8,6... | collective-permute-start | bytes 786440 | tf_op jit(solution)/shard_map/ppermute | solution.py:108
  130.0 3.9 %collective-permute-done.9.refs_1_ = bf16[4,128,256]{2,1,0:T(8,128)(2,1)S(1)} collective-permute-done((bf16[4,128,256]{2,1,0:T(8,128)(2,1)S(1)}, bf16[4,128,256]{2,1,0:T(8,128)(2,1)S(1)}, u32[]{:S(2)}, u32[]{:S(2)}) %collective-permute-start.9) | collective-permute-done | bytes 262176 | tf_op jit(solution)/shard_map/ppermute | solution.py:107
  133.8 2.8 %collective-permute-start.10 = (bf16[4,128,256]{2,1,0:T(8,128)(2,1)S(1)}, bf16[4,128,256]{2,1,0:T(8,128)(2,1)S(1)}, u32[]{:S(2)}, u32[]{:S(2)}) collective-permute-start(bf16[4,128,256]{2,1,0:T(8,128)(2,1)S(1)} %collective-permute-done.9.refs_1_), channel_id=1, source_target_pairs={{0,96},{1,673},{2,98},{3,675},{4,100},{5,677},{6,102},{7,679},{8,1... | collective-permute-start | bytes 786440 | tf_op jit(solution)/shard_map/ppermute | solution.py:107
  136.6 0.0 collective-permute-done.13.refs_8_
  136.6 3.1 %collective-permute-start.14 = (bf16[4,128,256]{2,1,0:T(8,128)(2,1)S(1)}, bf16[4,128,256]{2,1,0:T(8,128)(2,1)S(1)}, u32[]{:S(2)}, u32[]{:S(2)}) collective-permute-start(bf16[4,128,256]{2,1,0:T(8,128)(2,1)S(1)} %collective-permute-done.13.refs_8_), channel_id=1, source_target_pairs={{0,672},{1,97},{2,674},{3,99},{4,676},{5,101},{6,678},{7,103},{8,6... | collective-permute-start | bytes 786440 | tf_op jit(solution)/shard_map/ppermute | solution.py:108
  139.7 3.2 %collective-permute-done.10.refs_2_ = bf16[4,128,256]{2,1,0:T(8,128)(2,1)S(1)} collective-permute-done((bf16[4,128,256]{2,1,0:T(8,128)(2,1)S(1)}, bf16[4,128,256]{2,1,0:T(8,128)(2,1)S(1)}, u32[]{:S(2)}, u32[]{:S(2)}) %collective-permute-start.10) | collective-permute-done | bytes 262176 | tf_op jit(solution)/shard_map/ppermute | solution.py:107
  142.9 5.5 %collective-permute-start.11 = (bf16[4,128,256]{2,1,0:T(8,128)(2,1)S(1)}, bf16[4,128,256]{2,1,0:T(8,128)(2,1)S(1)}, u32[]{:S(2)}, u32[]{:S(2)}) collective-permute-start(bf16[4,128,256]{2,1,0:T(8,128)(2,1)S(1)} %collective-permute-done.10.refs_2_), channel_id=1, source_target_pairs={{0,96},{1,673},{2,98},{3,675},{4,100},{5,677},{6,102},{7,679},{8,1... | collective-permute-start | bytes 786440 | tf_op jit(solution)/shard_map/ppermute | solution.py:107
  148.4 0.0 collective-permute-done.14.refs_7_
  148.5 1.9 collective-permute-start.15
  150.4 4.0 %collective-permute-done.11.refs_3_ = bf16[4,128,256]{2,1,0:T(8,128)(2,1)S(1)} collective-permute-done((bf16[4,128,256]{2,1,0:T(8,128)(2,1)S(1)}, bf16[4,128,256]{2,1,0:T(8,128)(2,1)S(1)}, u32[]{:S(2)}, u32[]{:S(2)}) %collective-permute-start.11) | collective-permute-done | bytes 262176 | tf_op jit(solution)/shard_map/ppermute | solution.py:107
  154.4 5.6 %collective-permute-start.12 = (bf16[2,128,256]{2,1,0:T(8,128)(2,1)S(1)}, bf16[2,128,256]{2,1,0:T(8,128)(2,1)S(1)}, u32[]{:S(2)}, u32[]{:S(2)}) collective-permute-start(bf16[2,128,256]{2,1,0:T(8,128)(2,1)S(1)} %slice.18), channel_id=1, source_target_pairs={{0,96},{1,673},{2,98},{3,675},{4,100},{5,677},{6,102},{7,679},{8,1... | collective-permute-start | bytes 393224 | tf_op jit(solution)/shard_map/ppermute | solution.py:110
  160.0 0.0 collective-permute-done.15.refs_6_
  160.1 1.9 collective-permute-start.16
  162.0 0.5 collective-permute-done.12.refs_4_
  162.5 5.6 %collective-permute-done.16.refs_5_ = bf16[2,128,256]{2,1,0:T(8,128)(2,1)S(1)} collective-permute-done((bf16[2,128,256]{2,1,0:T(8,128)(2,1)S(1)}, bf16[2,128,256]{2,1,0:T(8,128)(2,1)S(1)}, u32[]{:S(2)}, u32[]{:S(2)}) %collective-permute-start.16) | collective-permute-done | bytes 131104 | tf_op jit(solution)/shard_map/ppermute | solution.py:111
  168.2 2.1 %copy-done.1 = bf16[12,2,5,128,128]{4,3,2,1,0:T(8,128)(2,1)S(1)} copy-done((bf16[12,2,5,128,128]{4,3,2,1,0:T(8,128)(2,1)S(1)}, bf16[12,2,5,128,128]{4,3,2,1,0:T(8,128)(2,1)}, u32[]{:S(2)}) %copy-start.1) | copy-done | bytes 3932184
  170.3 2.5 %shard_map.76 = bf16[12,128,256]{2,1,0:T(8,128)(2,1)S(1)} custom-call(s32[1]{0:T(128)S(6)} %sub.28.parity, s32[120]{0:T(128)S(1)} %fusion.2.slots, bf16[12,2,5,128,128]{4,3,2,1,0:T(8,128)(2,1)S(1)} %copy-done.1, bf16[4,128,256]{2,1,0:T(8,128)(2,1)S(1)} %all_to_all.32.refs_0_, bf16[4,128,256]{2,1,0:T(8,128)(2,1)S(1)} %collective-permute-done.9.refs_1_, ...), custom_call_target="tpu_custom_call" | custom-call | flops 503316480 | bytes 6291456 | tf_op jit(solution)/shard_map/pallas_call | solution.py:89
  172.7 1.9 collective-permute-start.17
  174.7 2.5 %shard_map.75 = f32[12,128,256]{2,1,0:T(8,128)S(1)} custom-call(s32[1]{0:T(128)} %bitcast.parity, s32[120]{0:T(128)S(1)} %fusion.2.slots, bf16[12,2,5,128,128]{4,3,2,1,0:T(8,128)(2,1)S(1)} %copy-done.2, bf16[4,128,256]{2,1,0:T(8,128)(2,1)S(1)} %all_to_all.32.refs_0_, bf16[4,128,256]{2,1,0:T(8,128)(2,1)S(1)} %collective-permute-done.9.refs_1_, ...), custom_call_target="tpu_custom_call" | custom-call | flops 503316480 | bytes 6291456 | tf_op jit(solution)/shard_map/pallas_call | solution.py:89
  177.1 0.0 collective-permute-done.17
  177.1 0.2 add_convert_fusion
  177.4 15.6 %all_to_all.33 = bf16[4,3,128,256]{3,2,1,0:T(8,128)(2,1)S(1)} all-to-all(bf16[4,3,128,256]{3,2,1,0:T(8,128)(2,1)S(1)} %bitcast.8), channel_id=1, replica_groups={{0,6,12,18},{1,7,13,19},{2,8,14,20},{3,9,15,21},{4,10,16,22},{5,11,17,2..., dimensions={0} | all-to-all | bytes 1572864 | tf_op jit(solution)/shard_map/all_to_all | solution.py:142
  193.0 0.2 reduce_sum.44
  193.2 14.9 %all_to_all.34 = bf16[3,128,256]{2,1,0:T(8,128)(2,1)S(1)} all-to-all(bf16[3,128,256]{2,1,0:T(8,128)(2,1)S(1)} %reduce_sum.44), channel_id=1, replica_groups={{0,2,4},{1,3,5},{6,8,10},{7,9,11},{12,14,16},{13,15,17},{18,20,22},{19,..., dimensions={0} | all-to-all | bytes 393216 | tf_op jit(solution)/shard_map/all_to_all | solution.py:144
  208.1 0.8 convert_select_fusion
  (20 shorter events, 0.2 us)
Async XLA Ops:
  17.6 10.0 %collective-permute-start = (bf16[4,128,256]{2,1,0:T(8,128)(2,1)S(1)}, bf16[4,128,256]{2,1,0:T(8,128)(2,1)S(1)}, u32[]{:S(2)}, u32[]{:S(2)}) collective-permute-start(bf16[4,128,256]{2,1,0:T(8,128)(2,1)S(1)} %all_to_all.30.refs_0_), channel_id=1, source_target_pairs={{0,96},{1,673},{2,98},{3,675},{4,100},{5,677},{6,102},{7,679},{8,1... | collective-permute-start | bytes 786440 | tf_op jit(solution)/shard_map/ppermute | solution.py:107
  22.3 12.1 %collective-permute-start.4 = (bf16[4,128,256]{2,1,0:T(8,128)(2,1)S(1)}, bf16[4,128,256]{2,1,0:T(8,128)(2,1)S(1)}, u32[]{:S(2)}, u32[]{:S(2)}) collective-permute-start(bf16[4,128,256]{2,1,0:T(8,128)(2,1)S(1)} %all_to_all.30.refs_0_), channel_id=1, source_target_pairs={{0,672},{1,97},{2,674},{3,99},{4,676},{5,101},{6,678},{7,103},{8,6... | collective-permute-start | bytes 786440 | tf_op jit(solution)/shard_map/ppermute | solution.py:108
  27.7 11.6 %collective-permute-start.1 = (bf16[4,128,256]{2,1,0:T(8,128)(2,1)S(1)}, bf16[4,128,256]{2,1,0:T(8,128)(2,1)S(1)}, u32[]{:S(2)}, u32[]{:S(2)}) collective-permute-start(bf16[4,128,256]{2,1,0:T(8,128)(2,1)S(1)} %collective-permute-done.refs_1_), channel_id=1, source_target_pairs={{0,96},{1,673},{2,98},{3,675},{4,100},{5,677},{6,102},{7,679},{8,1... | collective-permute-start | bytes 786440 | tf_op jit(solution)/shard_map/ppermute | solution.py:107
  34.4 11.6 %collective-permute-start.5 = (bf16[4,128,256]{2,1,0:T(8,128)(2,1)S(1)}, bf16[4,128,256]{2,1,0:T(8,128)(2,1)S(1)}, u32[]{:S(2)}, u32[]{:S(2)}) collective-permute-start(bf16[4,128,256]{2,1,0:T(8,128)(2,1)S(1)} %collective-permute-done.4.refs_8_), channel_id=1, source_target_pairs={{0,672},{1,97},{2,674},{3,99},{4,676},{5,101},{6,678},{7,103},{8,6... | collective-permute-start | bytes 786440 | tf_op jit(solution)/shard_map/ppermute | solution.py:108
  39.2 11.1 %collective-permute-start.2 = (bf16[4,128,256]{2,1,0:T(8,128)(2,1)S(1)}, bf16[4,128,256]{2,1,0:T(8,128)(2,1)S(1)}, u32[]{:S(2)}, u32[]{:S(2)}) collective-permute-start(bf16[4,128,256]{2,1,0:T(8,128)(2,1)S(1)} %collective-permute-done.1.refs_2_), channel_id=1, source_target_pairs={{0,96},{1,673},{2,98},{3,675},{4,100},{5,677},{6,102},{7,679},{8,1... | collective-permute-start | bytes 786440 | tf_op jit(solution)/shard_map/ppermute | solution.py:107
  46.0 9.6 %collective-permute-start.6 = (bf16[4,128,256]{2,1,0:T(8,128)(2,1)S(1)}, bf16[4,128,256]{2,1,0:T(8,128)(2,1)S(1)}, u32[]{:S(2)}, u32[]{:S(2)}) collective-permute-start(bf16[4,128,256]{2,1,0:T(8,128)(2,1)S(1)} %collective-permute-done.5.refs_7_), channel_id=1, source_target_pairs={{0,672},{1,97},{2,674},{3,99},{4,676},{5,101},{6,678},{7,103},{8,6... | collective-permute-start | bytes 786440 | tf_op jit(solution)/shard_map/ppermute | solution.py:108
  50.4 17.7 %copy-start = (bf16[12,2,5,128,128]{4,3,2,1,0:T(8,128)(2,1)}, bf16[12,2,5,128,128]{4,3,2,1,0:T(8,128)(2,1)S(1)}, u32[]{:S(2)}) copy-start(bf16[12,2,5,128,128]{4,3,2,1,0:T(8,128)(2,1)S(1)} %broadcast_select_fusion.weights) | copy-start | bytes 11796484
  50.4 7.6 %collective-permute-start.3 = (bf16[2,128,256]{2,1,0:T(8,128)(2,1)S(1)}, bf16[2,128,256]{2,1,0:T(8,128)(2,1)S(1)}, u32[]{:S(2)}, u32[]{:S(2)}) collective-permute-start(bf16[2,128,256]{2,1,0:T(8,128)(2,1)S(1)} %slice.16), channel_id=1, source_target_pairs={{0,96},{1,673},{2,98},{3,675},{4,100},{5,677},{6,102},{7,679},{8,1... | collective-permute-start | bytes 393224 | tf_op jit(solution)/shard_map/ppermute | solution.py:110
  55.6 8.1 %collective-permute-start.7 = (bf16[2,128,256]{2,1,0:T(8,128)(2,1)S(1)}, bf16[2,128,256]{2,1,0:T(8,128)(2,1)S(1)}, u32[]{:S(2)}, u32[]{:S(2)}) collective-permute-start(bf16[2,128,256]{2,1,0:T(8,128)(2,1)S(1)} %slice.17), channel_id=1, source_target_pairs={{0,672},{1,97},{2,674},{3,99},{4,676},{5,101},{6,678},{7,103},{8,6... | collective-permute-start | bytes 393224 | tf_op jit(solution)/shard_map/ppermute | solution.py:111
  66.1 4.4 %collective-permute-start.8 = (bf16[12,128,256]{2,1,0:T(8,128)(2,1)S(1)}, bf16[12,128,256]{2,1,0:T(8,128)(2,1)S(1)}, u32[]{:S(2)}, u32[]{:S(2)}) collective-permute-start(bf16[12,128,256]{2,1,0:T(8,128)(2,1)S(1)} %shard_map.74), channel_id=1, source_target_pairs={{0,1},{1,0},{2,3},{3,2},{4,5},{5,4},{6,7},{7,6},{8,9},{9,8},{10,11... | collective-permute-start | bytes 2359304 | tf_op jit(solution)/shard_map/ppermute | solution.py:138
  70.8 29.2 %copy-start.5 = (s32[128]{0:T(128)S(1)}, s32[128]{0:T(128)}, u32[]{:S(2)}) copy-start(s32[128]{0:T(128)} %param.9) | copy-start | bytes 1540
  70.8 40.4 %copy-start.3 = (f32[128,256]{1,0:T(8,128)S(1)}, f32[128,256]{1,0:T(8,128)}, u32[]{:S(2)}) copy-start(f32[128,256]{1,0:T(8,128)} %param.7) | copy-start | bytes 393220
  70.8 40.4 %copy-start.4 = (s32[128]{0:T(128)S(1)}, s32[128]{0:T(128)}, u32[]{:S(2)}) copy-start(s32[128]{0:T(128)} %param.10) | copy-start | bytes 1540
  88.8 22.3 %all-to-all-start.2 = ((bf16[3,128,256]{2,1,0:T(8,128)(2,1)}), bf16[3,128,256]{2,1,0:T(8,128)(2,1)S(1)}, u32[]{:S(2)}, u32[]{:S(2)}) async-start(bf16[3,128,256]{2,1,0:T(8,128)(2,1)} %reduce_sum.42), calls=%async_computation.2 | async-start | bytes 393216 | tf_op jit(solution)/shard_map/all_to_all | solution.py:144
  124.1 9.7 %collective-permute-start.9 = (bf16[4,128,256]{2,1,0:T(8,128)(2,1)S(1)}, bf16[4,128,256]{2,1,0:T(8,128)(2,1)S(1)}, u32[]{:S(2)}, u32[]{:S(2)}) collective-permute-start(bf16[4,128,256]{2,1,0:T(8,128)(2,1)S(1)} %all_to_all.32.refs_0_), channel_id=1, source_target_pairs={{0,96},{1,673},{2,98},{3,675},{4,100},{5,677},{6,102},{7,679},{8,1... | collective-permute-start | bytes 786440 | tf_op jit(solution)/shard_map/ppermute | solution.py:107
  126.0 10.6 %collective-permute-start.13 = (bf16[4,128,256]{2,1,0:T(8,128)(2,1)S(1)}, bf16[4,128,256]{2,1,0:T(8,128)(2,1)S(1)}, u32[]{:S(2)}, u32[]{:S(2)}) collective-permute-start(bf16[4,128,256]{2,1,0:T(8,128)(2,1)S(1)} %all_to_all.32.refs_0_), channel_id=1, source_target_pairs={{0,672},{1,97},{2,674},{3,99},{4,676},{5,101},{6,678},{7,103},{8,6... | collective-permute-start | bytes 786440 | tf_op jit(solution)/shard_map/ppermute | solution.py:108
  133.8 9.1 %collective-permute-start.10 = (bf16[4,128,256]{2,1,0:T(8,128)(2,1)S(1)}, bf16[4,128,256]{2,1,0:T(8,128)(2,1)S(1)}, u32[]{:S(2)}, u32[]{:S(2)}) collective-permute-start(bf16[4,128,256]{2,1,0:T(8,128)(2,1)S(1)} %collective-permute-done.9.refs_1_), channel_id=1, source_target_pairs={{0,96},{1,673},{2,98},{3,675},{4,100},{5,677},{6,102},{7,679},{8,1... | collective-permute-start | bytes 786440 | tf_op jit(solution)/shard_map/ppermute | solution.py:107
  136.6 11.8 %collective-permute-start.14 = (bf16[4,128,256]{2,1,0:T(8,128)(2,1)S(1)}, bf16[4,128,256]{2,1,0:T(8,128)(2,1)S(1)}, u32[]{:S(2)}, u32[]{:S(2)}) collective-permute-start(bf16[4,128,256]{2,1,0:T(8,128)(2,1)S(1)} %collective-permute-done.13.refs_8_), channel_id=1, source_target_pairs={{0,672},{1,97},{2,674},{3,99},{4,676},{5,101},{6,678},{7,103},{8,6... | collective-permute-start | bytes 786440 | tf_op jit(solution)/shard_map/ppermute | solution.py:108
  142.9 11.5 %collective-permute-start.11 = (bf16[4,128,256]{2,1,0:T(8,128)(2,1)S(1)}, bf16[4,128,256]{2,1,0:T(8,128)(2,1)S(1)}, u32[]{:S(2)}, u32[]{:S(2)}) collective-permute-start(bf16[4,128,256]{2,1,0:T(8,128)(2,1)S(1)} %collective-permute-done.10.refs_2_), channel_id=1, source_target_pairs={{0,96},{1,673},{2,98},{3,675},{4,100},{5,677},{6,102},{7,679},{8,1... | collective-permute-start | bytes 786440 | tf_op jit(solution)/shard_map/ppermute | solution.py:107
  148.5 11.6 %collective-permute-start.15 = (bf16[4,128,256]{2,1,0:T(8,128)(2,1)S(1)}, bf16[4,128,256]{2,1,0:T(8,128)(2,1)S(1)}, u32[]{:S(2)}, u32[]{:S(2)}) collective-permute-start(bf16[4,128,256]{2,1,0:T(8,128)(2,1)S(1)} %collective-permute-done.14.refs_7_), channel_id=1, source_target_pairs={{0,672},{1,97},{2,674},{3,99},{4,676},{5,101},{6,678},{7,103},{8,6... | collective-permute-start | bytes 786440 | tf_op jit(solution)/shard_map/ppermute | solution.py:108
  154.4 8.1 %collective-permute-start.12 = (bf16[2,128,256]{2,1,0:T(8,128)(2,1)S(1)}, bf16[2,128,256]{2,1,0:T(8,128)(2,1)S(1)}, u32[]{:S(2)}, u32[]{:S(2)}) collective-permute-start(bf16[2,128,256]{2,1,0:T(8,128)(2,1)S(1)} %slice.18), channel_id=1, source_target_pairs={{0,96},{1,673},{2,98},{3,675},{4,100},{5,677},{6,102},{7,679},{8,1... | collective-permute-start | bytes 393224 | tf_op jit(solution)/shard_map/ppermute | solution.py:110
  160.1 8.1 %collective-permute-start.16 = (bf16[2,128,256]{2,1,0:T(8,128)(2,1)S(1)}, bf16[2,128,256]{2,1,0:T(8,128)(2,1)S(1)}, u32[]{:S(2)}, u32[]{:S(2)}) collective-permute-start(bf16[2,128,256]{2,1,0:T(8,128)(2,1)S(1)} %slice.19), channel_id=1, source_target_pairs={{0,672},{1,97},{2,674},{3,99},{4,676},{5,101},{6,678},{7,103},{8,6... | collective-permute-start | bytes 393224 | tf_op jit(solution)/shard_map/ppermute | solution.py:111
  168.2 2.1 %copy-start.1 = (bf16[12,2,5,128,128]{4,3,2,1,0:T(8,128)(2,1)S(1)}, bf16[12,2,5,128,128]{4,3,2,1,0:T(8,128)(2,1)}, u32[]{:S(2)}) copy-start(bf16[12,2,5,128,128]{4,3,2,1,0:T(8,128)(2,1)} %copy-done) | copy-start | bytes 11796484
  170.3 4.4 %copy-start.2 = (bf16[12,2,5,128,128]{4,3,2,1,0:T(8,128)(2,1)S(1)}, bf16[12,2,5,128,128]{4,3,2,1,0:T(8,128)(2,1)}, u32[]{:S(2)}) copy-start(bf16[12,2,5,128,128]{4,3,2,1,0:T(8,128)(2,1)} %copy-done) | copy-start | bytes 11796484
  172.7 4.4 %collective-permute-start.17 = (bf16[12,128,256]{2,1,0:T(8,128)(2,1)S(1)}, bf16[12,128,256]{2,1,0:T(8,128)(2,1)S(1)}, u32[]{:S(2)}, u32[]{:S(2)}) collective-permute-start(bf16[12,128,256]{2,1,0:T(8,128)(2,1)S(1)} %shard_map.76), channel_id=1, source_target_pairs={{0,1},{1,0},{2,3},{3,2},{4,5},{5,4},{6,7},{7,6},{8,9},{9,8},{10,11... | collective-permute-start | bytes 2359304 | tf_op jit(solution)/shard_map/ppermute | solution.py:138

commit v4 on v3

v4 whole, which is shorter than its diff:
```python
import jax
import jax.numpy as jnp
from jax import lax
from jax.experimental import pallas as pl
from jax.experimental.pallas import tpu as pltpu
from jax.sharding import PartitionSpec as P

SWEEPS = 2
RETAIN = 0.8

Y, ZL, X, ZH, CORES = 8, 4, 4, 3, 2
PAIRS = X * ZH
STEP = 4

Z_GROUPS = [[y * ZL + z for z in range(ZL)] for y in range(Y)]
Y_GROUPS = [[y * ZL + z for y in range(Y)] for z in range(ZL)]
X_GROUPS = [
    [(x * ZH + z) * CORES + c for x in range(X)] for z in range(ZH) for c in range(CORES)
]
H_GROUPS = [
    [(x * ZH + z) * CORES + c for z in range(ZH)] for x in range(X) for c in range(CORES)
]
SWAP = [(d, d ^ 1) for d in range(X * ZH * CORES)]


def sum_kernel(parity, slots, weights, near, far, out):
    depth = weights.shape[2]
    for q in range(STEP):
        base = ((pl.program_id(0) * STEP + q) * CORES + parity[0]) * depth
        total = None
        for t in range(0, depth, 2):
            group = range(t, min(t + 2, depth))
            left = jnp.concatenate([weights[q, 0, u] for u in group], axis=1)
            rows = []
            for u in group:
                column = slots[base + u]
                y, z = column // ZL, column % ZL
                rows += [near[column], far[z * Y + y]]
            right = jnp.concatenate(rows, axis=0)
            term = jnp.dot(left, right, preferred_element_type=jnp.float32)
            total = term if total is None else total + term
        out[q] = total.astype(out.dtype)


def partial_sums(parity, slots, weights, near, far, dtype):
    _, _, depth, size, _ = weights.shape
    classes = near.shape[-1]
    whole = lambda i, parity, slots: (0, 0, 0)
    grid_spec = pltpu.PrefetchScalarGridSpec(
        num_scalar_prefetch=2,
        grid=(PAIRS // STEP,),
        in_specs=[
            pl.BlockSpec(
                (STEP, 1, depth, size, size), lambda i, parity, slots: (i, parity[0], 0, 0, 0)
            ),
            pl.BlockSpec(near.shape, whole),
            pl.BlockSpec(far.shape, whole),
        ],
        out_specs=pl.BlockSpec((STEP, size, classes), lambda i, parity, slots: (i, 0, 0)),
    )
    return pl.pallas_call(
        sum_kernel,
        grid_spec=grid_spec,
        out_shape=jax.ShapeDtypeStruct((PAIRS, size, classes), dtype),
        compiler_params=pltpu.CompilerParams(vmem_limit_bytes=32 * 1024 * 1024),
        cost_estimate=pl.CostEstimate(
            flops=2 * PAIRS * depth * size * size * classes,
            bytes_accessed=6 * 1024 * 1024,
            transcendentals=0,
        ),
    )(parity, slots, weights, near, far)


def spread(block, groups):
    count = len(groups[0])
    copies = jnp.broadcast_to(block[None], (count,) + block.shape)
    return lax.all_to_all(copies, "src", 0, 0, axis_index_groups=groups)


def per_device(prior, degrees, seed_mask, seed_labels, adjacency, block_cols, slot_counts):
    classes = prior.shape[1]
    depth, size = adjacency.shape[3], adjacency.shape[4]
    active = jnp.arange(depth, dtype=jnp.int32)[None, :] < slot_counts[0, 0][:, None]
    core = lax.axis_index("dst").astype(jnp.int32) % CORES
    mine = core.reshape(1)
    other = 1 - mine
    slots = block_cols[0, 0].reshape(-1)
    half = size // 2
    inverse_root = lax.rsqrt(degrees.astype(jnp.float32))[:, None]
    onehot = (seed_labels[:, None] == jnp.arange(classes, dtype=jnp.int32)[None, :]).astype(
        jnp.float32
    )
    seeded = seed_mask[:, None] > 0
    scores = prior
    for _ in range(SWEEPS):
        outgoing = (inverse_root * scores).astype(jnp.bfloat16)
        own = spread(outgoing[:half], Z_GROUPS)
        near = lax.all_gather(own, "src", axis_index_groups=Y_GROUPS)
        own, edges = lax.optimization_barrier((own, adjacency))
        ahead = own[0, 0, 0] > jnp.inf
        rest = jnp.where(ahead, jnp.zeros((), outgoing.dtype), outgoing[half:])
        far = spread(spread(rest, Y_GROUPS), Z_GROUPS)
        near = near.reshape(Y * ZL, half, classes)
        far = far.reshape(ZL * Y, half, classes)
        weights = jnp.where(active[:, :, None, None], edges[0, 0], jnp.zeros((), edges.dtype))
        weights = weights.reshape(PAIRS, CORES, depth, size, size)
        send = partial_sums(other, slots, weights, near, far, jnp.bfloat16)
        swapped = lax.ppermute(send, "dst", SWAP)
        keep = partial_sums(mine, slots, weights, near, far, jnp.float32)
        chip = (keep + swapped.astype(jnp.float32)).astype(jnp.bfloat16)
        chip = chip.reshape(X, ZH, size, classes)
        rows = lax.all_to_all(chip, "dst", 0, 0, axis_index_groups=X_GROUPS)
        rows = jnp.sum(rows.astype(jnp.float32), axis=0).astype(jnp.bfloat16)
        parts = lax.all_to_all(rows, "dst", 0, 0, axis_index_groups=H_GROUPS)
        summed = jnp.sum(parts.astype(jnp.float32), axis=0)
        hidden = RETAIN * inverse_root * summed + (1.0 - RETAIN) * prior
        scores = jnp.where(seeded, onehot, hidden)
    return scores


def solution(mesh):
    in_specs = (
        P(("src", "dst"), None),
        P(("src", "dst")),
        P(("src", "dst")),
        P(("src", "dst")),
        P("src", "dst", None, None, None, None),
        P("src", "dst", None, None),
        P("src", "dst", None),
    )
    out_specs = P(("src", "dst"), None)
    return jax.shard_map(
        per_device, mesh=mesh, in_specs=in_specs, out_specs=out_specs, check_vma=False
    )
```

time: 210 us -> 257 us (1.22)
  starting transfers between devices: 69.9 us -> 19.4 us
  waiting for transfers between devices: 40.7 us -> 88.2 us
  blocking collectives: 76.4 us -> 102 us
  between operations: 0.45 us -> 15 us
  local copies, waits for them, and re-layouts: 3.7 us -> 11 us
  other arithmetic: 7.94 us -> 13.5 us
    all_gather x0 -> x2, waiting for transfers between devices: none -> 76.4 us  [per_device(): near = lax.all_gather(own, 'src', axis_index_groups=Y_GROUPS)]
    ppermute x16 -> x0, starting transfers between devices: 54.8 us -> none  [the longest x6 25.6 us: gather_blocks(): first.append(lax.ppermute(first[-1], ('src', 'dst'), ALONG))]
    ppermute x16 -> x0, waiting for transfers between devices: 29.6 us -> none  [the longest x6 14.6 us: gather_blocks(): first.append(lax.ppermute(first[-1], ('src', 'dst'), ALONG))]
    all_to_all x2 -> x4, blocking collectives: 28.7 us -> 50.2 us  [spread(): return lax.all_to_all(copies, 'src', 0, 0, axis_index_groups=groups)]
    all_to_all x0 -> x2, starting transfers between devices: none -> 7.37 us  [spread(): return lax.all_to_all(copies, 'src', 0, 0, axis_index_groups=groups)]
    select_n x1 -> x4, other arithmetic: 2.45 us -> 8.65 us  [the longest x2 8.63 us: per_device(): jnp.where(active[:, :, None, None], edges[0, 0], jnp.zeros((), edges.dtype))]
    unnamed x14 -> x26, local copies, waits for them, and re-layouts: 3.44 us -> 7.34 us
    all_to_all x1, starting transfers between devices: 11.2 us -> 8.14 us  [per_device(): parts = lax.all_to_all(rows, 'dst', 0, 0, axis_index_groups=H_GROUPS)]
  transfers between devices with their start and end apart: 19 -> 7, of which waited for: 11 -> 5; matrix products, arithmetic and copies ran while one was open for 3% -> 4% of each run, Pallas kernels for 2% -> 2%
where the time goes in v4:
time: 257 us; the launch traced here: 256 us
  blocking collectives  102 us (40%)
  waiting for transfers between devices  88.2 us (34%)
  starting transfers between devices  19.4 us (8%)
  between operations  15 us (6%)
  other arithmetic  13.5 us (5%)
  local copies, waits for them, and re-layouts  11 us (4%)
  Pallas kernels  7.77 us (3%)
    all_gather x2, waiting for transfers between devices, per_device(): near = lax.all_gather(own, 'src', axis_index_groups=Y_GROUPS)  76.4 us
    all_to_all x4, blocking collectives, spread(): return lax.all_to_all(copies, 'src', 0, 0, axis_index_groups=groups)  50.2 us
    all_to_all x2, blocking collectives, per_device(): rows = lax.all_to_all(chip, 'dst', 0, 0, axis_index_groups=X_GROUPS)  33.6 us
    all_to_all x1, blocking collectives, per_device(): parts = lax.all_to_all(rows, 'dst', 0, 0, axis_index_groups=H_GROUPS)  17.7 us
    all_to_all x1, waiting for transfers between devices, per_device(): parts = lax.all_to_all(rows, 'dst', 0, 0, axis_index_groups=H_GROUPS)  9.82 us
    select_n x2, other arithmetic, per_device(): jnp.where(active[:, :, None, None], edges[0, 0], jnp.zeros((), edges.dtype))  8.63 us
    all_to_all x1, starting transfers between devices, per_device(): parts = lax.all_to_all(rows, 'dst', 0, 0, axis_index_groups=H_GROUPS)  8.14 us
    pallas_call x4, Pallas kernels, partial_sums(): pl.pallas_call(sum_kernel, grid_spec=grid_spec, out_shape=jax.ShapeDtypeS...  7.77 us
  transfers between devices with their start and end apart: 7, of which 5 were waited for; matrix products, arithmetic and copies ran while one was open for 4% of the time, Pallas kernels for 2%

profile of v4, /device:TPU:24, one launch (start us, length us, event | category | flops | bytes accessed | tf_op | source)
XLA Modules:
  0.0 256.3 jit_solution(15331015447049401244)
XLA Ops:
  6.5 0.7 broadcast_multiply_fusion
  7.2 1.0 multiply_convert_fusion
  8.2 13.1 %all_to_all.50 = bf16[4,64,256]{2,1,0:T(8,128)(2,1)S(1)} all-to-all(bf16[4,64,256]{2,1,0:T(8,128)(2,1)S(1)} %broadcast_in_dim.46), channel_id=1, replica_groups={{0,24,48,72},{96,120,144,168},{192,216,240,264},{288,312,336,360},{384,..., dimensions={0} | all-to-all | bytes 262144 | tf_op jit(solution)/shard_map/all_to_all | solution.py:77
  21.4 0.6 slice.19
  22.6 0.0 copy-start.10
  22.6 0.0 copy-start.8
  22.6 14.2 %all_to_all.51 = bf16[8,64,256]{2,1,0:T(8,128)(2,1)S(1)} all-to-all(bf16[8,64,256]{2,1,0:T(8,128)(2,1)S(1)} %broadcast_in_dim.80), channel_id=1, replica_groups={{0,96,192,288,384,480,576,672},{24,120,216,312,408,504,600,696},{48,144..., dimensions={0} | all-to-all | bytes 524288 | tf_op jit(solution)/shard_map/all_to_all | solution.py:77
  36.8 1.1 broadcast_in_dim.81
  37.9 0.0 copy-done.6
  37.9 3.5 %all-to-all-start.2 = ((bf16[4,8,64,256]{3,2,1,0:T(8,128)(2,1)}), bf16[4,8,64,256]{3,2,1,0:T(8,128)(2,1)S(1)}, u32[]{:S(2)}, u32[]{:S(2)}) async-start(bf16[4,8,64,256]{3,2,1,0:T(8,128)(2,1)} %broadcast_in_dim.81), calls=%async_computation.2 | async-start | bytes 2097152 | tf_op jit(solution)/shard_map/all_to_all | solution.py:77
  41.4 0.0 all-gather.5.cloned.1.call-start
  41.5 0.7 all-gather.5.cloned.1.call-update
  42.2 0.5 broadcast.44
  42.7 0.0 copy-done.10
  42.7 0.7 reduce.5
  43.4 0.1 lt.27
  43.5 0.0 copy-done.8
  43.5 0.1 copy.11
  43.6 0.1 reshape_squeeze.3.slots
  43.7 0.1 iota_compare_fusion.1
  43.8 4.3 %broadcast_select_fusion.1.weights = bf16[12,2,5,128,128]{4,3,2,1,0:T(8,128)(2,1)} fusion(bf16[12,2,5,128,128]{4,3,2,1,0:T(8,128)(2,1)} %bitcast.15, pred[12,2,5]{2,1,0:T(4,128)(4,1)S(1)} %iota_compare_fusion.1), kind=kLoop, calls=%fused_computation.1 | loop fusion | flops 1966080 | bytes 7864440 | tf_op jit(solution)/shard_map/jit(_where)/select_n | solution.py:105
  48.1 42.2 %all-gather.5.cloned.1.call-done.near = bf16[32,64,256]{2,1,0:T(8,128)(2,1)} async-done(((bf16[4,64,256]{2,1,0:T(8,128)(2,1)}), bf16[32,64,256]{2,1,0:T(8,128)(2,1)}) %all-gather.5.cloned.1.call-update) | async-done | bytes 1048592 | tf_op jit(solution)/shard_map/all_gather | solution.py:98
  90.3 0.0 all-to-all-done.2
  90.3 2.1 copy-done.1
  92.4 1.2 copy-done.3
  93.7 1.9 shard_map.74
  95.6 1.9 collective-permute-start
  97.5 0.0 copy-done.2
  97.5 1.9 shard_map.73
  99.5 0.3 collective-permute-done
  99.8 0.2 add_convert_fusion.1
  100.0 0.0 copy-start.11
  100.0 0.0 copy-start.5
  100.0 0.0 copy-start.9
  100.1 16.8 %all_to_all.52 = bf16[4,3,128,256]{3,2,1,0:T(8,128)(2,1)S(1)} all-to-all(bf16[4,3,128,256]{3,2,1,0:T(8,128)(2,1)S(1)} %bitcast.17), channel_id=1, replica_groups={{0,6,12,18},{1,7,13,19},{2,8,14,20},{3,9,15,21},{4,10,16,22},{5,11,17,2..., dimensions={0} | all-to-all | bytes 1572864 | tf_op jit(solution)/shard_map/all_to_all | solution.py:112
  116.9 0.8 reduce_sum.42
  117.7 8.1 %all-to-all-start.4 = ((bf16[3,128,256]{2,1,0:T(8,128)(2,1)}), bf16[3,128,256]{2,1,0:T(8,128)(2,1)S(1)}, u32[]{:S(2)}, u32[]{:S(2)}) async-start(bf16[3,128,256]{2,1,0:T(8,128)(2,1)} %reduce_sum.42), calls=%async_computation.4 | async-start | bytes 393216 | tf_op jit(solution)/shard_map/all_to_all | solution.py:114
  125.9 0.0 copy-done.11
  125.9 9.8 %all-to-all-done.4 = bf16[3,128,256]{2,1,0:T(8,128)(2,1)S(1)} async-done(((bf16[3,128,256]{2,1,0:T(8,128)(2,1)}), bf16[3,128,256]{2,1,0:T(8,128)(2,1)S(1)}, u32[]{:S(2)}, u32[]{:S(2)}) %all-to-all-start.4) | async-done | bytes 196640 | tf_op jit(solution)/shard_map/all_to_all | solution.py:114
  135.7 0.0 copy-done.5
  135.7 0.0 copy-done.9
  135.8 0.1 fusion.1
  135.9 11.1 %all_to_all.53 = bf16[4,64,256]{2,1,0:T(8,128)(2,1)S(1)} all-to-all(bf16[4,64,256]{2,1,0:T(8,128)(2,1)S(1)} %broadcast_in_dim.82), channel_id=1, replica_groups={{0,24,48,72},{96,120,144,168},{192,216,240,264},{288,312,336,360},{384,..., dimensions={0} | all-to-all | bytes 262144 | tf_op jit(solution)/shard_map/all_to_all | solution.py:77
  147.1 0.6 slice.22
  148.3 11.8 %all_to_all.54 = bf16[8,64,256]{2,1,0:T(8,128)(2,1)S(1)} all-to-all(bf16[8,64,256]{2,1,0:T(8,128)(2,1)S(1)} %broadcast_in_dim.83), channel_id=1, replica_groups={{0,96,192,288,384,480,576,672},{24,120,216,312,408,504,600,696},{48,144..., dimensions={0} | all-to-all | bytes 524288 | tf_op jit(solution)/shard_map/all_to_all | solution.py:77
  160.1 1.1 broadcast_in_dim.84
  161.3 0.0 copy-done.7
  161.3 3.9 %all-to-all-start.7 = ((bf16[4,8,64,256]{3,2,1,0:T(8,128)(2,1)}), bf16[4,8,64,256]{3,2,1,0:T(8,128)(2,1)S(1)}, u32[]{:S(2)}, u32[]{:S(2)}) async-start(bf16[4,8,64,256]{3,2,1,0:T(8,128)(2,1)} %broadcast_in_dim.84), calls=%async_computation.7 | async-start | bytes 2097152 | tf_op jit(solution)/shard_map/all_to_all | solution.py:77
  165.1 0.0 all-gather.7.cloned.1.call-start
  165.1 0.7 all-gather.7.cloned.1.call-update
  165.9 4.3 %broadcast_select_fusion.weights = bf16[12,2,5,128,128]{4,3,2,1,0:T(8,128)(2,1)} fusion(bf16[12,2,5,128,128]{4,3,2,1,0:T(8,128)(2,1)} %bitcast.16, pred[12,2,5]{2,1,0:T(4,128)(4,1)S(1)} %iota_compare_fusion.1), kind=kLoop, calls=%fused_computation | loop fusion | flops 1966080 | bytes 7864440 | tf_op jit(solution)/shard_map/jit(_where)/select_n | solution.py:105
  170.2 34.1 %all-gather.7.cloned.1.call-done.near = bf16[32,64,256]{2,1,0:T(8,128)(2,1)} async-done(((bf16[4,64,256]{2,1,0:T(8,128)(2,1)}), bf16[32,64,256]{2,1,0:T(8,128)(2,1)}) %all-gather.7.cloned.1.call-update) | async-done | bytes 1048592 | tf_op jit(solution)/shard_map/all_gather | solution.py:98
  204.3 0.0 all-to-all-done.7
  204.3 2.1 copy-done
  206.4 1.2 copy-done.4
  207.7 1.9 shard_map.76
  209.6 1.9 collective-permute-start.1
  211.5 1.9 shard_map.75
  213.5 0.3 collective-permute-done.1
  213.8 0.2 add_convert_fusion
  214.0 16.8 %all_to_all.55 = bf16[4,3,128,256]{3,2,1,0:T(8,128)(2,1)S(1)} all-to-all(bf16[4,3,128,256]{3,2,1,0:T(8,128)(2,1)S(1)} %bitcast.18), channel_id=1, replica_groups={{0,6,12,18},{1,7,13,19},{2,8,14,20},{3,9,15,21},{4,10,16,22},{5,11,17,2..., dimensions={0} | all-to-all | bytes 1572864 | tf_op jit(solution)/shard_map/all_to_all | solution.py:112
  230.8 0.2 reduce_sum.44
  230.9 17.7 %all_to_all.56 = bf16[3,128,256]{2,1,0:T(8,128)(2,1)S(1)} all-to-all(bf16[3,128,256]{2,1,0:T(8,128)(2,1)S(1)} %reduce_sum.44), channel_id=1, replica_groups={{0,2,4},{1,3,5},{6,8,10},{7,9,11},{12,14,16},{13,15,17},{18,20,22},{19,..., dimensions={0} | all-to-all | bytes 393216 | tf_op jit(solution)/shard_map/all_to_all | solution.py:114
  248.7 0.8 convert_select_fusion
  (18 shorter events, 0.2 us)
Async XLA Ops:
  21.4 16.6 %copy-start.6 = (bf16[4,64,256]{2,1,0:T(8,128)(2,1)}, bf16[4,64,256]{2,1,0:T(8,128)(2,1)S(1)}, u32[]{:S(2)}) copy-start(bf16[4,64,256]{2,1,0:T(8,128)(2,1)S(1)} %all_to_all.50) | copy-start | bytes 393220
  22.6 20.1 %copy-start.10 = (s32[1,1,24]{2,1,0:T(1,128)S(1)}, s32[1,1,24]{2,1,0:T(1,128)}, u32[]{:S(2)}) copy-start(s32[1,1,24]{2,1,0:T(1,128)} %param.13) | copy-start | bytes 292
  22.6 20.9 %copy-start.8 = (s32[1,1,24,5]{2,1,3,0:T(1,128)S(1)}, s32[1,1,24,5]{2,1,3,0:T(1,128)}, u32[]{:S(2)}) copy-start(s32[1,1,24,5]{2,1,3,0:T(1,128)} %param.12) | copy-start | bytes 1444
  37.9 52.4 %all-to-all-start.2 = ((bf16[4,8,64,256]{3,2,1,0:T(8,128)(2,1)}), bf16[4,8,64,256]{3,2,1,0:T(8,128)(2,1)S(1)}, u32[]{:S(2)}, u32[]{:S(2)}) async-start(bf16[4,8,64,256]{3,2,1,0:T(8,128)(2,1)} %broadcast_in_dim.81), calls=%async_computation.2 | async-start | bytes 2097152 | tf_op jit(solution)/shard_map/all_to_all | solution.py:77
  41.4 48.9 %all-gather.5.cloned.1.call-start = ((), (), s32[]{:S(2)}) async-start(), calls=%async_computation.10 | async-start | bytes 1179648 | tf_op jit(solution)/shard_map/all_gather | solution.py:98
  90.3 2.1 copy-start.1
  92.4 1.2 copy-start.3
  93.6 3.9 %copy-start.2 = (bf16[12,2,5,128,128]{4,3,2,1,0:T(8,128)(2,1)S(1)}, bf16[12,2,5,128,128]{4,3,2,1,0:T(8,128)(2,1)}, u32[]{:S(2)}) copy-start(bf16[12,2,5,128,128]{4,3,2,1,0:T(8,128)(2,1)} %broadcast_select_fusion.1.weights) | copy-start | bytes 11796484
  95.6 4.2 %collective-permute-start = (bf16[12,128,256]{2,1,0:T(8,128)(2,1)S(1)}, bf16[12,128,256]{2,1,0:T(8,128)(2,1)S(1)}, u32[]{:S(2)}, u32[]{:S(2)}) collective-permute-start(bf16[12,128,256]{2,1,0:T(8,128)(2,1)S(1)} %shard_map.74), channel_id=1, source_target_pairs={{0,1},{1,0},{2,3},{3,2},{4,5},{5,4},{6,7},{7,6},{8,9},{9,8},{10,11... | collective-permute-start | bytes 2359304 | tf_op jit(solution)/shard_map/ppermute | solution.py:108
  100.0 25.8 %copy-start.11 = (s32[128]{0:T(128)S(1)}, s32[128]{0:T(128)}, u32[]{:S(2)}) copy-start(s32[128]{0:T(128)} %param.9) | copy-start | bytes 1540
  100.0 35.7 %copy-start.5 = (f32[128,256]{1,0:T(8,128)S(1)}, f32[128,256]{1,0:T(8,128)}, u32[]{:S(2)}) copy-start(f32[128,256]{1,0:T(8,128)} %param.7) | copy-start | bytes 393220
  100.0 35.7 %copy-start.9 = (s32[128]{0:T(128)S(1)}, s32[128]{0:T(128)}, u32[]{:S(2)}) copy-start(s32[128]{0:T(128)} %param.10) | copy-start | bytes 1540
  117.7 18.0 %all-to-all-start.4 = ((bf16[3,128,256]{2,1,0:T(8,128)(2,1)}), bf16[3,128,256]{2,1,0:T(8,128)(2,1)S(1)}, u32[]{:S(2)}, u32[]{:S(2)}) async-start(bf16[3,128,256]{2,1,0:T(8,128)(2,1)} %reduce_sum.42), calls=%async_computation.4 | async-start | bytes 393216 | tf_op jit(solution)/shard_map/all_to_all | solution.py:114
  147.1 14.2 %copy-start.7 = (bf16[4,64,256]{2,1,0:T(8,128)(2,1)}, bf16[4,64,256]{2,1,0:T(8,128)(2,1)S(1)}, u32[]{:S(2)}) copy-start(bf16[4,64,256]{2,1,0:T(8,128)(2,1)S(1)} %all_to_all.53) | copy-start | bytes 393220
  161.3 43.1 %all-to-all-start.7 = ((bf16[4,8,64,256]{3,2,1,0:T(8,128)(2,1)}), bf16[4,8,64,256]{3,2,1,0:T(8,128)(2,1)S(1)}, u32[]{:S(2)}, u32[]{:S(2)}) async-start(bf16[4,8,64,256]{3,2,1,0:T(8,128)(2,1)} %broadcast_in_dim.84), calls=%async_computation.7 | async-start | bytes 2097152 | tf_op jit(solution)/shard_map/all_to_all | solution.py:77
  165.1 39.2 %all-gather.7.cloned.1.call-start = ((), (), s32[]{:S(2)}) async-start(), calls=%async_computation.11 | async-start | bytes 1179648 | tf_op jit(solution)/shard_map/all_gather | solution.py:98
  204.3 2.1 copy-start
  206.4 1.2 copy-start.4
  209.6 4.2 %collective-permute-start.1 = (bf16[12,128,256]{2,1,0:T(8,128)(2,1)S(1)}, bf16[12,128,256]{2,1,0:T(8,128)(2,1)S(1)}, u32[]{:S(2)}, u32[]{:S(2)}) collective-permute-start(bf16[12,128,256]{2,1,0:T(8,128)(2,1)S(1)} %shard_map.76), channel_id=1, source_target_pairs={{0,1},{1,0},{2,3},{3,2},{4,5},{5,4},{6,7},{7,6},{8,9},{9,8},{10,11... | collective-permute-start | bytes 2359304 | tf_op jit(solution)/shard_map/ppermute | solution.py:108
Sparse Core Ops, SparseCore 0:
  44.7 45.6 all-gather.4
  168.3 35.9 all-gather.6

commit v5 on v1

--- a/solution.py
+++ b/solution.py
@@ -51,13 +51,13 @@
         for copy in copies:
             copy.wait()
 
-    depth = weights.shape[2]
+    depth = weights.shape[1]
     for q in range(STEP):
         base = ((step * STEP + q) * CORES + parity[0]) * depth
         total = None
         for t in range(0, depth, 2):
             group = range(t, min(t + 2, depth))
-            left = jnp.concatenate([weights[q, 0, u] for u in group], axis=1)
+            left = jnp.concatenate([weights[q, u] for u in group], axis=1)
             right = jnp.concatenate([blocks[slots[base + u]] for u in group], axis=0)
             term = jnp.dot(left, right, preferred_element_type=jnp.float32)
             total = term if total is None else total + term
@@ -65,15 +65,13 @@
 
 
 def partial_sums(parity, slots, weights, pieces, dtype):
-    _, _, depth, size, _ = weights.shape
+    _, depth, size, _ = weights.shape
     classes = pieces[0].shape[-1]
     grid_spec = pltpu.PrefetchScalarGridSpec(
         num_scalar_prefetch=2,
         grid=(PAIRS // STEP,),
         in_specs=[
-            pl.BlockSpec(
-                (STEP, 1, depth, size, size), lambda i, parity, slots: (i, parity[0], 0, 0, 0)
-            )
+            pl.BlockSpec((STEP, depth, size, size), lambda i, parity, slots: (i, 0, 0, 0))
         ]
         + [pl.BlockSpec(memory_space=pl.ANY)] * len(pieces),
         out_specs=pl.BlockSpec((STEP, size, classes), lambda i, parity, slots: (i, 0, 0)),
@@ -98,13 +96,16 @@
 def gather_blocks(outgoing):
     spread = jnp.broadcast_to(outgoing[None], (ZL,) + outgoing.shape)
     own = lax.all_to_all(spread, "src", 0, 0, axis_index_groups=Z_GROUPS)
-    up, down = [own], [own]
-    for _ in range(3):
-        up.append(lax.ppermute(up[-1], "src", UP))
-        down.append(lax.ppermute(down[-1], "src", DOWN))
-    far_up = lax.ppermute(up[3][:2], "src", UP)
-    far_down = lax.ppermute(down[3][2:], "src", DOWN)
-    return [own, down[1], down[2], down[3], far_up, far_down, up[3], up[2], up[1]]
+    half = ZL // 2
+    up2 = lax.ppermute(own, "src", y_shift(2))
+    down2 = lax.ppermute(own, "src", y_shift(-2))
+    up1 = lax.ppermute(own, "src", UP)
+    down1 = lax.ppermute(own, "src", DOWN)
+    up3 = lax.ppermute(up2, "src", UP)
+    down3 = lax.ppermute(down2, "src", DOWN)
+    far_up = lax.ppermute(up2[:half], "src", y_shift(2))
+    far_down = lax.ppermute(down2[half:], "src", y_shift(-2))
+    return [own, down1, down2, down3, far_up, far_down, up3, up2, up1]
 
 
 def per_device(prior, degrees, seed_mask, seed_labels, adjacency, block_cols, slot_counts):
@@ -112,6 +113,8 @@
     depth, size = adjacency.shape[3], adjacency.shape[4]
     weights = adjacency.reshape(PAIRS, CORES, depth, size, size)
     core = lax.axis_index("dst") % CORES
+    here = lax.dynamic_index_in_dim(weights, core, 1, keepdims=False)
+    away = lax.dynamic_index_in_dim(weights, 1 - core, 1, keepdims=False)
     mine = core.astype(jnp.int32).reshape(1)
     other = 1 - mine
     y = lax.axis_index("src") // ZL
@@ -128,9 +131,9 @@
     for _ in range(SWEEPS):
         outgoing = (inverse_root * scores).astype(jnp.bfloat16)
         pieces = gather_blocks(outgoing)
-        send = partial_sums(other, slots, weights, pieces, jnp.bfloat16)
+        send = partial_sums(other, slots, away, pieces, jnp.bfloat16)
         swapped = lax.ppermute(send, "dst", SWAP)
-        keep = partial_sums(mine, slots, weights, pieces, jnp.float32)
+        keep = partial_sums(mine, slots, here, pieces, jnp.float32)
         chip = (keep + swapped.astype(jnp.float32)).astype(jnp.bfloat16)
         chip = chip.reshape(X, ZH, size, classes)
         rows = lax.all_to_all(chip, "dst", 0, 0, axis_index_groups=X_GROUPS)

time: 200 us -> 195 us (0.975)
  the two profiles are of different devices: /device:TPU:24 before, /device:TPU:17 now
where the time goes in v5:
time: 195 us; the launch traced here: 194 us
  starting transfers between devices  78.1 us (40%)
  blocking collectives  71.9 us (37%)
  waiting for transfers between devices  23.5 us (12%)
  Pallas kernels  11.1 us (6%)
  other arithmetic  5.5 us (3%)
  local copies, waits for them, and re-layouts  3.5 us (2%)
    all_to_all x2, blocking collectives, per_device(): rows = lax.all_to_all(chip, 'dst', 0, 0, axis_index_groups=X_GROUPS)  30.2 us
    all_to_all x2, blocking collectives, gather_blocks(): own = lax.all_to_all(spread, 'src', 0, 0, axis_index_groups=Z_GROUPS)  27.1 us
    ppermute x2, starting transfers between devices, per_device(): swapped = lax.ppermute(send, 'dst', SWAP)  17.8 us
    all_to_all x1, blocking collectives, per_device(): parts = lax.all_to_all(rows, 'dst', 0, 0, axis_index_groups=H_GROUPS)  14.6 us
    pallas_call x4, Pallas kernels, partial_sums(): pl.pallas_call(sum_kernel, grid_spec=grid_spec, out_shape=jax.ShapeDtypeS...  11.1 us
    ppermute x2, starting transfers between devices, gather_blocks(): up2 = lax.ppermute(own, 'src', y_shift(2))  10.9 us
    all_to_all x1, starting transfers between devices, per_device(): parts = lax.all_to_all(rows, 'dst', 0, 0, axis_index_groups=H_GROUPS)  10.9 us
    all_to_all x1, waiting for transfers between devices, per_device(): parts = lax.all_to_all(rows, 'dst', 0, 0, axis_index_groups=H_GROUPS)  9.19 us
  transfers between devices with their start and end apart: 19, of which 7 were waited for; matrix products, arithmetic and copies ran while one was open for 3% of the time, Pallas kernels for 3%

profile of v5, /device:TPU:17, one launch (start us, length us, event | category | flops | bytes accessed | tf_op | source)
XLA Modules:
  0.0 194.0 jit_solution(6497414828947341358)
XLA Ops:
  0.0 0.7 broadcast_multiply_fusion
  0.7 1.0 multiply_convert_fusion
  1.7 13.7 %all_to_all.30.refs_0_ = bf16[4,128,256]{2,1,0:T(8,128)(2,1)S(1)} all-to-all(bf16[4,128,256]{2,1,0:T(8,128)(2,1)S(1)} %broadcast_in_dim.34), channel_id=1, replica_groups={{0,24,48,72},{96,120,144,168},{192,216,240,264},{288,312,336,360},{384,..., dimensions={0} | all-to-all | bytes 524288 | tf_op jit(solution)/shard_map/all_to_all | solution.py:98
  15.3 1.9 collective-permute-start.1
  17.3 5.5 %collective-permute-start.3 = (bf16[4,128,256]{2,1,0:T(8,128)(2,1)S(1)}, bf16[4,128,256]{2,1,0:T(8,128)(2,1)S(1)}, u32[]{:S(2)}, u32[]{:S(2)}) collective-permute-start(bf16[4,128,256]{2,1,0:T(8,128)(2,1)S(1)} %all_to_all.30.refs_0_), channel_id=1, source_target_pairs={{0,192},{24,216},{48,240},{72,264},{96,288},{120,312},{144,336},{1... | collective-permute-start | bytes 786440 | tf_op jit(solution)/shard_map/ppermute | solution.py:100
  22.7 1.9 collective-permute-start
  24.7 0.7 iota_compare_fusion.1
  25.4 0.8 copy.14
  26.2 0.1 squeeze.10
  26.3 0.1 lt.47
  26.4 3.4 %collective-permute-start.7 = (bf16[4,128,256]{2,1,0:T(8,128)(2,1)S(1)}, bf16[4,128,256]{2,1,0:T(8,128)(2,1)S(1)}, u32[]{:S(2)}, u32[]{:S(2)}) collective-permute-start(bf16[4,128,256]{2,1,0:T(8,128)(2,1)S(1)} %all_to_all.30.refs_0_), channel_id=1, source_target_pairs={{0,96},{24,120},{48,144},{72,168},{96,192},{120,216},{144,240},{16... | collective-permute-start | bytes 786440 | tf_op jit(solution)/shard_map/ppermute | solution.py:102
  29.8 1.8 collective-permute-done.1.refs_2_
  31.6 1.9 collective-permute-start.2
  33.5 0.0 collective-permute-done.3.refs_7_
  33.5 3.4 %collective-permute-start.6 = (bf16[4,128,256]{2,1,0:T(8,128)(2,1)S(1)}, bf16[4,128,256]{2,1,0:T(8,128)(2,1)}, u32[]{:S(2)}, u32[]{:S(2)}) collective-permute-start(bf16[4,128,256]{2,1,0:T(8,128)(2,1)S(1)} %collective-permute-done.3.refs_7_), channel_id=1, source_target_pairs={{0,96},{24,120},{48,144},{72,168},{96,192},{120,216},{144,240},{16... | collective-permute-start | bytes 786440 | tf_op jit(solution)/shard_map/ppermute | solution.py:104
  36.9 5.4 %collective-permute-start.4 = (bf16[2,128,256]{2,1,0:T(8,128)(2,1)S(1)}, bf16[2,128,256]{2,1,0:T(8,128)(2,1)S(1)}, u32[]{:S(2)}, u32[]{:S(2)}) collective-permute-start(bf16[2,128,256]{2,1,0:T(8,128)(2,1)S(1)} %slice.16), channel_id=1, source_target_pairs={{0,192},{24,216},{48,240},{72,264},{96,288},{120,312},{144,336},{1... | collective-permute-start | bytes 393224 | tf_op jit(solution)/shard_map/ppermute | solution.py:106
  42.4 0.0 collective-permute-done.refs_1_
  42.4 1.9 collective-permute-start.5
  44.3 2.4 %dynamic-slice_bitcast_fusion = (bf16[12,5,128,128]{3,2,1,0:T(8,128)(2,1)S(1)}, bf16[12,5,128,128]{3,2,1,0:T(8,128)(2,1)S(1)}) fusion(bf16[12,2,5,128,128]{4,3,2,1,0:T(8,128)(2,1)} %bitcast.15, s32[]{:T(128)S(6)} %select_n.55, s32[]{:T(128)S(6)} %select_n.54), kind=kLoop, calls=%fused_computation | loop fusion | bytes 7864328 | tf_op jit(solution)/shard_map/jit(dynamic_index_in_dim)/squeeze | solution.py:117
  46.7 0.0 copy-start
  46.8 0.0 collective-permute-done.7.refs_8_
  46.8 1.3 collective-permute-done.4.refs_4_
  48.1 3.5 %collective-permute-done.5.refs_5_ = bf16[2,128,256]{2,1,0:T(8,128)(2,1)S(1)} collective-permute-done((bf16[2,128,256]{2,1,0:T(8,128)(2,1)S(1)}, bf16[2,128,256]{2,1,0:T(8,128)(2,1)S(1)}, u32[]{:S(2)}, u32[]{:S(2)}) %collective-permute-start.5) | collective-permute-done | bytes 131104 | tf_op jit(solution)/shard_map/ppermute | solution.py:107
  51.5 0.0 collective-permute-done.2.refs_3_
  51.5 0.0 collective-permute-done.6.refs_6_
  51.5 3.3 %shard_map.74 = bf16[12,128,256]{2,1,0:T(8,128)(2,1)S(1)} custom-call(s32[1]{0:T(128)S(6)} %sub.27.parity, s32[120]{0:T(128)S(1)} %fusion.3.slots, bf16[12,5,128,128]{3,2,1,0:T(8,128)(2,1)S(1)} %get-tuple-element.5.weights, bf16[4,128,256]{2,1,0:T(8,128)(2,1)S(1)} %all_to_all.30.refs_0_, bf16[4,128,256]{2,1,0:T(8,128)(2,1)S(1)} %collective-permute-done.refs_1_, ...), custom_call_target="tpu_custom_call" | custom-call | flops 503316480 | bytes 6291456 | tf_op jit(solution)/shard_map/pallas_call | solution.py:83
  54.8 6.8 %collective-permute-start.8 = (bf16[12,128,256]{2,1,0:T(8,128)(2,1)S(1)}, bf16[12,128,256]{2,1,0:T(8,128)(2,1)S(1)}, u32[]{:S(2)}, u32[]{:S(2)}) collective-permute-start(bf16[12,128,256]{2,1,0:T(8,128)(2,1)S(1)} %shard_map.74), channel_id=1, source_target_pairs={{0,1},{1,0},{2,3},{3,2},{4,5},{5,4},{6,7},{7,6},{8,9},{9,8},{10,11... | collective-permute-start | bytes 2359304 | tf_op jit(solution)/shard_map/ppermute | solution.py:135
  61.7 3.2 %shard_map.73 = f32[12,128,256]{2,1,0:T(8,128)S(1)} custom-call(s32[1]{0:T(128)} %bitcast.parity, s32[120]{0:T(128)S(1)} %fusion.3.slots, bf16[12,5,128,128]{3,2,1,0:T(8,128)(2,1)S(1)} %get-tuple-element.6.weights, bf16[4,128,256]{2,1,0:T(8,128)(2,1)S(1)} %all_to_all.30.refs_0_, bf16[4,128,256]{2,1,0:T(8,128)(2,1)S(1)} %collective-permute-done.refs_1_, ...), custom_call_target="tpu_custom_call" | custom-call | flops 503316480 | bytes 6291456 | tf_op jit(solution)/shard_map/pallas_call | solution.py:83
  64.8 0.0 collective-permute-done.8
  64.8 0.2 add_convert_fusion.1
  65.1 0.0 copy-start.3
  65.1 15.7 %all_to_all.31 = bf16[4,3,128,256]{3,2,1,0:T(8,128)(2,1)S(1)} all-to-all(bf16[4,3,128,256]{3,2,1,0:T(8,128)(2,1)S(1)} %bitcast.16), channel_id=1, replica_groups={{0,6,12,18},{1,7,13,19},{2,8,14,20},{3,9,15,21},{4,10,16,22},{5,11,17,2..., dimensions={0} | all-to-all | bytes 1572864 | tf_op jit(solution)/shard_map/all_to_all | solution.py:139
  80.8 0.8 reduce_sum.42
  81.6 10.9 %all-to-all-start.2 = ((bf16[3,128,256]{2,1,0:T(8,128)(2,1)}), bf16[3,128,256]{2,1,0:T(8,128)(2,1)S(1)}, u32[]{:S(2)}, u32[]{:S(2)}) async-start(bf16[3,128,256]{2,1,0:T(8,128)(2,1)} %reduce_sum.42), calls=%async_computation.2 | async-start | bytes 393216 | tf_op jit(solution)/shard_map/all_to_all | solution.py:141
  92.5 0.7 broadcast_compare_fusion
  93.2 9.2 %all-to-all-done.2 = bf16[3,128,256]{2,1,0:T(8,128)(2,1)S(1)} async-done(((bf16[3,128,256]{2,1,0:T(8,128)(2,1)}), bf16[3,128,256]{2,1,0:T(8,128)(2,1)S(1)}, u32[]{:S(2)}, u32[]{:S(2)}) %all-to-all-start.2) | async-done | bytes 196640 | tf_op jit(solution)/shard_map/all_to_all | solution.py:141
  102.4 0.0 copy-done.3
  102.4 0.1 fusion.1
  102.6 13.4 %all_to_all.32.refs_0_ = bf16[4,128,256]{2,1,0:T(8,128)(2,1)S(1)} all-to-all(bf16[4,128,256]{2,1,0:T(8,128)(2,1)S(1)} %broadcast_in_dim.35), channel_id=1, replica_groups={{0,24,48,72},{96,120,144,168},{192,216,240,264},{288,312,336,360},{384,..., dimensions={0} | all-to-all | bytes 524288 | tf_op jit(solution)/shard_map/all_to_all | solution.py:98
  116.0 1.9 collective-permute-start.10
  117.9 5.5 %collective-permute-start.12 = (bf16[4,128,256]{2,1,0:T(8,128)(2,1)S(1)}, bf16[4,128,256]{2,1,0:T(8,128)(2,1)S(1)}, u32[]{:S(2)}, u32[]{:S(2)}) collective-permute-start(bf16[4,128,256]{2,1,0:T(8,128)(2,1)S(1)} %all_to_all.32.refs_0_), channel_id=1, source_target_pairs={{0,192},{24,216},{48,240},{72,264},{96,288},{120,312},{144,336},{1... | collective-permute-start | bytes 786440 | tf_op jit(solution)/shard_map/ppermute | solution.py:100
  123.4 1.9 collective-permute-start.16
  125.3 3.4 %collective-permute-start.9 = (bf16[4,128,256]{2,1,0:T(8,128)(2,1)S(1)}, bf16[4,128,256]{2,1,0:T(8,128)(2,1)S(1)}, u32[]{:S(2)}, u32[]{:S(2)}) collective-permute-start(bf16[4,128,256]{2,1,0:T(8,128)(2,1)S(1)} %all_to_all.32.refs_0_), channel_id=1, source_target_pairs={{0,672},{24,696},{48,720},{72,744},{96,0},{120,24},{144,48},{168,7... | collective-permute-start | bytes 786440 | tf_op jit(solution)/shard_map/ppermute | solution.py:103
  128.7 4.0 %collective-permute-done.10.refs_2_ = bf16[4,128,256]{2,1,0:T(8,128)(2,1)S(1)} collective-permute-done((bf16[4,128,256]{2,1,0:T(8,128)(2,1)S(1)}, bf16[4,128,256]{2,1,0:T(8,128)(2,1)S(1)}, u32[]{:S(2)}, u32[]{:S(2)}) %collective-permute-start.10) | collective-permute-done | bytes 262176 | tf_op jit(solution)/shard_map/ppermute | solution.py:101
  132.7 1.9 collective-permute-start.11
  134.6 0.0 collective-permute-done.12.refs_7_
  134.6 3.4 %collective-permute-start.15 = (bf16[4,128,256]{2,1,0:T(8,128)(2,1)S(1)}, bf16[4,128,256]{2,1,0:T(8,128)(2,1)S(1)}, u32[]{:S(2)}, u32[]{:S(2)}) collective-permute-start(bf16[4,128,256]{2,1,0:T(8,128)(2,1)S(1)} %collective-permute-done.12.refs_7_), channel_id=1, source_target_pairs={{0,96},{24,120},{48,144},{72,168},{96,192},{120,216},{144,240},{16... | collective-permute-start | bytes 786440 | tf_op jit(solution)/shard_map/ppermute | solution.py:104
  138.0 2.1 %collective-permute-start.13 = (bf16[2,128,256]{2,1,0:T(8,128)(2,1)S(1)}, bf16[2,128,256]{2,1,0:T(8,128)(2,1)S(1)}, u32[]{:S(2)}, u32[]{:S(2)}) collective-permute-start(bf16[2,128,256]{2,1,0:T(8,128)(2,1)S(1)} %slice.18), channel_id=1, source_target_pairs={{0,192},{24,216},{48,240},{72,264},{96,288},{120,312},{144,336},{1... | collective-permute-start | bytes 393224 | tf_op jit(solution)/shard_map/ppermute | solution.py:106
  140.1 0.0 collective-permute-done.16.refs_8_
  140.1 4.1 %collective-permute-start.14 = (bf16[2,128,256]{2,1,0:T(8,128)(2,1)S(1)}, bf16[2,128,256]{2,1,0:T(8,128)(2,1)S(1)}, u32[]{:S(2)}, u32[]{:S(2)}) collective-permute-start(bf16[2,128,256]{2,1,0:T(8,128)(2,1)S(1)} %slice.19), channel_id=1, source_target_pairs={{0,576},{24,600},{48,624},{72,648},{96,672},{120,696},{144,720},{1... | collective-permute-start | bytes 393224 | tf_op jit(solution)/shard_map/ppermute | solution.py:107
  144.2 0.0 collective-permute-done.9.refs_1_
  144.2 3.6 %collective-permute-done.13.refs_4_ = bf16[2,128,256]{2,1,0:T(8,128)(2,1)S(1)} collective-permute-done((bf16[2,128,256]{2,1,0:T(8,128)(2,1)S(1)}, bf16[2,128,256]{2,1,0:T(8,128)(2,1)S(1)}, u32[]{:S(2)}, u32[]{:S(2)}) %collective-permute-start.13) | collective-permute-done | bytes 131104 | tf_op jit(solution)/shard_map/ppermute | solution.py:106
  147.8 0.2 collective-permute-done.14.refs_5_
  148.0 0.0 collective-permute-done.11.refs_3_
  148.0 0.0 collective-permute-done.15.refs_6_
  148.0 2.4 %shard_map.76 = bf16[12,128,256]{2,1,0:T(8,128)(2,1)S(1)} custom-call(s32[1]{0:T(128)S(6)} %sub.27.parity, s32[120]{0:T(128)S(1)} %fusion.3.slots, bf16[12,5,128,128]{3,2,1,0:T(8,128)(2,1)S(1)} %copy-done.1, bf16[4,128,256]{2,1,0:T(8,128)(2,1)S(1)} %all_to_all.32.refs_0_, bf16[4,128,256]{2,1,0:T(8,128)(2,1)S(1)} %collective-permute-done.9.refs_1_, ...), custom_call_target="tpu_custom_call" | custom-call | flops 503316480 | bytes 6291456 | tf_op jit(solution)/shard_map/pallas_call | solution.py:83
  150.4 10.9 %collective-permute-start.17 = (bf16[12,128,256]{2,1,0:T(8,128)(2,1)S(1)}, bf16[12,128,256]{2,1,0:T(8,128)(2,1)S(1)}, u32[]{:S(2)}, u32[]{:S(2)}) collective-permute-start(bf16[12,128,256]{2,1,0:T(8,128)(2,1)S(1)} %shard_map.76), channel_id=1, source_target_pairs={{0,1},{1,0},{2,3},{3,2},{4,5},{5,4},{6,7},{7,6},{8,9},{9,8},{10,11... | collective-permute-start | bytes 2359304 | tf_op jit(solution)/shard_map/ppermute | solution.py:135
  161.3 2.3 %shard_map.75 = f32[12,128,256]{2,1,0:T(8,128)S(1)} custom-call(s32[1]{0:T(128)} %bitcast.parity, s32[120]{0:T(128)S(1)} %fusion.3.slots, bf16[12,5,128,128]{3,2,1,0:T(8,128)(2,1)S(1)} %get-tuple-element.6.weights, bf16[4,128,256]{2,1,0:T(8,128)(2,1)S(1)} %all_to_all.32.refs_0_, bf16[4,128,256]{2,1,0:T(8,128)(2,1)S(1)} %collective-permute-done.9.refs_1_, ...), custom_call_target="tpu_custom_call" | custom-call | flops 503316480 | bytes 6291456 | tf_op jit(solution)/shard_map/pallas_call | solution.py:83
  163.6 0.0 collective-permute-done.17
  163.6 0.3 add_convert_fusion
  163.9 14.6 %all_to_all.33 = bf16[4,3,128,256]{3,2,1,0:T(8,128)(2,1)S(1)} all-to-all(bf16[4,3,128,256]{3,2,1,0:T(8,128)(2,1)S(1)} %bitcast.17), channel_id=1, replica_groups={{0,6,12,18},{1,7,13,19},{2,8,14,20},{3,9,15,21},{4,10,16,22},{5,11,17,2..., dimensions={0} | all-to-all | bytes 1572864 | tf_op jit(solution)/shard_map/all_to_all | solution.py:139
  178.5 0.2 reduce_sum.44
  178.6 14.6 %all_to_all.34 = bf16[3,128,256]{2,1,0:T(8,128)(2,1)S(1)} all-to-all(bf16[3,128,256]{2,1,0:T(8,128)(2,1)S(1)} %reduce_sum.44), channel_id=1, replica_groups={{0,2,4},{1,3,5},{6,8,10},{7,9,11},{12,14,16},{13,15,17},{18,20,22},{19,..., dimensions={0} | all-to-all | bytes 393216 | tf_op jit(solution)/shard_map/all_to_all | solution.py:141
  193.2 0.8 convert_select_fusion
  (14 shorter events, 0.2 us)
Async XLA Ops:
  15.3 16.2 %collective-permute-start.1 = (bf16[4,128,256]{2,1,0:T(8,128)(2,1)S(1)}, bf16[4,128,256]{2,1,0:T(8,128)(2,1)S(1)}, u32[]{:S(2)}, u32[]{:S(2)}) collective-permute-start(bf16[4,128,256]{2,1,0:T(8,128)(2,1)S(1)} %all_to_all.30.refs_0_), channel_id=1, source_target_pairs={{0,576},{24,600},{48,624},{72,648},{96,672},{120,696},{144,720},{1... | collective-permute-start | bytes 786440 | tf_op jit(solution)/shard_map/ppermute | solution.py:101
  17.3 16.2 %collective-permute-start.3 = (bf16[4,128,256]{2,1,0:T(8,128)(2,1)S(1)}, bf16[4,128,256]{2,1,0:T(8,128)(2,1)S(1)}, u32[]{:S(2)}, u32[]{:S(2)}) collective-permute-start(bf16[4,128,256]{2,1,0:T(8,128)(2,1)S(1)} %all_to_all.30.refs_0_), channel_id=1, source_target_pairs={{0,192},{24,216},{48,240},{72,264},{96,288},{120,312},{144,336},{1... | collective-permute-start | bytes 786440 | tf_op jit(solution)/shard_map/ppermute | solution.py:100
  22.7 19.6 %collective-permute-start = (bf16[4,128,256]{2,1,0:T(8,128)(2,1)S(1)}, bf16[4,128,256]{2,1,0:T(8,128)(2,1)S(1)}, u32[]{:S(2)}, u32[]{:S(2)}) collective-permute-start(bf16[4,128,256]{2,1,0:T(8,128)(2,1)S(1)} %all_to_all.30.refs_0_), channel_id=1, source_target_pairs={{0,672},{24,696},{48,720},{72,744},{96,0},{120,24},{144,48},{168,7... | collective-permute-start | bytes 786440 | tf_op jit(solution)/shard_map/ppermute | solution.py:103
  26.4 20.4 %collective-permute-start.7 = (bf16[4,128,256]{2,1,0:T(8,128)(2,1)S(1)}, bf16[4,128,256]{2,1,0:T(8,128)(2,1)S(1)}, u32[]{:S(2)}, u32[]{:S(2)}) collective-permute-start(bf16[4,128,256]{2,1,0:T(8,128)(2,1)S(1)} %all_to_all.30.refs_0_), channel_id=1, source_target_pairs={{0,96},{24,120},{48,144},{72,168},{96,192},{120,216},{144,240},{16... | collective-permute-start | bytes 786440 | tf_op jit(solution)/shard_map/ppermute | solution.py:102
  31.6 20.0 %collective-permute-start.2 = (bf16[4,128,256]{2,1,0:T(8,128)(2,1)S(1)}, bf16[4,128,256]{2,1,0:T(8,128)(2,1)S(1)}, u32[]{:S(2)}, u32[]{:S(2)}) collective-permute-start(bf16[4,128,256]{2,1,0:T(8,128)(2,1)S(1)} %collective-permute-done.1.refs_2_), channel_id=1, source_target_pairs={{0,672},{24,696},{48,720},{72,744},{96,0},{120,24},{144,48},{168,7... | collective-permute-start | bytes 786440 | tf_op jit(solution)/shard_map/ppermute | solution.py:105
  33.5 18.0 %collective-permute-start.6 = (bf16[4,128,256]{2,1,0:T(8,128)(2,1)S(1)}, bf16[4,128,256]{2,1,0:T(8,128)(2,1)}, u32[]{:S(2)}, u32[]{:S(2)}) collective-permute-start(bf16[4,128,256]{2,1,0:T(8,128)(2,1)S(1)} %collective-permute-done.3.refs_7_), channel_id=1, source_target_pairs={{0,96},{24,120},{48,144},{72,168},{96,192},{120,216},{144,240},{16... | collective-permute-start | bytes 786440 | tf_op jit(solution)/shard_map/ppermute | solution.py:104
  36.9 11.1 %collective-permute-start.4 = (bf16[2,128,256]{2,1,0:T(8,128)(2,1)S(1)}, bf16[2,128,256]{2,1,0:T(8,128)(2,1)S(1)}, u32[]{:S(2)}, u32[]{:S(2)}) collective-permute-start(bf16[2,128,256]{2,1,0:T(8,128)(2,1)S(1)} %slice.16), channel_id=1, source_target_pairs={{0,192},{24,216},{48,240},{72,264},{96,288},{120,312},{144,336},{1... | collective-permute-start | bytes 393224 | tf_op jit(solution)/shard_map/ppermute | solution.py:106
  42.4 9.1 %collective-permute-start.5 = (bf16[2,128,256]{2,1,0:T(8,128)(2,1)S(1)}, bf16[2,128,256]{2,1,0:T(8,128)(2,1)S(1)}, u32[]{:S(2)}, u32[]{:S(2)}) collective-permute-start(bf16[2,128,256]{2,1,0:T(8,128)(2,1)S(1)} %slice.17), channel_id=1, source_target_pairs={{0,576},{24,600},{48,624},{72,648},{96,672},{120,696},{144,720},{1... | collective-permute-start | bytes 393224 | tf_op jit(solution)/shard_map/ppermute | solution.py:107
  46.7 8.1 %copy-start = (bf16[12,5,128,128]{3,2,1,0:T(8,128)(2,1)}, bf16[12,5,128,128]{3,2,1,0:T(8,128)(2,1)S(1)}, u32[]{:S(2)}) copy-start(bf16[12,5,128,128]{3,2,1,0:T(8,128)(2,1)S(1)} %get-tuple-element.5.weights) | copy-start | bytes 5898244
  54.8 10.0 %collective-permute-start.8 = (bf16[12,128,256]{2,1,0:T(8,128)(2,1)S(1)}, bf16[12,128,256]{2,1,0:T(8,128)(2,1)S(1)}, u32[]{:S(2)}, u32[]{:S(2)}) collective-permute-start(bf16[12,128,256]{2,1,0:T(8,128)(2,1)S(1)} %shard_map.74), channel_id=1, source_target_pairs={{0,1},{1,0},{2,3},{3,2},{4,5},{5,4},{6,7},{7,6},{8,9},{9,8},{10,11... | collective-permute-start | bytes 2359304 | tf_op jit(solution)/shard_map/ppermute | solution.py:135
  65.1 37.3 %copy-start.3 = (s32[128]{0:T(128)S(1)}, s32[128]{0:T(128)}, u32[]{:S(2)}) copy-start(s32[128]{0:T(128)} %param.10) | copy-start | bytes 1540
  80.8 21.6 %copy-start.2 = (f32[128,256]{1,0:T(8,128)S(1)}, f32[128,256]{1,0:T(8,128)}, u32[]{:S(2)}) copy-start(f32[128,256]{1,0:T(8,128)} %param.7) | copy-start | bytes 393220
  81.6 20.8 %all-to-all-start.2 = ((bf16[3,128,256]{2,1,0:T(8,128)(2,1)}), bf16[3,128,256]{2,1,0:T(8,128)(2,1)S(1)}, u32[]{:S(2)}, u32[]{:S(2)}) async-start(bf16[3,128,256]{2,1,0:T(8,128)(2,1)} %reduce_sum.42), calls=%async_computation.2 | async-start | bytes 393216 | tf_op jit(solution)/shard_map/all_to_all | solution.py:141
  102.4 45.6 %copy-start.1 = (bf16[12,5,128,128]{3,2,1,0:T(8,128)(2,1)S(1)}, bf16[12,5,128,128]{3,2,1,0:T(8,128)(2,1)}, u32[]{:S(2)}) copy-start(bf16[12,5,128,128]{3,2,1,0:T(8,128)(2,1)} %copy-done) | copy-start | bytes 5898244
  116.0 16.7 %collective-permute-start.10 = (bf16[4,128,256]{2,1,0:T(8,128)(2,1)S(1)}, bf16[4,128,256]{2,1,0:T(8,128)(2,1)S(1)}, u32[]{:S(2)}, u32[]{:S(2)}) collective-permute-start(bf16[4,128,256]{2,1,0:T(8,128)(2,1)S(1)} %all_to_all.32.refs_0_), channel_id=1, source_target_pairs={{0,576},{24,600},{48,624},{72,648},{96,672},{120,696},{144,720},{1... | collective-permute-start | bytes 786440 | tf_op jit(solution)/shard_map/ppermute | solution.py:101
  117.9 16.7 %collective-permute-start.12 = (bf16[4,128,256]{2,1,0:T(8,128)(2,1)S(1)}, bf16[4,128,256]{2,1,0:T(8,128)(2,1)S(1)}, u32[]{:S(2)}, u32[]{:S(2)}) collective-permute-start(bf16[4,128,256]{2,1,0:T(8,128)(2,1)S(1)} %all_to_all.32.refs_0_), channel_id=1, source_target_pairs={{0,192},{24,216},{48,240},{72,264},{96,288},{120,312},{144,336},{1... | collective-permute-start | bytes 786440 | tf_op jit(solution)/shard_map/ppermute | solution.py:100
  123.4 16.7 %collective-permute-start.16 = (bf16[4,128,256]{2,1,0:T(8,128)(2,1)S(1)}, bf16[4,128,256]{2,1,0:T(8,128)(2,1)S(1)}, u32[]{:S(2)}, u32[]{:S(2)}) collective-permute-start(bf16[4,128,256]{2,1,0:T(8,128)(2,1)S(1)} %all_to_all.32.refs_0_), channel_id=1, source_target_pairs={{0,96},{24,120},{48,144},{72,168},{96,192},{120,216},{144,240},{16... | collective-permute-start | bytes 786440 | tf_op jit(solution)/shard_map/ppermute | solution.py:102
  125.3 18.9 %collective-permute-start.9 = (bf16[4,128,256]{2,1,0:T(8,128)(2,1)S(1)}, bf16[4,128,256]{2,1,0:T(8,128)(2,1)S(1)}, u32[]{:S(2)}, u32[]{:S(2)}) collective-permute-start(bf16[4,128,256]{2,1,0:T(8,128)(2,1)S(1)} %all_to_all.32.refs_0_), channel_id=1, source_target_pairs={{0,672},{24,696},{48,720},{72,744},{96,0},{120,24},{144,48},{168,7... | collective-permute-start | bytes 786440 | tf_op jit(solution)/shard_map/ppermute | solution.py:103
  132.7 15.3 %collective-permute-start.11 = (bf16[4,128,256]{2,1,0:T(8,128)(2,1)S(1)}, bf16[4,128,256]{2,1,0:T(8,128)(2,1)S(1)}, u32[]{:S(2)}, u32[]{:S(2)}) collective-permute-start(bf16[4,128,256]{2,1,0:T(8,128)(2,1)S(1)} %collective-permute-done.10.refs_2_), channel_id=1, source_target_pairs={{0,672},{24,696},{48,720},{72,744},{96,0},{120,24},{144,48},{168,7... | collective-permute-start | bytes 786440 | tf_op jit(solution)/shard_map/ppermute | solution.py:105
  134.6 13.4 %collective-permute-start.15 = (bf16[4,128,256]{2,1,0:T(8,128)(2,1)S(1)}, bf16[4,128,256]{2,1,0:T(8,128)(2,1)S(1)}, u32[]{:S(2)}, u32[]{:S(2)}) collective-permute-start(bf16[4,128,256]{2,1,0:T(8,128)(2,1)S(1)} %collective-permute-done.12.refs_7_), channel_id=1, source_target_pairs={{0,96},{24,120},{48,144},{72,168},{96,192},{120,216},{144,240},{16... | collective-permute-start | bytes 786440 | tf_op jit(solution)/shard_map/ppermute | solution.py:104
  138.0 9.8 %collective-permute-start.13 = (bf16[2,128,256]{2,1,0:T(8,128)(2,1)S(1)}, bf16[2,128,256]{2,1,0:T(8,128)(2,1)S(1)}, u32[]{:S(2)}, u32[]{:S(2)}) collective-permute-start(bf16[2,128,256]{2,1,0:T(8,128)(2,1)S(1)} %slice.18), channel_id=1, source_target_pairs={{0,192},{24,216},{48,240},{72,264},{96,288},{120,312},{144,336},{1... | collective-permute-start | bytes 393224 | tf_op jit(solution)/shard_map/ppermute | solution.py:106
  140.1 7.8 %collective-permute-start.14 = (bf16[2,128,256]{2,1,0:T(8,128)(2,1)S(1)}, bf16[2,128,256]{2,1,0:T(8,128)(2,1)S(1)}, u32[]{:S(2)}, u32[]{:S(2)}) collective-permute-start(bf16[2,128,256]{2,1,0:T(8,128)(2,1)S(1)} %slice.19), channel_id=1, source_target_pairs={{0,576},{24,600},{48,624},{72,648},{96,672},{120,696},{144,720},{1... | collective-permute-start | bytes 393224 | tf_op jit(solution)/shard_map/ppermute | solution.py:107
  150.4 13.2 %collective-permute-start.17 = (bf16[12,128,256]{2,1,0:T(8,128)(2,1)S(1)}, bf16[12,128,256]{2,1,0:T(8,128)(2,1)S(1)}, u32[]{:S(2)}, u32[]{:S(2)}) collective-permute-start(bf16[12,128,256]{2,1,0:T(8,128)(2,1)S(1)} %shard_map.76), channel_id=1, source_target_pairs={{0,1},{1,0},{2,3},{3,2},{4,5},{5,4},{6,7},{7,6},{8,9},{9,8},{10,11... | collective-permute-start | bytes 2359304 | tf_op jit(solution)/shard_map/ppermute | solution.py:135
